TPU v7x, 32 devices: a whole 2x2x4 slice. The times are simulated.
32 devices in a mesh: fsdp: 4 (over z), context: 4 (over y, x), tensor: 2 (over core).
Axes of the slice: x: 2, y: 2, z: 4, core: 2. Of those that a mesh axis runs over, the one named last changes fastest.
Arguments:
- tokens: bfloat16 [8192, 1024], P(('fsdp', 'context')), may hold values from -6 to 6
- segments: int32 [4, 2048], P('fsdp'), may hold values from 0 to 2, never falling along the last dimension, each value on 1 to 1024 neighbouring positions
- deal: int32 [4, 8], P('fsdp'), may hold values from 0 to 7, as said below
- gain_mix: float32 [1024], replicated, may hold values from 0.5 to 1.5
- w_query: bfloat16 [1024, 512], P('fsdp', 'tensor'), may hold values from -0.1875 to 0.1875
- w_keyval: bfloat16 [1024, 256], P('fsdp', 'tensor'), may hold values from -0.1875 to 0.1875
- w_attn_out: bfloat16 [1024, 512], P('fsdp', 'tensor'), may hold values from -1.5 to 1.5
- w_gate_z: bfloat16 [1024, 1536], P('fsdp', 'tensor'), may hold values from -0.1875 to 0.1875
- w_in_x: bfloat16 [1024, 1536], P('fsdp', 'tensor'), may hold values from -0.1875 to 0.1875
- w_bc: bfloat16 [1024, 256], P('fsdp'), may hold values from -0.1875 to 0.1875
- w_step: bfloat16 [1024, 24], P('fsdp', 'tensor'), may hold values from -0.1875 to 0.1875
- conv_x: float32 [4, 1536], P(None, 'tensor'), may hold values from -0.5 to 0.5
- conv_bc: float32 [4, 256], replicated, may hold values from -0.5 to 0.5
- step_bias: float32 [24], P('tensor'), may hold values from -5 to -1
- decay_log: float32 [24], P('tensor'), may hold values from -4 to 1
- skip: float32 [24], P('tensor'), may hold values from 0.5 to 1.5
- w_ssm_out: bfloat16 [1024, 1536], P('fsdp', 'tensor'), may hold values from -0.15625 to 0.15625
- gain_ffn: float32 [1024], replicated, may hold values from 0.5 to 1.5
- w_ffn_gate: bfloat16 [1024, 2048], P('fsdp', 'tensor'), may hold values from -0.1875 to 0.1875
- w_ffn_up: bfloat16 [1024, 2048], P('fsdp', 'tensor'), may hold values from -0.1875 to 0.1875
- w_ffn_down: bfloat16 [1024, 2048], P('fsdp', 'tensor'), may hold values from -0.125 to 0.125
- cotangent: bfloat16 [8192, 1024], P(('fsdp', 'context')), may hold values from -6 to 6
Outputs:
- mixed_out: bfloat16 [8192, 1024], P(('fsdp', 'context'))
- tokens_grad: bfloat16 [8192, 1024], P(('fsdp', 'context'))
- gain_mix_grad: float32 [1024], replicated
- w_query_grad: float32 [1024, 512], P('fsdp', 'tensor')
- w_keyval_grad: float32 [1024, 256], P('fsdp', 'tensor')
- w_attn_out_grad: float32 [1024, 512], P('fsdp', 'tensor')
- w_gate_z_grad: float32 [1024, 1536], P('fsdp', 'tensor')
- w_in_x_grad: float32 [1024, 1536], P('fsdp', 'tensor')
- w_bc_grad: float32 [1024, 256], P('fsdp')
- w_step_grad: float32 [1024, 24], P('fsdp', 'tensor')
- conv_x_grad: float32 [4, 1536], P(None, 'tensor')
- conv_bc_grad: float32 [4, 256], replicated
- step_bias_grad: float32 [24], P('tensor')
- decay_log_grad: float32 [24], P('tensor')
- skip_grad: float32 [24], P('tensor')
- w_ssm_out_grad: float32 [1024, 1536], P('fsdp', 'tensor')
- gain_ffn_grad: float32 [1024], replicated
- w_ffn_gate_grad: float32 [1024, 2048], P('fsdp', 'tensor')
- w_ffn_up_grad: float32 [1024, 2048], P('fsdp', 'tensor')
- w_ffn_down_grad: float32 [1024, 2048], P('fsdp', 'tensor')
Inputs may be any that keep to these rules, and one draw needn't show every extreme that they name: `segments`: in each stream document numbers start at 0 and never fall; every one of the 3 documents is present, none is longer than 1024 tokens and one is exactly that long. `deal`: each row names every half-block once. Half-blocks h and 7 - h never stand in slots 2 c and 2 c + 1 of one c: for each such pair one stands in slot 2 c or 2 c + 1 and the other in slot 2 c' or 2 c' + 1 with c' = (c - 1) mod (4).
All inputs are finite; a program needn't handle non-finite values.
Results may differ from a plain program's by a relative error of at most 0.014.
Values may be sent and summed in bfloat16 or wider, within the bound.
A program may use at most 192 MiB of HBM per device.

v0:
```python
import math

import jax
import jax.numpy as jnp
from jax import lax
from jax.sharding import PartitionSpec as P

HEAD_DIM = 64
SSM_DIM = 64
STATE = 128
CONV = 4
SPAN = 256
QBLOCK = 512


exact = lax.Precision.HIGHEST
epsilon = 1e-05
masked = -1e30


def padded_2(cells, sides, width):
    for axis, dim in sides:
        count = lax.axis_size(axis)
        ends = count - 1
        head = lax.slice_in_dim(cells, 0, width, axis=dim)
        tail = lax.slice_in_dim(cells, cells.shape[dim] - width, cells.shape[dim], axis=dim)
        cells = jnp.concatenate(
            [
                lax.ppermute(tail, axis, [(i, (i + 1) % count) for i in range(ends)]),
                cells,
                lax.ppermute(head, axis, [((i + 1) % count, i) for i in range(ends)]),
            ],
            axis=dim,
        )
    return cells


def to_low(values):
    return lax.optimization_barrier(values.astype(jnp.bfloat16)).astype(jnp.float32)


def lowdot(left, right):
    return jnp.dot(left, right, preferred_element_type=jnp.float32)


def highdot(left, right):
    return jnp.dot(left, right.astype(jnp.float32), precision=exact)


def norm_rows(values, gain):
    scale = lax.rsqrt(jnp.mean(values * values, axis=-1, keepdims=True) + epsilon)
    return values * scale * gain


def swish_product(gate, upper):
    return jax.nn.silu(gate) * upper


def positions(segment_ids):
    count = segment_ids.shape[0]
    order = jnp.arange(count, dtype=jnp.int32)
    before = jnp.concatenate([jnp.full((1,), -1, jnp.int32), segment_ids[:-1]])
    starts = jnp.where(segment_ids != before, order, jnp.zeros_like(order))
    return (order - lax.cummax(starts, axis=0)).astype(jnp.float32)


def rotate(values, where_at):
    half = values.shape[-1] // 2
    freqs = 10000.0 ** (-jnp.arange(half, dtype=jnp.float32) / half)
    angles = where_at[:, None] * freqs[None, :]
    cosine = jnp.cos(angles)[:, None, :]
    sine = jnp.sin(angles)[:, None, :]
    first = values[..., :half]
    second = values[..., half:]
    return jnp.concatenate(
        [first * cosine - second * sine, second * cosine + first * sine], axis=-1
    )


def softmax_probs(grouped, keys, query_ids, key_ids, query_order, key_order):
    width = grouped.shape[3]
    scores = jnp.einsum("rkgd,skd->kgrs", grouped, keys, precision=exact) / math.sqrt(width)
    allowed = (key_order[None, :] <= query_order[:, None]) & (
        key_ids[None, :] == query_ids[:, None]
    )
    scores = jnp.where(allowed[None, None], scores, masked)
    highest = jnp.max(scores, axis=-1, keepdims=True)
    weights = jnp.exp(scores - highest)
    return weights / jnp.sum(weights, axis=-1, keepdims=True)


def attend_block(query, keys, values, query_ids, key_ids, query_order, key_order):
    count = query.shape[0]
    kv_heads = keys.shape[1]
    groups = query.shape[1] // kv_heads
    width = query.shape[2]
    grouped = query.reshape(count, kv_heads, groups, width)
    probs = to_low(softmax_probs(grouped, keys, query_ids, key_ids, query_order, key_order))
    result = jnp.einsum("kgrs,skd->rkgd", probs, values, precision=exact)
    return result.reshape(count, kv_heads * groups * width)


def attention(query, keys, values, query_ids, key_ids, query_order, key_order, block):
    count = query.shape[0]
    blocks = count // block

    def one_block(pieces):
        return attend_block(pieces[0], keys, values, pieces[1], key_ids, pieces[2], key_order)

    result = lax.map(
        one_block,
        (
            query.reshape((blocks, block) + query.shape[1:]),
            query_ids.reshape(blocks, block),
            query_order.reshape(blocks, block),
        ),
    )
    return result.reshape(count, -1)


def attention_back(
    query, keys, values, grad_result, query_ids, key_ids, query_order, key_order, block
):
    count = query.shape[0]
    blocks = count // block
    kv_heads = keys.shape[1]
    groups = query.shape[1] // kv_heads
    width = query.shape[2]

    def one_block(carry, pieces):
        query_part, grad_part, ids_part, order_part = pieces
        grouped = query_part.reshape(block, kv_heads, groups, width)
        grad_grouped = grad_part.reshape(block, kv_heads, groups, width)
        probs = softmax_probs(grouped, keys, ids_part, key_ids, order_part, key_order)
        probs_low = to_low(probs)
        grad_probs = jnp.einsum("rkgd,skd->kgrs", grad_grouped, values, precision=exact)
        grad_scores = (
            probs
            * (grad_probs - jnp.sum(probs * grad_probs, axis=-1, keepdims=True))
            / math.sqrt(width)
        )
        grad_query_part = jnp.einsum("kgrs,skd->rkgd", grad_scores, keys, precision=exact).reshape(
            block, kv_heads * groups, width
        )
        grad_keys_part = jnp.einsum("kgrs,rkgd->skd", grad_scores, grouped, precision=exact)
        grad_values_part = jnp.einsum("kgrs,rkgd->skd", probs_low, grad_grouped, precision=exact)
        return ((carry[0] + grad_keys_part, carry[1] + grad_values_part), grad_query_part)

    start = (jnp.zeros(keys.shape, jnp.float32), jnp.zeros(values.shape, jnp.float32))
    totals, grad_query = lax.scan(
        one_block,
        start,
        (
            query.reshape((blocks, block) + query.shape[1:]),
            grad_result.reshape(blocks, block, -1),
            query_ids.reshape(blocks, block),
            query_order.reshape(blocks, block),
        ),
    )
    return (grad_query.reshape(query.shape), totals[0], totals[1])


def causal_conv(values, rim_rows, taps, segment_ids, rim_ids):
    count = values.shape[0]
    width = taps.shape[0]
    padded = jnp.concatenate([rim_rows, values], axis=0)
    padded_ids = jnp.concatenate([rim_ids, segment_ids])
    result = jnp.zeros_like(values)
    for tap_index in range(width):
        window = padded[tap_index : tap_index + count]
        alike = (padded_ids[tap_index : tap_index + count] == segment_ids).astype(jnp.float32)
        result = result + taps[tap_index][None, :] * window * alike[:, None]
    return result


def ssd_block(state, pieces):
    inner_x, b_rows, c_rows, step, rate, segment_ids, before_id = pieces
    count = inner_x.shape[0]
    totals = jnp.cumsum(-rate, axis=0)
    order = jnp.arange(count, dtype=jnp.int32)
    alike = (segment_ids[:, None] == segment_ids[None, :]) & (order[None, :] <= order[:, None])
    gaps = totals[:, None, :] - totals[None, :, :]
    decays = jnp.exp(jnp.where(alike[:, :, None], gaps, masked))
    inner = jnp.dot(c_rows, b_rows.T, precision=exact)
    weights = decays * inner[:, :, None] * step[None, :, :]
    result = jnp.einsum("tsh,shp->thp", weights, inner_x, precision=exact)
    carry_on = (segment_ids == before_id).astype(jnp.float32)
    factor = jnp.exp(totals) * carry_on[:, None]
    result = result + factor[:, :, None] * jnp.einsum("hpn,tn->thp", state, c_rows, precision=exact)
    keep_last = (segment_ids == segment_ids[count - 1]).astype(jnp.float32)
    tails = jnp.exp(totals[count - 1][None, :] - totals) * keep_last[:, None] * step
    carried = (jnp.exp(totals[count - 1]) * carry_on[count - 1])[:, None, None] * state
    new_state = carried + jnp.einsum("sh,shp,sn->hpn", tails, inner_x, b_rows, precision=exact)
    return (new_state, result)


def ssd(inner_x, b_rows, c_rows, step, rate, segment_ids, first_before, state, span):
    count = inner_x.shape[0]
    blocks = count // span
    lasts = segment_ids[span - 1 :: span]
    befores = jnp.concatenate([jnp.reshape(first_before, (1,)), lasts[: blocks - 1]])

    def shaped(values):
        return values.reshape((blocks, span) + values.shape[1:])

    final, result = lax.scan(
        jax.checkpoint(ssd_block),
        state,
        (
            shaped(inner_x),
            shaped(b_rows),
            shaped(c_rows),
            shaped(step),
            shaped(rate),
            shaped(segment_ids),
            befores,
        ),
    )
    return (result.reshape(inner_x.shape), final)


def tensor_sum(values):
    return lax.psum(values, "tensor")


def per_device(
    tokens,
    segments,
    deal,
    gain_mix,
    w_query,
    w_keyval,
    w_attn_out,
    w_gate_z,
    w_in_x,
    w_bc,
    w_step,
    conv_x,
    conv_bc,
    step_bias,
    decay_log,
    skip,
    w_ssm_out,
    gain_ffn,
    w_ffn_gate,
    w_ffn_up,
    w_ffn_down,
    cotangent,
):
    row_count = tokens.shape[0]
    width_model = tokens.shape[1]
    half = row_count // 2
    tail_rows = CONV - 1
    segment_all = segments[0]
    deal_row = deal[0]
    ctx_count = lax.axis_size("context")
    halves = 2 * ctx_count
    device = lax.axis_index("context")
    last_device = (device == ctx_count - 1).astype(jnp.float32)

    def owner(which):
        return jnp.where(which < ctx_count, which, halves - 1 - which)

    half_ids = jnp.arange(halves, dtype=jnp.int32)
    slot_of = jnp.sum(
        jnp.where(deal_row[None, :] == half_ids[:, None], half_ids[None, :], 0), axis=1
    )
    held = lax.dynamic_slice_in_dim(deal_row, 2 * device, 2)
    targets = owner(held)
    mine_halves = jnp.stack([device, halves - 1 - device])
    sources = slot_of[mine_halves] // 2
    peer_ids = jnp.arange(ctx_count, dtype=jnp.int32)

    def into_slots(rows, goals):
        hit = goals[None, :] == peer_ids[:, None]
        empty = jnp.zeros_like(rows[0])
        return jnp.where(
            hit[:, 0, None, None],
            rows[0][None],
            jnp.where(hit[:, 1, None, None], rows[1][None], empty[None]),
        )

    sent = (
        into_slots(tokens.reshape(2, half, width_model), targets),
        into_slots(cotangent.reshape(2, half, width_model), targets),
    )
    arrived = (
        lax.all_to_all(sent[0], "context", split_axis=0, concat_axis=0, tiled=True),
        lax.all_to_all(sent[1], "context", split_axis=0, concat_axis=0, tiled=True),
    )
    work_tokens = jnp.take(arrived[0], sources, axis=0).reshape(row_count, width_model)
    work_cotangent = jnp.take(arrived[1], sources, axis=0).reshape(row_count, width_model)
    local_rows = jnp.arange(half, dtype=jnp.int32)
    half_starts = mine_halves * half
    order_mine = (half_starts[:, None] + local_rows[None, :]).reshape(row_count)
    where_all = positions(segment_all)
    segment_mine = jnp.take(segment_all, order_mine)
    where_mine = jnp.take(where_all, order_mine)
    side_ids = jnp.arange(2, dtype=jnp.int32)
    key_halves = jnp.where(
        side_ids[None, :] == 0, peer_ids[:, None], halves - 1 - peer_ids[:, None]
    )
    order_keys = (key_halves[:, :, None] * half + local_rows[None, None, :]).reshape(-1)
    segment_keys = jnp.take(segment_all, order_keys)
    before_ids = jnp.where(
        half_starts > 0, jnp.take(segment_all, jnp.maximum(half_starts - 1, 0)), -1
    )
    rim_index = half_starts[:, None] - tail_rows + jnp.arange(tail_rows, dtype=jnp.int32)[None, :]
    rim_ids = jnp.where(rim_index >= 0, jnp.take(segment_all, jnp.maximum(rim_index, 0)), -1)
    rim_mask = (mine_halves > 0).astype(jnp.float32)
    stream_slot = owner(half_ids) * 2 + (half_ids >= ctx_count).astype(jnp.int32)
    gathered = (
        lax.all_gather(w_query, "fsdp", axis=0, tiled=True),
        lax.all_gather(w_keyval, "fsdp", axis=0, tiled=True),
        lax.all_gather(w_attn_out, "fsdp", axis=0, tiled=True),
        lax.all_gather(w_gate_z, "fsdp", axis=0, tiled=True),
        lax.all_gather(w_in_x, "fsdp", axis=0, tiled=True),
        lax.all_gather(w_bc, "fsdp", axis=0, tiled=True),
        lax.all_gather(w_step, "fsdp", axis=0, tiled=True),
        lax.all_gather(w_ssm_out, "fsdp", axis=0, tiled=True),
        lax.all_gather(w_ffn_gate, "fsdp", axis=0, tiled=True),
        lax.all_gather(w_ffn_up, "fsdp", axis=0, tiled=True),
        lax.all_gather(w_ffn_down, "fsdp", axis=0, tiled=True),
    )
    (
        query_w,
        keyval_w,
        attn_w,
        gate_w,
        inner_w,
        bc_w,
        step_w,
        ssm_w,
        ffn_gate_w,
        ffn_up_w,
        ffn_down_w,
    ) = gathered

    def pack(query_raw, keyval_raw):
        query = rotate(query_raw.reshape(row_count, -1, HEAD_DIM), where_mine)
        pairs = keyval_raw.reshape(row_count, -1, 2, HEAD_DIM)
        keys = rotate(pairs[:, :, 0], where_mine)
        keyval = jnp.stack([keys, pairs[:, :, 1]], axis=2).reshape(row_count, -1)
        return (query, keyval)

    def convolve(inner_x, bc_raw, rims, taps_x, taps_bc):
        joined = jnp.concatenate([inner_x, bc_raw], axis=1).reshape(2, half, -1)
        taps = jnp.concatenate([taps_x, taps_bc], axis=1)
        convolved = jax.vmap(causal_conv, in_axes=(0, 0, None, 0, 0))(
            joined, rims, taps, segment_mine.reshape(2, half), rim_ids
        )
        convolved = jax.nn.silu(convolved).reshape(row_count, -1)
        inner_width = inner_x.shape[1]
        return (convolved[:, :inner_width], convolved[:, inner_width:])

    def scan_local(ssm_x, ssm_bc, step_raw, step_shift, decay_logs, skip_gain):
        heads = step_shift.shape[0]
        step = jax.nn.softplus(step_raw + step_shift)
        rate = step * jnp.exp(decay_logs)
        inner_x = ssm_x.reshape(row_count, heads, SSM_DIM)

        def one_half(x_rows, b_rows, c_rows, step_rows, rate_rows, segment_rows, before_one):
            start_state = jnp.zeros((heads, SSM_DIM, STATE), jnp.float32)
            result, final = ssd(
                x_rows,
                b_rows,
                c_rows,
                step_rows,
                rate_rows,
                segment_rows,
                before_one,
                start_state,
                SPAN,
            )
            keep_all = (segment_rows[half - 1] == before_one).astype(jnp.float32)
            return (result, final, jnp.exp(-jnp.sum(rate_rows, axis=0)) * keep_all)

        results, finals, decays = jax.vmap(one_half)(
            inner_x.reshape(2, half, heads, SSM_DIM),
            ssm_bc[:, :STATE].reshape(2, half, STATE),
            ssm_bc[:, STATE:].reshape(2, half, STATE),
            step.reshape(2, half, heads),
            rate.reshape(2, half, heads),
            segment_mine.reshape(2, half),
            before_ids,
        )
        return (
            results.reshape(row_count, heads, SSM_DIM) + skip_gain[None, :, None] * inner_x,
            finals,
            decays,
        )

    def finish(ssm_y, state_in, ssm_bc, gate_z, step_raw, step_shift, decay_logs):
        heads = step_shift.shape[0]
        step = jax.nn.softplus(step_raw + step_shift)
        rate = step * jnp.exp(decay_logs)
        totals = jnp.cumsum(-rate.reshape(2, half, heads), axis=1)
        carry_on = (segment_mine.reshape(2, half) == before_ids[:, None]).astype(jnp.float32)
        factor = jnp.exp(totals) * carry_on[:, :, None]
        incoming = jnp.einsum(
            "jhpn,jtn->jthp", state_in, ssm_bc[:, STATE:].reshape(2, half, STATE), precision=exact
        )
        full_y = ssm_y + (factor[:, :, :, None] * incoming).reshape(row_count, heads, SSM_DIM)
        return full_y.reshape(row_count, -1) * jax.nn.silu(gate_z)

    inputs = work_tokens.astype(jnp.float32)
    normed = to_low(norm_rows(inputs, gain_mix))
    normed_low = normed.astype(jnp.bfloat16)
    query_raw = lowdot(normed_low, query_w)
    keyval_raw = lowdot(normed_low, keyval_w)
    gate_z = lowdot(normed_low, gate_w)
    inner_x = lowdot(normed_low, inner_w)
    bc_raw = lowdot(normed_low, bc_w)
    step_raw = lowdot(normed_low, step_w)
    query_full, keyval_full = pack(query_raw, keyval_raw)
    query = to_low(query_full)
    keyval = to_low(keyval_full)
    keyval_all = lax.all_gather(keyval.astype(jnp.bfloat16), "context", axis=0, tiled=True).astype(
        jnp.float32
    )
    pairs = keyval_all.reshape(keyval_all.shape[0], -1, 2, HEAD_DIM)
    keys_all = pairs[:, :, 0]
    values_all = pairs[:, :, 1]
    edges = jnp.concatenate([inner_x, bc_raw], axis=1).reshape(2, half, -1)[:, half - tail_rows :]
    padded_edges = padded_2(jnp.stack([edges[1], edges[0]]), (("context", 0),), 1)
    rim_second = padded_edges[3] + last_device * edges[0]
    rims = jnp.stack([padded_edges[0], rim_second]) * rim_mask[:, None, None]
    attended = to_low(
        attention(
            query, keys_all, values_all, segment_mine, segment_keys, order_mine, order_keys, QBLOCK
        )
    )
    conv_inner, conv_bc_rows = convolve(inner_x, bc_raw, rims, conv_x, conv_bc)
    ssm_x = to_low(conv_inner)
    ssm_bc = to_low(conv_bc_rows)
    ssm_y, finals, decays = scan_local(ssm_x, ssm_bc, step_raw, step_bias, decay_log, skip)
    all_decays, all_finals = (
        lax.all_gather(decays, "context", axis=0, tiled=True),
        lax.all_gather(finals, "context", axis=0, tiled=True),
    )
    decay_stream = jnp.take(all_decays, stream_slot, axis=0)
    final_stream = jnp.take(all_finals, stream_slot, axis=0)

    def advance(carry, pieces):
        return (pieces[0][:, None, None] * carry + pieces[1], carry)

    zero_state = jnp.zeros(finals.shape[1:], jnp.float32)
    ins_stream = lax.scan(advance, zero_state, (decay_stream, final_stream))[1]
    state_in = jnp.take(ins_stream, mine_halves, axis=0)
    gated = to_low(finish(ssm_y, state_in, ssm_bc, gate_z, step_raw, step_bias, decay_log))
    mixer_part = lowdot(attended.astype(jnp.bfloat16), attn_w.T) + lowdot(
        gated.astype(jnp.bfloat16), ssm_w.T
    )
    mixed_rows = inputs + tensor_sum(mixer_part)
    normed_ffn = to_low(norm_rows(mixed_rows, gain_ffn))
    ffn_low = normed_ffn.astype(jnp.bfloat16)
    gate = lowdot(ffn_low, ffn_gate_w)
    upper = lowdot(ffn_low, ffn_up_w)
    hidden = to_low(swish_product(gate, upper))
    hidden_low = hidden.astype(jnp.bfloat16)
    output = mixed_rows + tensor_sum(lowdot(hidden_low, ffn_down_w.T))
    back_weights = (
        lax.all_gather(w_query, "fsdp", axis=0, tiled=True),
        lax.all_gather(w_keyval, "fsdp", axis=0, tiled=True),
        lax.all_gather(w_attn_out, "fsdp", axis=0, tiled=True),
        lax.all_gather(w_gate_z, "fsdp", axis=0, tiled=True),
        lax.all_gather(w_in_x, "fsdp", axis=0, tiled=True),
        lax.all_gather(w_bc, "fsdp", axis=0, tiled=True),
        lax.all_gather(w_step, "fsdp", axis=0, tiled=True),
        lax.all_gather(w_ssm_out, "fsdp", axis=0, tiled=True),
        lax.all_gather(w_ffn_gate, "fsdp", axis=0, tiled=True),
        lax.all_gather(w_ffn_up, "fsdp", axis=0, tiled=True),
        lax.all_gather(w_ffn_down, "fsdp", axis=0, tiled=True),
    )
    (
        query_b,
        keyval_b,
        attn_b,
        gate_b,
        inner_b,
        bc_b,
        step_b,
        ssm_b,
        ffn_gate_b,
        ffn_up_b,
        ffn_down_b,
    ) = back_weights
    grad_out = work_cotangent.astype(jnp.float32)
    grad_hidden = to_low(lowdot(work_cotangent, ffn_down_b))
    grad_ffn_down = lowdot(work_cotangent.T, hidden_low)
    pull_swish = jax.vjp(swish_product, gate, upper)[1]
    grad_gate_raw, grad_up_raw = pull_swish(grad_hidden)
    grad_gate_low = grad_gate_raw.astype(jnp.bfloat16)
    grad_up_low = grad_up_raw.astype(jnp.bfloat16)
    grad_ffn_gate = lowdot(ffn_low.T, grad_gate_low)
    grad_ffn_up = lowdot(ffn_low.T, grad_up_low)
    grad_normed_ffn = tensor_sum(
        lowdot(grad_gate_low, ffn_gate_b.T) + lowdot(grad_up_low, ffn_up_b.T)
    )
    pull_norm_ffn = jax.vjp(norm_rows, mixed_rows, gain_ffn)[1]
    grad_mixed_norm, grad_gain_ffn = pull_norm_ffn(grad_normed_ffn)
    grad_mixed = grad_out + grad_mixed_norm
    grad_attn_out = highdot(grad_mixed.T, attended)
    grad_ssm_out = highdot(grad_mixed.T, gated)
    pull_finish = jax.vjp(finish, ssm_y, state_in, ssm_bc, gate_z, step_raw, step_bias, decay_log)[
        1
    ]
    (
        grad_ssm_y,
        grad_state_in,
        grad_bc_finish,
        grad_gate_z,
        grad_step_finish,
        grad_shift_finish,
        grad_decay_finish,
    ) = pull_finish(to_low(highdot(grad_mixed, ssm_b)))
    all_state_grads = lax.all_gather(grad_state_in, "context", axis=0, tiled=True)
    direct_stream = jnp.take(all_state_grads, stream_slot, axis=0)

    def retreat(carry, pieces):
        return (pieces[1] + pieces[0][:, None, None] * carry, carry)

    later_stream = lax.scan(retreat, zero_state, (decay_stream, direct_stream), reverse=True)[1]
    grad_finals = jnp.take(later_stream, mine_halves, axis=0)
    grad_decays = jnp.sum(grad_finals * state_in, axis=(2, 3))
    pull_scan = jax.vjp(scan_local, ssm_x, ssm_bc, step_raw, step_bias, decay_log, skip)[1]
    grad_ssm_x, grad_bc_scan, grad_step_scan, grad_shift_scan, grad_decay_scan, grad_skip = (
        pull_scan((grad_ssm_y, grad_finals, grad_decays))
    )
    grad_ssm_bc = tensor_sum(grad_bc_finish + grad_bc_scan)
    grad_attended = to_low(highdot(grad_mixed, attn_b))
    grad_query_full, grad_keys_all, grad_values_all = attention_back(
        query,
        keys_all,
        values_all,
        grad_attended,
        segment_mine,
        segment_keys,
        order_mine,
        order_keys,
        QBLOCK,
    )
    grad_query = to_low(grad_query_full)
    grad_keyval_all = jnp.stack([grad_keys_all, grad_values_all], axis=2).reshape(
        keyval_all.shape[0], -1
    )
    grad_keyval = to_low(
        lax.psum_scatter(grad_keyval_all, "context", scatter_dimension=0, tiled=True)
    )
    pull_pack = jax.vjp(pack, query_raw, keyval_raw)[1]
    grad_query_raw, grad_keyval_raw = pull_pack((grad_query, grad_keyval))
    pull_conv = jax.vjp(convolve, inner_x, bc_raw, rims, conv_x, conv_bc)[1]
    grad_inner, grad_bc_raw, grad_rims, grad_conv_x, grad_conv_bc = pull_conv(
        (grad_ssm_x, grad_ssm_bc)
    )
    grad_pair = jnp.stack([grad_rims[0], grad_rims[1] * (1.0 - last_device)])
    padded_grads = padded_2(grad_pair, (("context", 0),), 1)
    rim_back = jnp.stack([padded_grads[3] + last_device * grad_rims[1], padded_grads[0]])
    inner_width = inner_x.shape[1]
    grad_joined = jnp.concatenate([grad_inner, grad_bc_raw], axis=1).reshape(2, half, -1)
    grad_joined = (
        grad_joined + jnp.pad(rim_back, ((0, 0), (half - tail_rows, 0), (0, 0)))
    ).reshape(row_count, -1)
    grad_inner = grad_joined[:, :inner_width]
    grad_bc_raw = grad_joined[:, inner_width:]
    grad_step = grad_step_finish + grad_step_scan
    grad_w_query = highdot(normed.T, grad_query_raw)
    grad_w_keyval = highdot(normed.T, grad_keyval_raw)
    grad_w_gate_z = highdot(normed.T, grad_gate_z)
    grad_w_in_x = highdot(normed.T, grad_inner)
    grad_w_bc = highdot(normed.T, grad_bc_raw)
    grad_w_step = highdot(normed.T, grad_step)
    heads_part = (
        highdot(grad_query_raw, query_b.T)
        + highdot(grad_keyval_raw, keyval_b.T)
        + highdot(grad_gate_z, gate_b.T)
        + highdot(grad_inner, inner_b.T)
        + highdot(grad_step, step_b.T)
    )
    grad_normed = tensor_sum(heads_part) + highdot(grad_bc_raw, bc_b.T)
    pull_norm_mix = jax.vjp(norm_rows, inputs, gain_mix)[1]
    grad_inputs_norm, grad_gain_mix = pull_norm_mix(grad_normed)
    work_grad = (grad_mixed + grad_inputs_norm).astype(jnp.bfloat16)
    leaving = (
        into_slots(output.astype(jnp.bfloat16).reshape(2, half, width_model), sources),
        into_slots(work_grad.reshape(2, half, width_model), sources),
    )
    returned = (
        lax.all_to_all(leaving[0], "context", split_axis=0, concat_axis=0, tiled=True),
        lax.all_to_all(leaving[1], "context", split_axis=0, concat_axis=0, tiled=True),
    )
    mixed_out = jnp.take(returned[0], targets, axis=0).reshape(row_count, width_model)
    tokens_grad = jnp.take(returned[1], targets, axis=0).reshape(row_count, width_model)
    reduced = (
        lax.psum_scatter(grad_w_query, "fsdp", scatter_dimension=0, tiled=True),
        lax.psum_scatter(grad_w_keyval, "fsdp", scatter_dimension=0, tiled=True),
        lax.psum_scatter(grad_attn_out, "fsdp", scatter_dimension=0, tiled=True),
        lax.psum_scatter(grad_w_gate_z, "fsdp", scatter_dimension=0, tiled=True),
        lax.psum_scatter(grad_w_in_x, "fsdp", scatter_dimension=0, tiled=True),
        lax.psum_scatter(grad_w_bc, "fsdp", scatter_dimension=0, tiled=True),
        lax.psum_scatter(grad_w_step, "fsdp", scatter_dimension=0, tiled=True),
        lax.psum_scatter(grad_ssm_out, "fsdp", scatter_dimension=0, tiled=True),
        lax.psum_scatter(grad_ffn_gate, "fsdp", scatter_dimension=0, tiled=True),
        lax.psum_scatter(grad_ffn_up, "fsdp", scatter_dimension=0, tiled=True),
        lax.psum_scatter(grad_ffn_down, "fsdp", scatter_dimension=0, tiled=True),
    )
    reduced = lax.psum(
        (
            reduced[0],
            reduced[1],
            reduced[2],
            reduced[3],
            reduced[4],
            reduced[5],
            reduced[6],
            reduced[7],
            reduced[8],
            reduced[9],
            reduced[10],
        ),
        "context",
    )
    smaller = lax.psum(
        (
            grad_gain_mix,
            grad_conv_x,
            grad_conv_bc,
            grad_shift_finish + grad_shift_scan,
            grad_decay_finish + grad_decay_scan,
            grad_skip,
            grad_gain_ffn,
        ),
        ("fsdp", "context"),
    )
    return (
        mixed_out,
        tokens_grad,
        smaller[0],
        reduced[0],
        reduced[1],
        reduced[2],
        reduced[3],
        reduced[4],
        reduced[5],
        reduced[6],
        smaller[1],
        smaller[2],
        smaller[3],
        smaller[4],
        smaller[5],
        reduced[7],
        smaller[6],
        reduced[8],
        reduced[9],
        reduced[10],
    )


def solution(mesh):
    in_specs = (
        P(("fsdp", "context"), None),
        P("fsdp", None),
        P("fsdp", None),
        P(),
        P("fsdp", "tensor"),
        P("fsdp", "tensor"),
        P("fsdp", "tensor"),
        P("fsdp", "tensor"),
        P("fsdp", "tensor"),
        P("fsdp", None),
        P("fsdp", "tensor"),
        P(None, "tensor"),
        P(),
        P("tensor"),
        P("tensor"),
        P("tensor"),
        P("fsdp", "tensor"),
        P(),
        P("fsdp", "tensor"),
        P("fsdp", "tensor"),
        P("fsdp", "tensor"),
        P(("fsdp", "context"), None),
    )
    out_specs = (
        P(("fsdp", "context"), None),
        P(("fsdp", "context"), None),
        P(),
        P("fsdp", "tensor"),
        P("fsdp", "tensor"),
        P("fsdp", "tensor"),
        P("fsdp", "tensor"),
        P("fsdp", "tensor"),
        P("fsdp", None),
        P("fsdp", "tensor"),
        P(None, "tensor"),
        P(),
        P("tensor"),
        P("tensor"),
        P("tensor"),
        P("fsdp", "tensor"),
        P(),
        P("fsdp", "tensor"),
        P("fsdp", "tensor"),
        P("fsdp", "tensor"),
    )
    return jax.shard_map(
        per_device, mesh=mesh, in_specs=in_specs, out_specs=out_specs, check_vma=False
    )
```

profile of v0, /device:TPU:0, one launch (start us, length us, event | category | flops | bytes accessed | tf_op | source)
XLA Modules:
  0.0 1364.4 jit_solution(2577400445979137679)
XLA Ops:
  12.2 5.3 all-to-all-start
  24.4 23.7 %all_gather.61 = bf16[1024,256]{1,0:T(8,128)(2,1)S(1)} all-gather(bf16[256,256]{1,0:T(8,128)(2,1)S(1)} %copy-done.108), channel_id=1, replica_groups=mesh['fsdp'=4,'context'=4,'tensor'=2] {'fsdp'}, dimensions={0}, use_global_device_ids=true | all-gather | bytes 655360 | tf_op jit(solution)/shard_map/all_gather | solution.py:318
  49.0 13.4 all_gather.62
  77.3 3.7 collective-permute-done.1
  81.0 4.6 collective-permute-start
  100.1 13.9 %all_gather.56 = bf16[1024,128]{1,0:T(8,128)(2,1)S(1)} all-gather(bf16[256,128]{1,0:T(8,128)(2,1)S(1)} %copy-done.118), channel_id=1, replica_groups=mesh['fsdp'=4,'context'=4,'tensor'=2] {'fsdp'}, dimensions={0}, use_global_device_ids=true | all-gather | bytes 327680 | tf_op jit(solution)/shard_map/all_gather | solution.py:314
  117.9 15.5 %all_gather.58 = bf16[1024,256]{1,0:T(8,128)(2,1)} all-gather(bf16[256,256]{1,0:T(8,128)(2,1)S(1)} %copy-done.109), channel_id=1, replica_groups=mesh['fsdp'=4,'context'=4,'tensor'=2] {'fsdp'}, dimensions={0}, use_global_device_ids=true | all-gather | bytes 655360 | tf_op jit(solution)/shard_map/all_gather | solution.py:313
  133.7 11.8 gather_fusion.2
  149.0 19.4 %all_gather.59 = bf16[1024,256]{1,0:T(8,128)(2,1)S(1)} all-gather(bf16[256,256]{1,0:T(8,128)(2,1)S(1)} %copy-done.110), channel_id=1, replica_groups=mesh['fsdp'=4,'context'=4,'tensor'=2] {'fsdp'}, dimensions={0}, use_global_device_ids=true | all-gather | bytes 655360 | tf_op jit(solution)/shard_map/all_gather | solution.py:315
  171.3 11.3 all_gather.57
  186.2 3.7 fusion.10
  192.1 4.2 fusion.27
  199.8 6.7 all-gather
  209.1 5.8 bitcast_add_fusion.4
  220.4 4.4 gather_fusion.8
  224.8 4.2 broadcast_select_fusion.1
  231.0 15.3 %while.20 = (s32[]{:T(128)}, f32[12,64,128]{2,1,0:T(8,128)S(1)}, f32[8,12,64,128]{3,2,1,0:T(8,128)}, f32[8,12]{1,0:T(8,128)S(1)}, f32[8,12,64,128]{3,2,1,0:T(8,128)}, /*index=5*/s32[]{:T(128)}, s32[]{:T(128)}) while((s32[]{:T(128)}, f32[12,64,128]{2,1,0:T(8,128)S(1)}, f32[8,12,64,128]{3,2,1,0:T(8,128)}, f32[8,12]{1,0:T(8,128)S(1)}, ...), condition=%wide.region_10.13_spmd.clone, body=%wide.region_9.12_spmd.clone.sunk | while | flops 393219 | bytes 1966832 | solution.py:448
  258.5 4.6 multiply_convert_fusion.3
  269.3 19.2 %all_to_all.20 = bf16[4,256,1024]{2,1,0:T(8,128)(2,1)} all-to-all(bf16[4,256,1024]{2,1,0:T(8,128)(2,1)S(1)} %copy-done.34), channel_id=1, replica_groups=mesh['fsdp'=4,'context'=4,'tensor'=2] {'context'}, dimensions={0} | all-to-all | bytes 4194304 | tf_op jit(solution)/shard_map/all_to_all | solution.py:289
  291.1 4.2 convolution_convert_fusion
  299.1 39.4 %all-gather.20.cloned.1.call-done = bf16[1024,1024]{1,0:T(8,128)(2,1)} async-done(((bf16[256,1024]{1,0:T(8,128)(2,1)}), bf16[1024,1024]{1,0:T(8,128)(2,1)}) %all-gather.20.cloned.1.call-update) | async-done | bytes 2097168 | tf_op jit(solution)/shard_map/all_gather | solution.py:322
  338.5 4.5 fusion.201
  343.0 41.8 %all-gather.18.cloned.1.call-done = bf16[1024,1024]{1,0:T(8,128)(2,1)} async-done(((bf16[256,1024]{1,0:T(8,128)(2,1)}), bf16[1024,1024]{1,0:T(8,128)(2,1)}) %all-gather.18.cloned.1.call-update) | async-done | bytes 2097168 | tf_op jit(solution)/shard_map/all_gather | solution.py:321
  384.8 6.0 fusion.53
  411.1 5.4 all-reduce.33.cloned.1.call-done
  435.3 14.7 %fusion.6 = (f32[4,512]{1,0:T(4,128)S(1)}, f32[2048,512,4]{1,0,2:T(8,128)}) fusion(f32[4,512]{1,0:T(4,128)} %copy-done.130, f32[4,512]{1,0:T(4,128)S(1)} %get-tuple-element.544, f32[2048,512,4]{1,0,2:T(8,128)} %copy-done.2, pred[512,2048]{0,1:T(8,128)(4,1)} %copy-done.32, bf16[512,4,64]{0,2,1:T(8,128)(2,1)S(1)} %bitcast.517, ...), kind=kOutput, calls=%fused_computation.30 | convolution fusion | flops 562034688 | bytes 35151872 | tf_op jit(solution)/shard_map/while/body/eval_jaxpr/rkgd,skd->kgrs/dot_general | solution.py:136
  450.0 6.2 fusion.42
  456.2 21.3 %fusion.45 = f32[2048,1,1,64]{0,3,2,1:T(8,128)S(1)} fusion(bf16[512,4,64]{0,2,1:T(8,128)(2,1)S(1)} %copy-done.99, f32[2048,512,4]{1,0,2:T(8,128)} %get-tuple-element.548, f32[4,512]{1,0:T(4,128)S(1)} %get-tuple-element.547, f32[4,512]{1,0:T(4,128)S(1)} %copy-done.131, f32[4,512]{1,0:T(4,128)S(1)} %get-tuple-element.544, f32[2048,512,4]{1,0,2:T(8,128)} %copy-done.2, ...), kind=kOutput, calls=%fused_computation.82 | convolution fusion | flops 3250585600 | bytes 35414016 | tf_op jit(solution)/shard_map/while/body/eval_jaxpr/kgrs,rkgd->skd/dot_general | solution.py:145
  482.3 4.5 gather_fusion.12
  486.8 4.2 broadcast_select_fusion
  493.0 20.9 %while.21 = (s32[]{:T(128)}, f32[12,64,128]{2,1,0:T(8,128)S(1)}, f32[8,12,64,128]{3,2,1,0:T(8,128)}, f32[8,12,64,128]{3,2,1,0:T(8,128)}, f32[8,12]{1,0:T(8,128)}, /*index=5*/s32[]{:T(128)}, s32[]{:T(128)}, s32[]{:T(128)}) while((s32[]{:T(128)}, f32[12,64,128]{2,1,0:T(8,128)S(1)}, f32[8,12,64,128]{3,2,1,0:T(8,128)}, ...), condition=%wide.region_21.26_spmd.clone, body=%wide.region_20.25_spmd.clone.sunk | while | flops 393220 | bytes 1966344 | solution.py:523
  528.6 11.0 fusion.28
  560.8 4.4 fusion.210
  565.3 23.2 %fusion.100 = bf16[512,4,64]{0,2,1:T(8,128)(2,1)S(1)} fusion(f32[2048,512,4]{1,0,2:T(8,128)} %get-tuple-element.548, f32[4,512]{1,0:T(4,128)} %copy-done.193, f32[4,512]{1,0:T(4,128)} %copy-done.130, f32[4,512]{1,0:T(4,128)S(1)} %get-tuple-element.544, f32[2048,512,4]{1,0,2:T(8,128)} %copy-done.2, pred[512,2048]{0,1:T(8,128)(4,1)} %copy-done.32, ...), kind=kOutput, calls=%fused_computation.180 | convolution fusion | flops 3250716672 | bytes 35151872 | tf_op jit(solution)/shard_map/while/body/eval_jaxpr/kgrs,skd->rkgd/dot_general | solution.py:142
  596.1 5.7 fusion.179
  601.9 4.9 fusion.213
  607.2 6.3 fusion.212
  613.6 5.8 fusion.211
  619.4 4.9 fusion.214
  625.3 6.9 bitcast_add_fusion.3
  641.1 6.1 multiply_reduce_fusion.4
  652.7 4.3 collective-permute-done.2
  657.8 4.5 collective-permute-start.3
  667.7 6.3 fusion.81
  674.1 4.6 fusion.202
  679.5 5.2 reduce-window.59
  685.0 4.6 fusion.204
  689.7 4.1 fusion.206
  703.6 5.0 reduce-window.73
  712.8 6.2 add_add_fusion.2
  720.4 18.8 %reduce-scatter.33.cloned.1.call-done = f32[256,1024]{1,0:T(8,128)} async-done(((f32[1024,1024]{1,0:T(8,128)}), f32[256,1024]{1,0:T(8,128)}) %reduce-scatter.33.cloned.1.call-update) | async-done | bytes 1048592 | tf_op jit(solution)/shard_map/reduce_scatter | solution.py:604
  739.2 79.6 %reduce-scatter.31.cloned.1.call-done = f32[256,1024]{1,0:T(8,128)} async-done(((f32[1024,1024]{1,0:T(8,128)}), f32[256,1024]{1,0:T(8,128)}) %reduce-scatter.31.cloned.1.call-update) | async-done | bytes 1048592 | tf_op jit(solution)/shard_map/reduce_scatter | solution.py:603
  818.8 62.9 %reduce-scatter.29.cloned.1.call-done = f32[256,768]{1,0:T(8,128)} async-done(((f32[1024,768]{1,0:T(8,128)}), f32[256,768]{1,0:T(8,128)}) %reduce-scatter.29.cloned.1.call-update) | async-done | bytes 786448 | tf_op jit(solution)/shard_map/reduce_scatter | solution.py:602
  881.7 62.6 %reduce-scatter.21.cloned.1.call-done = f32[256,768]{1,0:T(8,128)} async-done(((f32[1024,768]{1,0:T(8,128)}), f32[256,768]{1,0:T(8,128)}) %reduce-scatter.21.cloned.1.call-update) | async-done | bytes 786448 | tf_op jit(solution)/shard_map/reduce_scatter | solution.py:598
  944.3 79.0 %reduce-scatter.35.cloned.1.call-done = f32[256,1024]{1,0:T(8,128)} async-done(((f32[1024,1024]{1,0:T(8,128)}), f32[256,1024]{1,0:T(8,128)}) %reduce-scatter.35.cloned.1.call-update) | async-done | bytes 1048592 | tf_op jit(solution)/shard_map/reduce_scatter | solution.py:605
  1023.3 30.7 %reduce-scatter.25.cloned.1.call-done = f32[256,256]{1,0:T(8,128)} async-done(((f32[1024,256]{1,0:T(8,128)}), f32[256,256]{1,0:T(8,128)}) %reduce-scatter.25.cloned.1.call-update) | async-done | bytes 262160 | tf_op jit(solution)/shard_map/reduce_scatter | solution.py:600
  1053.9 61.2 %reduce-scatter.23.cloned.1.call-done = f32[256,768]{1,0:T(8,128)} async-done(((f32[1024,768]{1,0:T(8,128)}), f32[256,768]{1,0:T(8,128)}) %reduce-scatter.23.cloned.1.call-update) | async-done | bytes 786448 | tf_op jit(solution)/shard_map/reduce_scatter | solution.py:599
  1115.9 30.4 %all-reduce.39.cloned.1.call-done = (f32[512,1024]{1,0:T(8,128)}, f32[512,1024]{1,0:T(8,128)}) async-done(((f32[512,1024]{1,0:T(8,128)}, f32[512,1024]{1,0:T(8,128)}), (f32[512,1024]{1,0:T(8,128)}, f32[512,1024]{1,0:T(8,128)})) %all-reduce.39.cloned.1.call-update) | async-done | bytes 4194320 | tf_op jit(solution)/shard_map/psum | solution.py:223
  1146.4 3.6 fusion.63
  1154.7 33.3 %all_to_all.21 = bf16[4,256,1024]{2,1,0:T(8,128)(2,1)} all-to-all(bf16[4,256,1024]{2,1,0:T(8,128)(2,1)S(1)} %get-tuple-element.525), channel_id=1, replica_groups=mesh['fsdp'=4,'context'=4,'tensor'=2] {'context'}, dimensions={0} | all-to-all | bytes 4194304 | tf_op jit(solution)/shard_map/all_to_all | solution.py:589
  1188.0 3.8 all-to-all-start.3
  1192.2 57.2 %psum.173 = f32[256,12]{0,1:T(8,128)} all-reduce(f32[256,12]{0,1:T(8,128)} %reduce-scatter.27.cloned.1.call-done), channel_id=1, replica_groups=mesh['fsdp'=4,'context'=4,'tensor'=2] {'context'}, use_global_device_ids=true, to_apply=%region_56.61 | all-reduce | flops 3072 | bytes 24576 | tf_op jit(solution)/shard_map/psum | solution.py:607
  1249.4 76.9 %all-reduce.22 = (f32[1024]{0:T(1024)}, f32[4,768]{1,0:T(4,128)}, f32[4,256]{1,0:T(4,128)}, f32[12]{0:T(128)}, f32[12]{0:T(128)}, /*index=5*/f32[12]{0:T(128)}, f32[1024]{0:T(1024)}) all-reduce(f32[1024]{0:T(1024)S(1)} %get-tuple-element.392, ...), channel_id=1, replica_groups=mesh['fsdp'=4,'context'=4,'tensor'=2] {'fsdp','context'}, use_global_device_ids=true, to_apply=%region_42.47 | all-reduce | flops 6180 | bytes 49440 | tf_op jit(solution)/shard_map/psum | solution.py:623
  1332.8 12.0 all-reduce.37.cloned.1.call-done
  (803 shorter events, 283.1 us)
Async XLA Ops:
  12.2 50.4 %all-to-all-start = ((bf16[4,256,1024]{2,1,0:T(8,128)(2,1)}), bf16[4,256,1024]{2,1,0:T(8,128)(2,1)}, u32[]{:S(2)}, u32[]{:S(2)}) async-start(bf16[4,256,1024]{2,1,0:T(8,128)(2,1)} %get-tuple-element.527), calls=%async_computation | async-start | bytes 4194304 | tf_op jit(solution)/shard_map/all_to_all | solution.py:288
  17.6 54.0 %all-gather.10.cloned.1.call-start = ((), (), s32[]{:S(2)}) async-start(), calls=%async_computation.16 | async-start | bytes 1966080 | tf_op jit(solution)/shard_map/all_gather | solution.py:317
  18.3 202.1 %all-gather.12.cloned.1.call-start = ((), (), s32[]{:S(2)}) async-start(), calls=%async_computation.17 | async-start | bytes 3932160 | tf_op jit(solution)/shard_map/all_gather | solution.py:439
  19.3 46.1 %copy-start.155 = (pred[2]{0:T(512)(128)(4,1)}, pred[2]{0:T(512)(128)(4,1)S(1)}, u32[]{:S(2)}) copy-start(pred[2]{0:T(512)(128)(4,1)S(1)} %get-tuple-element.459) | copy-start | bytes 10
  19.3 43.4 %copy-start.165 = (s32[1024]{0:T(1024)}, s32[1024]{0:T(1024)S(1)}, u32[]{:S(2)}) copy-start(s32[1024]{0:T(1024)S(1)} %pad_clamp_fusion.7) | copy-start | bytes 12292
  19.4 29.6 %copy-start.184 = (f32[12]{0:T(128)S(1)}, f32[12]{0:T(128)}, u32[]{:S(2)}) copy-start(f32[12]{0:T(128)} %param.47) | copy-start | bytes 148
  19.4 29.6 %copy-start.164 = (bf16[256,12]{0,1:T(8,128)(2,1)S(1)}, bf16[256,12]{0,1:T(8,128)(2,1)}, u32[]{:S(2)}) copy-start(bf16[256,12]{0,1:T(8,128)(2,1)} %param.43) | copy-start | bytes 18436
  20.6 44.3 %copy-start.170 = (s32[2]{0:T(128)}, s32[2]{0:T(128)S(1)}, u32[]{:S(2)}) copy-start(s32[2]{0:T(128)S(1)} %get-tuple-element.338) | copy-start | bytes 28
  24.1 122.9 %copy-start.116 = (s32[2,256]{1,0:T(2,128)}, s32[2,256]{1,0:T(2,128)S(1)}, u32[]{:S(2)}) copy-start(s32[2,256]{1,0:T(2,128)S(1)} %get-tuple-element.337) | copy-start | bytes 6148
  24.1 182.5 %copy-start.138 = (f32[2,256]{1,0:T(2,128)}, f32[2,256]{1,0:T(2,128)S(1)}, u32[]{:S(2)}) copy-start(f32[2,256]{1,0:T(2,128)S(1)} %get-tuple-element.455) | copy-start | bytes 6148
  62.6 24.5 %copy-start.144 = (f32[2,256]{1,0:T(2,128)}, f32[2,256]{1,0:T(2,128)S(1)}, u32[]{:S(2)}) copy-start(f32[2,256]{1,0:T(2,128)S(1)} %get-tuple-element.514) | copy-start | bytes 6148
  62.6 24.5 %copy-start.146 = (f32[2,256]{1,0:T(2,128)}, f32[2,256]{1,0:T(2,128)S(1)}, u32[]{:S(2)}) copy-start(f32[2,256]{1,0:T(2,128)S(1)} %get-tuple-element.515) | copy-start | bytes 6148
  62.6 24.5 %copy-start.148 = (f32[2,256]{1,0:T(2,128)}, f32[2,256]{1,0:T(2,128)S(1)}, u32[]{:S(2)}) copy-start(f32[2,256]{1,0:T(2,128)S(1)} %get-tuple-element.516) | copy-start | bytes 6148
  62.6 24.4 %copy-start.122 = (f32[1,1024]{1,0:T(1,128)}, f32[1,1024]{1,0:T(1,128)S(1)}, u32[]{:S(2)}) copy-start(f32[1,1024]{1,0:T(1,128)S(1)} %get-tuple-element.510) | copy-start | bytes 12292
  62.6 24.4 %copy-start.124 = (f32[1,1024]{1,0:T(1,128)}, f32[1,1024]{1,0:T(1,128)S(1)}, u32[]{:S(2)}) copy-start(f32[1,1024]{1,0:T(1,128)S(1)} %get-tuple-element.511) | copy-start | bytes 12292
  62.7 24.4 %copy-start.126 = (f32[1,1024]{1,0:T(1,128)}, f32[1,1024]{1,0:T(1,128)S(1)}, u32[]{:S(2)}) copy-start(f32[1,1024]{1,0:T(1,128)S(1)} %get-tuple-element.512) | copy-start | bytes 12292
  62.7 24.4 %copy-start.128 = (f32[1,1024]{1,0:T(1,128)}, f32[1,1024]{1,0:T(1,128)S(1)}, u32[]{:S(2)}) copy-start(f32[1,1024]{1,0:T(1,128)S(1)} %get-tuple-element.513) | copy-start | bytes 12292
  75.3 5.6 collective-permute-start.1
  77.3 131.7 %copy-start.107 = (f32[2,256,12]{1,2,0:T(8,128)}, f32[2,256,12]{1,2,0:T(8,128)S(1)}, u32[]{:S(2)}) copy-start(f32[2,256,12]{1,2,0:T(8,128)S(1)} %get-tuple-element.503) | copy-start | bytes 73732
  81.0 6.0 collective-permute-start
  89.8 168.7 %copy-start.28 = (bf16[512,768]{1,0:T(8,128)(2,1)}, bf16[512,768]{1,0:T(8,128)(2,1)S(1)}, u32[]{:S(2)}) copy-start(bf16[512,768]{1,0:T(8,128)(2,1)S(1)} %slice.366) | copy-start | bytes 2359300
  89.9 159.6 %copy-start.53 = (bf16[512,128]{1,0:T(8,128)(2,1)}, bf16[512,128]{1,0:T(8,128)(2,1)S(1)}, u32[]{:S(2)}) copy-start(bf16[512,128]{1,0:T(8,128)(2,1)S(1)} %get-tuple-element.494) | copy-start | bytes 393220
  97.6 160.9 %all-gather.14.cloned.1.call-start = ((), (), s32[]{:S(2)}) async-start(), calls=%async_computation.18 | async-start | bytes 1966080 | tf_op jit(solution)/shard_map/all_gather | solution.py:316
  98.3 164.8 %all-gather.16.cloned.1.call-start = ((), (), s32[]{:S(2)}) async-start(), calls=%async_computation.19 | async-start | bytes 1966080 | tf_op jit(solution)/shard_map/all_gather | solution.py:320
  98.9 192.2 %all-gather.22.cloned.1.call-start = ((), (), s32[]{:S(2)}) async-start(), calls=%async_computation.23 | async-start | bytes 2621440 | tf_op jit(solution)/shard_map/all_gather | solution.py:323
  99.5 195.8 %all-reduce.31.cloned.1.call-start = ((), (), s32[]{:S(2)}) async-start(), calls=%async_computation.20 | async-start | bytes 4194304 | tf_op jit(solution)/shard_map/psum | solution.py:223
  99.6 71.3 %copy-start.166 = (f32[32]{0:T(128)}, f32[32]{0:T(128)S(1)}, u32[]{:S(2)}) copy-start(f32[32]{0:T(128)S(1)} %multiply_power_fusion) | copy-start | bytes 388
  99.6 45.8 %copy-start.85 = (pred[256,256]{1,0:T(8,128)(4,1)}, pred[256,256]{1,0:T(8,128)(4,1)S(1)}, u32[]{:S(2)}) copy-start(pred[256,256]{1,0:T(8,128)(4,1)S(1)} %iota_compare_fusion.1) | copy-start | bytes 196612
  114.0 56.3 %copy-start.58 = (bf16[1024,128]{1,0:T(8,128)(2,1)}, bf16[1024,128]{1,0:T(8,128)(2,1)S(1)}, u32[]{:S(2)}) copy-start(bf16[1024,128]{1,0:T(8,128)(2,1)S(1)} %all_gather.56) | copy-start | bytes 786436
  117.9 53.0 %copy-start.136 = (f32[512]{0:T(512)}, f32[512]{0:T(512)S(1)}, u32[]{:S(2)}) copy-start(f32[512]{0:T(512)S(1)} %broadcast_select_fusion.9) | copy-start | bytes 6148
  168.4 97.4 %copy-start.42 = (bf16[1024,256]{1,0:T(8,128)(2,1)}, bf16[1024,256]{1,0:T(8,128)(2,1)S(1)}, u32[]{:S(2)}) copy-start(bf16[1024,256]{1,0:T(8,128)(2,1)S(1)} %all_gather.59) | copy-start | bytes 1572868
  199.6 66.2 %copy-start.60 = (bf16[64,4,512]{2,0,1:T(8,128)(2,1)}, bf16[64,4,512]{2,0,1:T(8,128)(2,1)S(1)}, u32[]{:S(2)}) copy-start(bf16[64,4,512]{2,0,1:T(8,128)(2,1)S(1)} %fusion.94) | copy-start | bytes 786436
  267.8 70.7 %all-gather.20.cloned.1.call-start = ((), (), s32[]{:S(2)}) async-start(), calls=%async_computation.22 | async-start | bytes 2621440 | tf_op jit(solution)/shard_map/all_gather | solution.py:322
  268.5 116.3 %all-gather.18.cloned.1.call-start = ((), (), s32[]{:S(2)}) async-start(), calls=%async_computation.21 | async-start | bytes 2621440 | tf_op jit(solution)/shard_map/all_gather | solution.py:321
  269.3 147.3 %all-reduce.33.cloned.1.call-start = ((), (), s32[]{:S(2)}) async-start(), calls=%async_computation.24 | async-start | bytes 4194304 | tf_op jit(solution)/shard_map/psum | solution.py:223
  297.6 45.4 %copy-start.150 = (f32[512]{0:T(512)}, f32[512]{0:T(512)S(1)}, u32[]{:S(2)}) copy-start(f32[512]{0:T(512)S(1)} %get-tuple-element.451) | copy-start | bytes 6148
  297.6 121.9 %copy-start.3 = (f32[512,1024]{1,0:T(8,128)}, f32[512,1024]{1,0:T(8,128)S(1)}, u32[]{:S(2)}) copy-start(f32[512,1024]{1,0:T(8,128)S(1)} %get-tuple-element.452) | copy-start | bytes 6291460
  297.6 45.3 %copy-start.134 = (f32[512]{0:T(512)}, f32[512]{0:T(512)S(1)}, u32[]{:S(2)}) copy-start(f32[512]{0:T(512)S(1)} %fusion.158) | copy-start | bytes 6148
  396.5 85.8 %all-gather.24.cloned.1.call-start = ((), (), s32[]{:S(2)}) async-start(), calls=%async_computation.26 | async-start | bytes 3932160 | tf_op jit(solution)/shard_map/all_gather | solution.py:517
  434.2 157.7 %reduce-scatter.13.cloned.1.call-start = ((), (), s32[]{:S(2)}) async-start(), calls=%async_computation.25 | async-start | bytes 1310720 | tf_op jit(solution)/shard_map/reduce_scatter | solution.py:548
  482.3 158.8 %all-reduce.35.cloned.1.call-start = ((), (), s32[]{:S(2)}) async-start(), calls=%async_computation.27 | async-start | bytes 1048576 | tf_op jit(solution)/shard_map/psum | solution.py:223
  560.8 159.6 %reduce-scatter.19.cloned.1.call-start = ((), (), s32[]{:S(2)}) async-start(), calls=%async_computation.30 | async-start | bytes 1310720 | tf_op jit(solution)/shard_map/reduce_scatter | solution.py:597
  565.3 23.4 %copy-start.82 = (f32[512,32]{0,1:T(8,128)S(1)}, f32[512,32]{0,1:T(8,128)}, u32[]{:S(2)}) copy-start(f32[512,32]{0,1:T(8,128)} %copy-done.81) | copy-start | bytes 196612
  565.3 23.4 %copy-start.84 = (f32[512,32]{0,1:T(8,128)S(1)}, f32[512,32]{0,1:T(8,128)}, u32[]{:S(2)}) copy-start(f32[512,32]{0,1:T(8,128)} %copy-done.83) | copy-start | bytes 196612
  565.3 155.1 %reduce-scatter.15.cloned.1.call-start = ((), (), s32[]{:S(2)}) async-start(), calls=%async_computation.28 | async-start | bytes 1310720 | tf_op jit(solution)/shard_map/reduce_scatter | solution.py:595
  591.8 128.6 %reduce-scatter.17.cloned.1.call-start = ((), (), s32[]{:S(2)}) async-start(), calls=%async_computation.29 | async-start | bytes 655360 | tf_op jit(solution)/shard_map/reduce_scatter | solution.py:596
  596.1 143.2 %reduce-scatter.33.cloned.1.call-start = ((), (), s32[]{:S(2)}) async-start(), calls=%async_computation.37 | async-start | bytes 5242880 | tf_op jit(solution)/shard_map/reduce_scatter | solution.py:604
  601.8 217.0 %reduce-scatter.31.cloned.1.call-start = ((), (), s32[]{:S(2)}) async-start(), calls=%async_computation.36 | async-start | bytes 5242880 | tf_op jit(solution)/shard_map/reduce_scatter | solution.py:603
  606.7 275.0 %reduce-scatter.29.cloned.1.call-start = ((), (), s32[]{:S(2)}) async-start(), calls=%async_computation.35 | async-start | bytes 3932160 | tf_op jit(solution)/shard_map/reduce_scatter | solution.py:602
  613.5 330.8 %reduce-scatter.21.cloned.1.call-start = ((), (), s32[]{:S(2)}) async-start(), calls=%async_computation.31 | async-start | bytes 3932160 | tf_op jit(solution)/shard_map/reduce_scatter | solution.py:598
  619.4 403.9 %reduce-scatter.35.cloned.1.call-start = ((), (), s32[]{:S(2)}) async-start(), calls=%async_computation.38 | async-start | bytes 5242880 | tf_op jit(solution)/shard_map/reduce_scatter | solution.py:605
  624.4 429.6 %reduce-scatter.25.cloned.1.call-start = ((), (), s32[]{:S(2)}) async-start(), calls=%async_computation.33 | async-start | bytes 1310720 | tf_op jit(solution)/shard_map/reduce_scatter | solution.py:600
  651.4 5.6 collective-permute-start.2
  657.8 6.0 collective-permute-start.3
  667.7 447.5 %reduce-scatter.23.cloned.1.call-start = ((), (), s32[]{:S(2)}) async-start(), calls=%async_computation.32 | async-start | bytes 3932160 | tf_op jit(solution)/shard_map/reduce_scatter | solution.py:599
  674.0 472.3 %all-reduce.39.cloned.1.call-start = ((), (), s32[]{:S(2)}) async-start(), calls=%async_computation.40 | async-start | bytes 8388608 | tf_op jit(solution)/shard_map/psum | solution.py:223
  719.1 473.1 %reduce-scatter.27.cloned.1.call-start = ((), (), s32[]{:S(2)}) async-start(), calls=%async_computation.34 | async-start | bytes 81920 | tf_op jit(solution)/shard_map/reduce_scatter | solution.py:601
  720.3 624.6 %all-reduce.37.cloned.1.call-start = ((), (), s32[]{:S(2)}) async-start(), calls=%async_computation.39 | async-start | bytes 12845056 | tf_op jit(solution)/shard_map/psum | solution.py:607
  1115.2 31.2 %copy-start.8 = (bf16[2,256,1024]{2,1,0:T(8,128)(2,1)S(1)}, bf16[2,256,1024]{2,1,0:T(8,128)(2,1)}, u32[]{:S(2)}) copy-start(bf16[2,256,1024]{2,1,0:T(8,128)(2,1)} %copy-done.7) | copy-start | bytes 3145732
  1115.2 31.2 %copy-start.121 = (f32[1024]{0:T(1024)S(1)}, f32[1024]{0:T(1024)}, u32[]{:S(2)}) copy-start(f32[1024]{0:T(1024)} %param.36) | copy-start | bytes 12292
  1115.2 31.2 %copy-start.133 = (f32[512]{0:T(512)S(1)}, f32[512]{0:T(512)}, u32[]{:S(2)}) copy-start(f32[512]{0:T(512)} %copy-done.132) | copy-start | bytes 6148
  1115.2 31.2 %copy-start.157 = (pred[2]{0:T(512)(128)(4,1)S(1)}, pred[2]{0:T(512)(128)(4,1)}, u32[]{:S(2)}) copy-start(pred[2]{0:T(512)(128)(4,1)} %copy-done.155) | copy-start | bytes 10
  1188.0 61.4 %copy-start.158 = (f32[1024]{0:T(1024)S(1)}, f32[1024]{0:T(1024)}, u32[]{:S(2)}) copy-start(f32[1024]{0:T(1024)} %get-tuple-element.390) | copy-start | bytes 12292
  1188.0 140.4 %all-to-all-start.3 = ((bf16[4,256,1024]{2,1,0:T(8,128)(2,1)}), bf16[4,256,1024]{2,1,0:T(8,128)(2,1)S(1)}, u32[]{:S(2)}, u32[]{:S(2)}) async-start(bf16[4,256,1024]{2,1,0:T(8,128)(2,1)} %get-tuple-element.524), calls=%async_computation.4 | async-start | bytes 4194304 | tf_op jit(solution)/shard_map/all_to_all | solution.py:590
  (161 other events, 853.0 us)
Sparse Core Ops, SparseCore 0:
  20.0 44.7 all-gather.9
  97.7 43.9 all-gather.11
  143.3 41.3 all-gather.13
  186.1 35.1 all-gather.15
  222.7 44.7 all-gather.21
  269.7 19.9 all-reduce.30
  291.3 47.1 all-gather.19
  340.1 44.6 all-gather.17
  396.6 19.9 all-reduce.32
  434.3 45.1 all-gather.23
  482.4 28.8 reduce-scatter.12
  560.9 19.8 all-reduce.34
  583.1 28.3 reduce-scatter.18
  613.7 25.7 reduce-scatter.14
  641.7 20.2 reduce-scatter.16
  664.2 74.9 reduce-scatter.32
  741.5 77.2 reduce-scatter.30
  820.9 60.7 reduce-scatter.28
  884.0 60.2 reduce-scatter.20
  946.5 76.7 reduce-scatter.34
  1026.3 27.6 reduce-scatter.24
  1056.2 58.8 reduce-scatter.22
  1117.7 28.5 all-reduce.38
  1149.1 20.1 reduce-scatter.26
  1174.6 170.1 all-reduce.36
where the time goes:
time: 1380 us; the launch traced here: 1360 us
  waiting for transfers between devices  538 us (39%)
  blocking collectives  290 us (21%)
  matrix products  227 us (16%)
  local copies, waits for them, and re-layouts  142 us (10%)
  other arithmetic  127 us (9%)
  starting transfers between devices  22.7 us (2%)
  between operations  17.7 us (1%)
    reduce_scatter x1, waiting for transfers between devices, per_device(): lax.psum_scatter(grad_ffn_gate, 'fsdp', scatter_dimension=0, tiled=True)  79.6 us
    reduce_scatter x1, waiting for transfers between devices, per_device(): lax.psum_scatter(grad_ffn_down, 'fsdp', scatter_dimension=0, tiled=True)  79 us
    psum x1, blocking collectives, per_device(): lax.psum((grad_gain_mix, grad_conv_x, grad_conv_bc, grad_shift_finish + g...  76.9 us
    reduce_scatter x1, waiting for transfers between devices, per_device(): lax.psum_scatter(grad_ssm_out, 'fsdp', scatter_dimension=0, tiled=True)  62.9 us
    reduce_scatter x1, waiting for transfers between devices, per_device(): lax.psum_scatter(grad_w_gate_z, 'fsdp', scatter_dimension=0, tiled=True)  62.6 us
    reduce_scatter x1, waiting for transfers between devices, per_device(): lax.psum_scatter(grad_w_in_x, 'fsdp', scatter_dimension=0, tiled=True)  61.2 us
    psum x1, blocking collectives, per_device(): lax.psum((reduced[0], reduced[1], reduced[2], reduced[3], reduced[4], red...  57.2 us
    dot_general x16, matrix products, highdot(): return jnp.dot(left, right.astype(jnp.float32), precision=exact)  56.1 us
  transfers between devices with their start and end apart: 31, of which 16 were waited for; matrix products, arithmetic and copies ran while one was open for 31% of the time, Pallas kernels for 0%

commit v1 on v0

v1 whole, which is shorter than its diff:
```python
import functools

import jax
import jax.numpy as jnp
from jax import lax
from jax.experimental import pallas as pl
from jax.experimental.pallas import tpu as pltpu
from jax.sharding import PartitionSpec as P

HEAD_DIM = 64
SSM_DIM = 64
STATE = 128
CONV = 4
HALF = 256
WINDOW = 4

epsilon = 1e-05
masked = -1e30
F32 = jnp.float32
BF16 = jnp.bfloat16
exact = lax.Precision.HIGHEST


def dot(left, right, left_dim=1, right_dim=0, precision=None):
    return lax.dot_general(
        left,
        right,
        (((left_dim,), (right_dim,)), ((), ())),
        precision=precision,
        preferred_element_type=F32,
    )


def sigmoid(v):
    return 1.0 / (1.0 + jnp.exp(-v))


def softplus(v):
    return jnp.maximum(v, 0.0) + jnp.log1p(jnp.exp(-jnp.abs(v)))


def swap_halves(v):
    half = v.shape[1] // 2
    return jnp.concatenate([v[:, half:], v[:, :half]], axis=1)


def iotas(rows, columns):
    return (
        lax.broadcasted_iota(jnp.int32, (rows, columns), 0),
        lax.broadcasted_iota(jnp.int32, (rows, columns), 1),
    )


def state_scale(last_row, carry_last, heads):
    pieces = [
        jnp.broadcast_to(last_row[:, h * SSM_DIM : h * SSM_DIM + 1], (SSM_DIM, STATE))
        for h in range(heads)
    ]
    return jnp.exp(jnp.concatenate(pieces, axis=0)) * carry_last


def block_decays(step_raw, heads_ref, lane_pos, heads):
    rows = step_raw.shape[0]
    inner = heads * SSM_DIM
    raw = step_raw + heads_ref[0:1, :inner]
    step = softplus(raw)
    rate = step * jnp.exp(heads_ref[1:2, :inner])
    row, col = iotas(rows, rows)
    lower = jnp.where(col <= row, 1.0, 0.0).astype(F32)
    totals = dot(lower, -rate, precision=exact)
    last_row = totals[rows - 1 : rows]
    pos_last = lane_pos[rows - 1 : rows, 0:1]
    local = lax.broadcasted_iota(jnp.int32, (rows, 1), 0).astype(F32)
    carry_on = (lane_pos[:, 0:1] > local).astype(F32)
    keep_last = (local >= (rows - 1) - pos_last).astype(F32)
    carry_last = (pos_last > rows - 1).astype(F32)
    factor = jnp.exp(totals) * carry_on
    tails = jnp.exp(last_row - totals) * keep_last
    return raw, step, rate, totals, last_row, carry_last, factor, tails


def local_mask(lane_pos, rows):
    row, col = iotas(rows, rows)
    gap = (row - col).astype(F32)
    return (gap >= 0) & (gap <= lane_pos[:, 0:1])


def key_window(block):
    start = jnp.maximum(block - WINDOW, 0)
    return start, (block - start) * HALF


def window_mask(lane_pos, offset, rows, keys):
    row, col = iotas(rows, keys)
    gap = (row - col + offset).astype(F32)
    return (gap >= 0) & (gap <= lane_pos[:, 0:1])


def head_decay(totals, totals_t, h, allowed):
    gap = totals[:, h * SSM_DIM : h * SSM_DIM + 1] - totals_t[h * SSM_DIM : h * SSM_DIM + 1, :]
    return jnp.exp(jnp.where(allowed, gap, masked))


def mixer_forward_kernel(
    slots_ref, u_ref, table_ref, heads_ref, taps_ref, ag_ref, y_ref, conv_ref, state_in_ref, kv_ref,
    ext, state, keyval,
):
    block = pl.program_id(0)
    heads = state.shape[0] // SSM_DIM
    inner = heads * SSM_DIM
    width = ext.shape[1]
    rows = u_ref.shape[0]

    @pl.when(block == 0)
    def _():
        ext[0:8, :] = jnp.zeros((8, width), F32)
        state[...] = jnp.zeros(state.shape, F32)
        keyval[...] = jnp.zeros(keyval.shape, BF16)

    lane_pos = table_ref[:, 128:256]
    cosine = table_ref[:, 0:64]
    sine = table_ref[:, 64:128]
    q_at = inner
    u = u_ref[:, :width].astype(F32)
    ext[8 : 8 + rows, :] = u
    conv = u * taps_ref[CONV - 1 : CONV, :]
    for back in range(1, CONV):
        reach = lane_pos[:, 0:1] >= back
        shifted = ext[8 - back : 8 - back + rows, :]
        conv = conv + jnp.where(reach, shifted, 0.0) * taps_ref[CONV - 1 - back : CONV - back, :]
    ext[0:8, :] = u[rows - 8 : rows]
    act = conv * sigmoid(conv)
    ssm_x = act[:, :inner].astype(BF16)
    ssm_b = act[:, 256:384].astype(BF16)
    ssm_c = act[:, 384:512].astype(BF16)
    conv_ref[:, 0:256] = conv[:, 0:256]
    conv_ref[:, 256:512] = conv[:, 256:512]
    query = u[:, q_at : q_at + HEAD_DIM]
    query = (query * cosine + swap_halves(query) * sine).astype(BF16)
    conv_ref[:, q_at : q_at + HEAD_DIM] = query.astype(F32)
    key = u_ref[:, 512 + inner : 512 + inner + HEAD_DIM].astype(F32)
    key = key * cosine + swap_halves(key) * sine
    value = u_ref[:, 768 + inner : 768 + inner + HEAD_DIM].astype(F32)
    pair = jnp.concatenate([key, value], axis=1).astype(BF16)
    kv_ref[...] = pair
    keyval[pl.ds(pl.multiple_of(block * rows, rows), rows), :] = pair
    first, offset = key_window(block)
    span = (WINDOW + 1) * HALF
    window = keyval[pl.ds(pl.multiple_of(first * rows, rows), span), :]
    scores = dot(query * 0.125, window[:, :HEAD_DIM], 1, 1)
    scores = jnp.where(window_mask(lane_pos, offset, rows, span), scores, masked)
    highest = jnp.max(scores, axis=1, keepdims=True)
    weights = jnp.exp(scores - highest)
    total = jnp.sum(weights, axis=1, keepdims=True)
    probs = (weights * (1.0 / total)).astype(BF16)
    attended = dot(probs, window[:, HEAD_DIM:])
    _, step, _, totals, last_row, carry_last, factor, tails = block_decays(
        u_ref[:, 768 : 768 + inner].astype(F32), heads_ref, lane_pos, heads
    )
    totals_t = totals.T
    allowed = local_mask(lane_pos, rows)
    cross = dot(ssm_c, ssm_b, 1, 1)
    x_f = ssm_x.astype(F32)
    stepped = step * x_f
    stepped_low = stepped.astype(BF16)
    parts = []
    for h in range(heads):
        lanes = slice(h * SSM_DIM, (h + 1) * SSM_DIM)
        mix = (head_decay(totals, totals_t, h, allowed) * cross).astype(BF16)
        parts.append(dot(mix, stepped_low[:, lanes]))
    held = state[...]
    state_in_ref[...] = held
    y_pure = jnp.concatenate(parts, axis=1) + factor * dot(ssm_c, held.astype(BF16), 1, 1)
    tailed = (tails * stepped_low.astype(F32)).astype(BF16)
    state[...] = state_scale(last_row, carry_last, heads) * held + dot(tailed, ssm_b, 0, 0)
    y_ref[:, :inner] = y_pure
    y_ref[:, inner : inner + HEAD_DIM] = jnp.broadcast_to(
        highest + jnp.log(total), (rows, HEAD_DIM)
    )
    y_full = y_pure + heads_ref[2:3, :inner] * x_f
    gate = u_ref[:, 512 : 512 + inner].astype(F32)
    gated = y_full * (gate * sigmoid(gate))
    ag_ref[...] = jnp.concatenate([gated, attended], axis=1).astype(BF16)


def mixer_backward_kernel(
    slots_ref, dag_ref, ag_ref, u_ref, table_ref, heads_ref, taps_ref, y_ref, conv_ref, state_in_ref,
    state_out_ref, kv_ref, du_ref, stats_ref, dext, dpos, dstate, dkey_t, dvalue_t,
):
    turn = pl.program_id(0)
    blocks = pl.num_programs(0)
    block = blocks - 1 - turn
    heads = dstate.shape[0] // SSM_DIM
    inner = heads * SSM_DIM
    rows = u_ref.shape[0]
    width = dext.shape[1]

    @pl.when(turn == 0)
    def _():
        dext[rows : rows + 8, :] = jnp.zeros((8, width), F32)
        dpos[rows : rows + 8, :] = jnp.full((8, dpos.shape[1]), -1.0, F32)
        dstate[...] = jnp.zeros(dstate.shape, F32)
        dkey_t[...] = jnp.zeros(dkey_t.shape, F32)
        dvalue_t[...] = jnp.zeros(dvalue_t.shape, F32)
        stats_ref[...] = jnp.zeros(stats_ref.shape, F32)

    lane_pos = table_ref[:, 128:256]
    cosine = table_ref[:, 0:64]
    sine = table_ref[:, 64:128]
    first, offset = key_window(block)
    span = (WINDOW + 1) * HALF
    begin = pl.multiple_of(first * rows, rows)
    window = kv_ref[pl.ds(begin, span), :]
    keys = window[:, :HEAD_DIM]
    values = window[:, HEAD_DIM:]
    query = conv_ref[:, inner : inner + HEAD_DIM] * 0.125
    query_low = query.astype(BF16)
    datt = dag_ref[:, inner : inner + HEAD_DIM]
    datt_f = datt.astype(F32)
    lse = y_ref[:, inner : inner + 1]
    scores = dot(query_low, keys, 1, 1)
    allowed_all = window_mask(lane_pos, offset, rows, span)
    probs = jnp.exp(jnp.where(allowed_all, scores, masked) - lse)
    inward = jnp.sum(datt_f * ag_ref[:, inner : inner + HEAD_DIM].astype(F32), axis=1, keepdims=True)
    dscores = (probs * (dot(datt, values, 1, 1) - inward)).astype(BF16)
    dquery = dot(dscores, keys) * 0.125
    dkey_t[:, pl.ds(begin, span)] += dot(query.T.astype(BF16), dscores)
    dvalue_t[:, pl.ds(begin, span)] += dot(datt_f.T.astype(BF16), probs.astype(BF16))
    here = pl.ds(pl.multiple_of(block * rows, rows), rows)
    dkey = dkey_t[:, here].T
    dvalue = dvalue_t[:, here].T
    dquery = dquery * cosine - swap_halves(dquery) * sine
    dkey = dkey * cosine - swap_halves(dkey) * sine
    conv = conv_ref[...]
    gate_conv = sigmoid(conv)
    act = conv * gate_conv
    dact = gate_conv * (1.0 + conv * (1.0 - gate_conv))
    ssm_x = act[:, :inner].astype(BF16)
    ssm_b = act[:, 256:384].astype(BF16)
    ssm_c = act[:, 384:512].astype(BF16)
    x_f = ssm_x.astype(F32)
    raw, step, rate, totals, last_row, carry_last, factor, tails = block_decays(
        u_ref[:, 768 : 768 + inner].astype(F32), heads_ref, lane_pos, heads
    )
    totals_t = totals.T
    allowed = local_mask(lane_pos, rows)
    cross = dot(ssm_c, ssm_b, 1, 1)
    gate = u_ref[:, 512 : 512 + inner].astype(F32)
    sig = sigmoid(gate)
    y_pure = y_ref[:, :inner]
    dgated = dag_ref[:, :inner].astype(F32)
    skip = heads_ref[2:3, :inner]
    dy = dgated * (gate * sig)
    dgate = dgated * (y_pure + skip * x_f) * (sig * (1.0 + gate * (1.0 - sig)))
    dy_low = dy.astype(BF16)
    dy_r = dy_low.astype(F32)
    dy_t = dy.T.astype(BF16)
    stepped_low = (step * x_f).astype(BF16)
    stepped_r = stepped_low.astype(F32)
    tailed = (tails * stepped_r).astype(BF16)
    dcross = jnp.zeros((rows, rows), F32)
    parts = []
    for h in range(heads):
        lanes = slice(h * SSM_DIM, (h + 1) * SSM_DIM)
        decay = head_decay(totals, totals_t, h, allowed)
        mix = (decay * cross).astype(BF16)
        parts.append(dot(dy_t[lanes, :], mix))
        dcross = dcross + dot(dy_low[:, lanes], stepped_low[:, lanes], 1, 1) * decay
    dstep_x = jnp.concatenate(parts, axis=0).T
    dcross_low = dcross.astype(BF16)
    held = state_in_ref[...].astype(BF16)
    dheld = dstate[...]
    dheld_low = dheld.astype(BF16)
    dfactored = (factor * dy).astype(BF16)
    from_state = dot(ssm_b, dheld_low, 1, 1)
    dssm_c = dot(dcross_low, ssm_b) + dot(dfactored, held)
    dssm_b = dot(dcross_low, ssm_c, 0, 0) + dot(tailed, dheld_low)
    dtotals = dy_r * y_pure - stepped_r * dstep_x - tailed.astype(F32) * from_state
    dstep_x = dstep_x + tails * from_state
    end_term = dot(
        jnp.ones((8, STATE), F32), dheld_low.astype(F32) * state_out_ref[...], 1, 1, exact
    )[0:1]
    end_term = jnp.where(turn == 0, jnp.zeros_like(end_term), end_term)
    row, col = iotas(rows, rows)
    upper = jnp.where(col >= row, 1.0, 0.0).astype(F32)
    drate = -(dot(upper, dtotals, precision=exact) + end_term)
    dstate[...] = state_scale(last_row, carry_last, heads) * dheld + dot(dfactored, ssm_c, 0, 0)
    dssm_x = step * dstep_x + skip * dy
    dstep = x_f * dstep_x + jnp.exp(heads_ref[1:2, :inner]) * drate
    draw = dstep * sigmoid(raw)
    none = jnp.zeros((rows, HEAD_DIM), F32)
    dconv = jnp.concatenate([dssm_x, none, dssm_b, dssm_c], axis=1) * dact
    dext[0:rows, :] = dconv
    dpos[0:rows, :] = lane_pos
    u = u_ref[:, :width].astype(F32)
    du = dconv * taps_ref[CONV - 1 : CONV, :]
    stats_ref[CONV - 1 : CONV, :] += jnp.sum(dconv * u, axis=0, keepdims=True)
    for ahead in range(1, CONV):
        reach = dpos[ahead : ahead + rows, 0:1] >= ahead
        shifted = jnp.where(reach, dext[ahead : ahead + rows, :], 0.0)
        tap = CONV - 1 - ahead
        du = du + shifted * taps_ref[tap : tap + 1, :]
        stats_ref[tap : tap + 1, :] += jnp.sum(shifted * u, axis=0, keepdims=True)
    dext[rows : rows + 8, :] = dconv[0:8]
    dpos[rows : rows + 8, :] = lane_pos[0:8]
    stats_ref[4:5, :inner] += jnp.sum(dy * x_f, axis=0, keepdims=True)
    stats_ref[5:6, :inner] += jnp.sum(draw, axis=0, keepdims=True)
    stats_ref[6:7, :inner] += jnp.sum(drate * rate, axis=0, keepdims=True)
    summed = [
        jnp.sum(draw[:, h * SSM_DIM : (h + 1) * SSM_DIM], axis=1, keepdims=True)
        for h in range(heads)
    ]
    lane = lax.broadcasted_iota(jnp.int32, (rows, HEAD_DIM), 1)
    dstep_all = jnp.zeros((rows, HEAD_DIM), F32)
    for h in range(heads):
        dstep_all = jnp.where(lane == h, summed[h], dstep_all)
    du_ref[:, 0:256] = jnp.concatenate([du[:, :inner], dquery], axis=1).astype(BF16)
    du_ref[:, 256:512] = du[:, 256:512].astype(BF16)
    du_ref[:, 512:768] = jnp.concatenate([dgate, dkey], axis=1).astype(BF16)
    du_ref[:, 768:896] = jnp.concatenate([dvalue, dstep_all], axis=1).astype(BF16)


def mixer_forward(u, table, head_rows, taps, slot_of):
    count = u.shape[0]
    blocks = count // HALF
    heads = 3
    inner = heads * SSM_DIM
    width = taps.shape[1]
    at_slot = lambda i, slots: (slots[i], 0)
    in_order = lambda i, slots: (i, 0)
    whole = lambda i, slots: (0, 0)
    return pl.pallas_call(
        mixer_forward_kernel,
        out_shape=(
            jax.ShapeDtypeStruct((count, inner + HEAD_DIM), BF16),
            jax.ShapeDtypeStruct((count, inner + HEAD_DIM), F32),
            jax.ShapeDtypeStruct((count, width), F32),
            jax.ShapeDtypeStruct((blocks * inner, STATE), F32),
            jax.ShapeDtypeStruct((count, 2 * HEAD_DIM), BF16),
        ),
        grid_spec=pltpu.PrefetchScalarGridSpec(
            num_scalar_prefetch=1,
            grid=(blocks,),
            in_specs=[
                pl.BlockSpec((HALF, u.shape[1]), at_slot),
                pl.BlockSpec((HALF, table.shape[1]), in_order),
                pl.BlockSpec(head_rows.shape, whole),
                pl.BlockSpec(taps.shape, whole),
            ],
            out_specs=(
                pl.BlockSpec((HALF, inner + HEAD_DIM), at_slot),
                pl.BlockSpec((HALF, inner + HEAD_DIM), in_order),
                pl.BlockSpec((HALF, width), in_order),
                pl.BlockSpec((inner, STATE), in_order),
                pl.BlockSpec((HALF, 2 * HEAD_DIM), in_order),
            ),
            scratch_shapes=[
                pltpu.VMEM((8 + HALF, width), F32),
                pltpu.VMEM((inner, STATE), F32),
                pltpu.VMEM((count, 2 * HEAD_DIM), BF16),
            ],
        ),
        compiler_params=pltpu.CompilerParams(vmem_limit_bytes=48 << 20),
    )(slot_of, u, table, head_rows, taps)


def mixer_backward(dag, ag, u, table, head_rows, taps, y, conv, states, keyval, slot_of):
    count = u.shape[0]
    blocks = count // HALF
    heads = 3
    inner = heads * SSM_DIM
    width = taps.shape[1]
    last = blocks - 1
    at_slot = lambda i, slots: (slots[last - i], 0)
    in_order = lambda i, slots: (last - i, 0)
    after = lambda i, slots: (jnp.minimum(last - i + 1, last), 0)
    whole = lambda i, slots: (0, 0)
    columns = inner + HEAD_DIM
    return pl.pallas_call(
        mixer_backward_kernel,
        out_shape=(
            jax.ShapeDtypeStruct((count, 896), BF16),
            jax.ShapeDtypeStruct((8, width), F32),
        ),
        grid_spec=pltpu.PrefetchScalarGridSpec(
            num_scalar_prefetch=1,
            grid=(blocks,),
            in_specs=[
                pl.BlockSpec((HALF, columns), at_slot),
                pl.BlockSpec((HALF, columns), at_slot),
                pl.BlockSpec((HALF, u.shape[1]), at_slot),
                pl.BlockSpec((HALF, table.shape[1]), in_order),
                pl.BlockSpec(head_rows.shape, whole),
                pl.BlockSpec(taps.shape, whole),
                pl.BlockSpec((HALF, columns), in_order),
                pl.BlockSpec((HALF, width), in_order),
                pl.BlockSpec((inner, STATE), in_order),
                pl.BlockSpec((inner, STATE), after),
                pl.BlockSpec((count, 2 * HEAD_DIM), whole),
            ],
            out_specs=(
                pl.BlockSpec((HALF, 896), at_slot),
                pl.BlockSpec((8, width), whole),
            ),
            scratch_shapes=[
                pltpu.VMEM((HALF + 8, width), F32),
                pltpu.VMEM((HALF + 8, 128), F32),
                pltpu.VMEM((inner, STATE), F32),
                pltpu.VMEM((HEAD_DIM, count), F32),
                pltpu.VMEM((HEAD_DIM, count), F32),
            ],
        ),
        compiler_params=pltpu.CompilerParams(vmem_limit_bytes=56 << 20),
    )(slot_of, dag, ag, u, table, head_rows, taps, y, conv, states, states, keyval)


GROUP = ("context", "tensor")


def low_dot(left, right, left_dim=1, right_dim=0):
    return dot(left.astype(BF16), right.astype(BF16), left_dim, right_dim)


def inverse_rms(values):
    return lax.rsqrt(jnp.mean(values * values, axis=-1, keepdims=True) + epsilon)


def norm_back(values, gain, grad):
    scale = inverse_rms(values)
    pull = jnp.mean(grad * gain * values, axis=-1, keepdims=True)
    gain_grad = jnp.sum(grad * values * scale, axis=0)
    return scale * (grad * gain - values * scale * scale * pull), gain_grad


def stream_table(segment_ids):
    count = segment_ids.shape[0]
    order = jnp.arange(count, dtype=jnp.int32)
    starts = jnp.sum((segment_ids[None, :] < segment_ids[:, None]).astype(jnp.int32), axis=1)
    pos = (order - starts).astype(F32)
    half = HEAD_DIM // 2
    freqs = 10000.0 ** (-jnp.arange(half, dtype=F32) / half)
    angles = pos[:, None] * freqs[None, :]
    cosine, sine = jnp.cos(angles), jnp.sin(angles)
    return jnp.concatenate(
        [cosine, cosine, -sine, sine, jnp.broadcast_to(pos[:, None], (count, 128))], axis=1
    )


def per_device(
    tokens, segments, deal, gain_mix, w_query, w_keyval, w_attn_out, w_gate_z, w_in_x, w_bc, w_step,
    conv_x, conv_bc, step_bias, decay_log, skip, w_ssm_out, gain_ffn, w_ffn_gate, w_ffn_up,
    w_ffn_down, cotangent,
):
    ctx = lax.axis_size("context")
    c = lax.axis_index("context")
    t = lax.axis_index("tensor")
    heads = skip.shape[0] // ctx
    inner = heads * SSM_DIM
    qd = w_query.shape[1] // ctx
    hid = w_ffn_gate.shape[1] // ctx
    ddt = cotangent.dtype

    def part(array, width):
        return lax.dynamic_slice_in_dim(array, c * width, width, axis=1)

    keys_w, values_w = w_keyval[:, :HEAD_DIM], w_keyval[:, HEAD_DIM:]
    pad = HEAD_DIM - heads
    mine = jnp.concatenate(
        [
            part(w_in_x, inner), part(w_query, qd), w_bc, part(w_gate_z, inner), keys_w, values_w,
            jnp.pad(part(w_step, heads), ((0, 0), (0, pad))),
        ],
        axis=1,
    )
    mine_out = jnp.concatenate([part(w_ssm_out, inner), part(w_attn_out, qd)], axis=1)
    mine_ffn = jnp.concatenate(
        [part(w_ffn_gate, hid), part(w_ffn_up, hid), part(w_ffn_down, hid)], axis=1
    )
    w_all = lax.all_gather(mine, "fsdp", axis=0, tiled=True)
    wout_all = lax.all_gather(mine_out, "fsdp", axis=0, tiled=True)
    wffn_all = lax.all_gather(mine_ffn, "fsdp", axis=0, tiled=True)
    at_step = 896 - HEAD_DIM
    w_wide = jnp.concatenate(
        [
            w_all[:, :768],
            jnp.repeat(w_all[:, at_step : at_step + heads], SSM_DIM, axis=1),
            w_all[:, 768 : 768 + HEAD_DIM],
        ],
        axis=1,
    )
    w_gate, w_up, w_down = wffn_all[:, :hid], wffn_all[:, hid : 2 * hid], wffn_all[:, 2 * hid :]

    order = deal[0]
    ids = jnp.arange(order.shape[0], dtype=jnp.int32)
    slot_of = jnp.sum(jnp.where(order[None, :] == ids[:, None], ids[None, :], 0), axis=1)
    table = stream_table(segments[0])

    def lanes(values):
        return jnp.repeat(lax.dynamic_slice_in_dim(values, c * heads, heads), SSM_DIM)

    head_rows = jnp.zeros((8, 256), F32)
    head_rows = head_rows.at[0, :inner].set(lanes(step_bias))
    head_rows = head_rows.at[1, :inner].set(lanes(decay_log))
    head_rows = head_rows.at[2, :inner].set(lanes(skip))
    taps = jnp.concatenate(
        [part(conv_x, inner), jnp.zeros((CONV, qd), F32), conv_bc], axis=1
    )

    x_all = lax.all_gather(tokens, "context", axis=0, tiled=True)
    cot_all = lax.all_gather(cotangent, "context", axis=0, tiled=True)
    row_count = tokens.shape[0]
    half = row_count // 2
    x_own = lax.dynamic_slice_in_dim(tokens, t * half, half, axis=0).astype(F32)
    cot_own = lax.dynamic_slice_in_dim(cotangent, t * half, half, axis=0).astype(F32)

    xf = x_all.astype(F32)
    normed = (xf * inverse_rms(xf) * gain_mix).astype(BF16)
    u = low_dot(normed, w_wide)
    ag, y, conv, states, keyval = mixer_forward(u, table, head_rows, taps, slot_of)

    def scatter(values):
        return lax.psum_scatter(
            values.astype(BF16), GROUP, scatter_dimension=0, tiled=True
        ).astype(F32)

    mixed = x_own + scatter(low_dot(ag, wout_all, 1, 1))
    nffn_own = (mixed * inverse_rms(mixed) * gain_ffn).astype(BF16)
    nffn = lax.all_gather(nffn_own, GROUP, axis=0, tiled=True)
    gate = low_dot(nffn, w_gate)
    up = low_dot(nffn, w_up)
    sig = sigmoid(gate)
    hidden = (gate * sig * up).astype(BF16)
    out_own = mixed + scatter(low_dot(hidden, w_down, 1, 1))
    dhidden = low_dot(cot_all, w_down).astype(BF16).astype(F32)
    dgate = (dhidden * up * (sig * (1.0 + gate * (1.0 - sig)))).astype(BF16)
    dup = (dhidden * gate * sig).astype(BF16)
    dnffn = scatter(low_dot(dgate, w_gate, 1, 1) + low_dot(dup, w_up, 1, 1))
    dm_norm, dgain_ffn = norm_back(mixed, gain_ffn, dnffn)
    dmixed = cot_own + dm_norm
    dm_all = lax.all_gather(dmixed.astype(BF16), GROUP, axis=0, tiled=True)
    dag = low_dot(dm_all, wout_all).astype(BF16)
    du, stats = mixer_backward(dag, ag, u, table, head_rows, taps, y, conv, states, keyval, slot_of)
    dnormed = scatter(low_dot(du, w_all, 1, 1))
    dx_norm, dgain_mix = norm_back(x_own, gain_mix, dnormed)
    dx_own = dmixed + dx_norm

    mixed_out = lax.all_gather(out_own.astype(BF16), "tensor", axis=0, tiled=True)
    tokens_grad = lax.all_gather(dx_own.astype(BF16), "tensor", axis=0, tiled=True)

    dw = jnp.concatenate(
        [
            low_dot(normed, du, 0, 0),
            low_dot(dm_all, ag, 0, 0),
            low_dot(nffn, dgate, 0, 0),
            low_dot(nffn, dup, 0, 0),
            low_dot(cot_all, hidden, 0, 0),
        ],
        axis=1,
    ).astype(BF16)
    dw = lax.psum_scatter(dw, "fsdp", scatter_dimension=0, tiled=True)
    dw_all = lax.all_gather(dw, "context", axis=0, tiled=False).astype(F32)

    def spread(begin, width):
        piece = dw_all[:, :, begin : begin + width]
        return piece.transpose(1, 0, 2).reshape(piece.shape[1], -1)

    summed = jnp.sum(dw_all, axis=0)
    dbc = lax.psum(summed[:, 256:512], "tensor")
    dkv = summed[:, 768 - HEAD_DIM : 768 + HEAD_DIM]

    def place(values, full, axis_start):
        zero = jnp.zeros(full, F32)
        return lax.dynamic_update_slice(zero, values, axis_start).reshape(-1)

    total_heads = skip.shape[0] * lax.axis_size("tensor")
    at_head = t * skip.shape[0] + c * heads

    def head_sum(row):
        return jnp.sum(row[:inner].reshape(heads, SSM_DIM), axis=1)

    x_width = conv_x.shape[1] * lax.axis_size("tensor")
    small = [
        dgain_mix,
        dgain_ffn,
        place(stats[0:CONV, :inner], (CONV, x_width), (0, t * conv_x.shape[1] + c * inner)),
        stats[0:CONV, 256:512].reshape(-1),
        place(stats[5, :inner].reshape(heads, SSM_DIM)[:, 0], (total_heads,), (at_head,)),
        place(head_sum(stats[6]), (total_heads,), (at_head,)),
        place(head_sum(stats[4]), (total_heads,), (at_head,)),
    ]
    small[4] = place(head_sum(stats[5]), (total_heads,), (at_head,))
    sizes = [s.shape[0] for s in small]
    joined = lax.psum(jnp.concatenate(small), ("fsdp", "context", "tensor"))
    pieces = []
    at = 0
    for size in sizes:
        pieces.append(joined[at : at + size])
        at += size

    def own(values, width, axis):
        return lax.dynamic_slice_in_dim(values, t * width, width, axis=axis)

    return (
        mixed_out,
        tokens_grad,
        pieces[0],
        spread(inner, qd),
        dkv,
        spread(896 + inner, qd),
        spread(512, inner),
        spread(0, inner),
        dbc,
        spread(at_step, heads),
        own(pieces[2].reshape(CONV, x_width), conv_x.shape[1], 1),
        pieces[3].reshape(CONV, -1),
        own(pieces[4], skip.shape[0], 0),
        own(pieces[5], skip.shape[0], 0),
        own(pieces[6], skip.shape[0], 0),
        spread(896, inner),
        pieces[1],
        spread(1152, hid),
        spread(1152 + hid, hid),
        spread(1152 + 2 * hid, hid),
    )


def solution(mesh):
    in_specs = (
        P(("fsdp", "context"), None),
        P("fsdp", None),
        P("fsdp", None),
        P(),
        P("fsdp", "tensor"),
        P("fsdp", "tensor"),
        P("fsdp", "tensor"),
        P("fsdp", "tensor"),
        P("fsdp", "tensor"),
        P("fsdp", None),
        P("fsdp", "tensor"),
        P(None, "tensor"),
        P(),
        P("tensor"),
        P("tensor"),
        P("tensor"),
        P("fsdp", "tensor"),
        P(),
        P("fsdp", "tensor"),
        P("fsdp", "tensor"),
        P("fsdp", "tensor"),
        P(("fsdp", "context"), None),
    )
    out_specs = (
        P(("fsdp", "context"), None),
        P(("fsdp", "context"), None),
        P(),
        P("fsdp", "tensor"),
        P("fsdp", "tensor"),
        P("fsdp", "tensor"),
        P("fsdp", "tensor"),
        P("fsdp", "tensor"),
        P("fsdp", None),
        P("fsdp", "tensor"),
        P(None, "tensor"),
        P(),
        P("tensor"),
        P("tensor"),
        P("tensor"),
        P("fsdp", "tensor"),
        P(),
        P("fsdp", "tensor"),
        P("fsdp", "tensor"),
        P("fsdp", "tensor"),
    )
    return jax.shard_map(
        per_device, mesh=mesh, in_specs=in_specs, out_specs=out_specs, check_vma=False
    )
```

time: 1380 us -> 827 us (0.60)
  blocking collectives: 290 us -> 65.9 us
  matrix products: 227 us -> 65.6 us
  other arithmetic: 127 us -> 37.4 us
  local copies, waits for them, and re-layouts: 142 us -> 67.6 us
  Pallas kernels: 0 us -> 71.2 us
  waiting for transfers between devices: 538 us -> 498 us
  starting transfers between devices: 22.7 us -> 1.52 us
    all_gather x8 -> x9, waiting for transfers between devices: 81.3 us -> 245 us  [the longest x1 51.2 us: per_device(): x_all = lax.all_gather(tokens, 'context', axis=0, tiled=True)]
    dot_general x55 -> x15, matrix products: 227 us -> 65.6 us  [dot(): lax.dot_general(left, right, (((left_dim,), (right_dim,)), ((), ())), pre...]
    reduce_scatter x12 -> x5, waiting for transfers between devices: 395 us -> 251 us  [the longest x4 180 us: scatter(): lax.psum_scatter(values.astype(BF16), GROUP, scatter_dimension=0, tiled=T...]
    psum x2 -> x1, blocking collectives: 134 us -> 41.4 us  [per_device(): joined = lax.psum(jnp.concatenate(small), ('fsdp', 'context', 'tensor'))]
    all_gather x7 -> x1, blocking collectives: 104 us -> 24.6 us  [per_device(): wout_all = lax.all_gather(mine_out, 'fsdp', axis=0, tiled=True)]
    pallas_call x0 -> x2, Pallas kernels: none -> 71.2 us  [the longest x1 43.3 us: mixer_backward(): pl.pallas_call(mixer_backward_kernel, out_shape=(jax.ShapeDtypeStruct((co...]
    all_to_all x2 -> x0, blocking collectives: 52.5 us -> none  [the longest x1 33.3 us: per_device(): lax.all_to_all(leaving[0], 'context', split_axis=0, concat_axis=0, tiled=...]
    psum x5 -> x1, waiting for transfers between devices: 47.9 us -> 0.01 us  [per_device(): dbc = lax.psum(summed[:, 256:512], 'tensor')]
  transfers between devices with their start and end apart: 31 -> 15, of which waited for: 16 -> 12; matrix products, arithmetic and copies ran while one was open for 31% -> 11% of each run, Pallas kernels for 0% -> 0%
where the time goes in v1:
time: 827 us; the launch traced here: 822 us
  waiting for transfers between devices  498 us (60%)
  Pallas kernels  71.2 us (9%)
  local copies, waits for them, and re-layouts  67.6 us (8%)
  blocking collectives  65.9 us (8%)
  matrix products  65.6 us (8%)
  other arithmetic  37.4 us (5%)
  between operations  14.8 us (2%)
    reduce_scatter x4, waiting for transfers between devices, scatter(): lax.psum_scatter(values.astype(BF16), GROUP, scatter_dimension=0, tiled=T...  180 us
    reduce_scatter x1, waiting for transfers between devices, per_device(): dw = lax.psum_scatter(dw, 'fsdp', scatter_dimension=0, tiled=True)  71 us
    dot_general x15, matrix products, dot(): lax.dot_general(left, right, (((left_dim,), (right_dim,)), ((), ())), pre...  65.6 us
    all_gather x1, waiting for transfers between devices, per_device(): x_all = lax.all_gather(tokens, 'context', axis=0, tiled=True)  51.2 us
    all_gather x1, waiting for transfers between devices, per_device(): cot_all = lax.all_gather(cotangent, 'context', axis=0, tiled=True)  45.8 us
    pallas_call x1, Pallas kernels, mixer_backward(): pl.pallas_call(mixer_backward_kernel, out_shape=(jax.ShapeDtypeStruct((co...  43.3 us
    psum x1, blocking collectives, per_device(): joined = lax.psum(jnp.concatenate(small), ('fsdp', 'context', 'tensor'))  41.4 us
    all_gather x1, waiting for transfers between devices, per_device(): nffn = lax.all_gather(nffn_own, GROUP, axis=0, tiled=True)  38.1 us
  transfers between devices with their start and end apart: 15, of which 12 were waited for; matrix products, arithmetic and copies ran while one was open for 11% of the time, Pallas kernels for 0%

profile of v1, /device:TPU:0, one launch (start us, length us, event | category | flops | bytes accessed | tf_op | source)
XLA Modules:
  0.0 822.3 jit_solution(14970287294636493930)
XLA Ops:
  9.1 1.2 constant_dynamic-slice_fusion.8
  10.3 1.9 concatenate.32
  16.1 2.6 convert_reduce_fusion
  18.7 5.4 multiply_sine_fusion
  24.1 1.3 broadcast_in_dim.29
  25.4 4.3 concatenate.34.table_ref
  31.8 24.6 %all_gather.35 = bf16[1024,256]{1,0:T(8,128)(2,1)S(1)} all-gather(bf16[256,256]{1,0:T(8,128)(2,1)S(1)} %pad_maximum_fusion.1), channel_id=1, replica_groups=mesh['fsdp'=4,'context'=4,'tensor'=2] {'fsdp'}, dimensions={0}, use_global_device_ids=true | all-gather | bytes 655360 | tf_op jit(solution)/shard_map/all_gather | solution.py:480
  56.4 8.3 %all-gather.13.cloned.1.call-done = bf16[1024,896]{1,0:T(8,128)(2,1)} async-done(((bf16[256,896]{1,0:T(8,128)(2,1)}), bf16[1024,896]{1,0:T(8,128)(2,1)}) %all-gather.13.cloned.1.call-update) | async-done | bytes 1835024 | tf_op jit(solution)/shard_map/all_gather | solution.py:479
  64.8 1.1 slice.183
  67.1 51.2 %all-gather.11.cloned.1.call-done = bf16[2048,1024]{1,0:T(8,128)(2,1)} async-done(((bf16[512,1024]{1,0:T(8,128)(2,1)}), bf16[2048,1024]{1,0:T(8,128)(2,1)}) %all-gather.11.cloned.1.call-update) | async-done | bytes 4194320 | tf_op jit(solution)/shard_map/all_gather | solution.py:509
  118.3 3.2 fusion
  121.7 7.0 fusion.5.u_ref
  128.7 27.9 %shard_map.365 = (bf16[2048,256]{1,0:T(8,128)(2,1)S(1)}, f32[2048,256]{1,0:T(8,128)S(1)}, f32[2048,512]{1,0:T(8,128)}, f32[1536,128]{1,0:T(8,128)S(1)}, bf16[2048,128]{1,0:T(8,128)(2,1)S(1)}) custom-call(s32[8]{0:T(128)S(1)} %select_reduce_fusion.slots_ref, f32[2048,1024]{1,0:T(8,128)} %fusion.5.u_ref, f32[2048,256]{1,0:T(8,128)} %concatenate.34.table_ref, ...), custom_call_target="tpu_custom_call" | custom-call | tf_op jit(solution)/shard_map/pallas_call | solution.py:332
  157.5 1.4 copy-done.5
  159.6 3.2 convolution_convert_fusion.1
  164.9 49.5 %reduce-scatter.6.cloned.1.call-done = bf16[256,1024]{1,0:T(8,128)(2,1)} async-done(((bf16[2048,1024]{1,0:T(8,128)(2,1)}), bf16[256,1024]{1,0:T(8,128)(2,1)}) %reduce-scatter.6.cloned.1.call-update) | async-done | bytes 524304 | tf_op jit(solution)/shard_map/reduce_scatter | solution.py:522
  214.4 1.3 multiply_reduce_fusion
  215.7 2.1 multiply_convert_fusion.3
  218.9 34.6 %all-gather.17.cloned.1.call-done = bf16[1024,768]{1,0:T(8,128)(2,1)} async-done(((bf16[256,768]{1,0:T(8,128)(2,1)}), bf16[1024,768]{1,0:T(8,128)(2,1)}) %all-gather.17.cloned.1.call-update) | async-done | bytes 1572880 | tf_op jit(solution)/shard_map/all_gather | solution.py:481
  253.6 38.1 %all-gather.15.cloned.1.call-done = bf16[2048,1024]{1,0:T(8,128)(2,1)} async-done(((bf16[256,1024]{1,0:T(8,128)(2,1)}), bf16[2048,1024]{1,0:T(8,128)(2,1)}) %all-gather.15.cloned.1.call-update) | async-done | bytes 4194320 | tf_op jit(solution)/shard_map/all_gather | solution.py:528
  291.7 5.1 fusion.38
  296.7 3.7 fusion.42
  300.5 45.8 %all-gather.21.cloned.1.call-done = bf16[2048,1024]{1,0:T(8,128)(2,1)} async-done(((bf16[512,1024]{1,0:T(8,128)(2,1)}), bf16[2048,1024]{1,0:T(8,128)(2,1)}) %all-gather.21.cloned.1.call-update) | async-done | bytes 4194320 | tf_op jit(solution)/shard_map/all_gather | solution.py:510
  346.2 6.6 multiply_convert_fusion
  352.9 1.3 fusion.40
  354.2 3.3 add_convert_fusion
  357.6 51.4 %reduce-scatter.10.cloned.1.call-done = bf16[256,1024]{1,0:T(8,128)(2,1)} async-done(((bf16[2048,1024]{1,0:T(8,128)(2,1)}), bf16[256,1024]{1,0:T(8,128)(2,1)}) %reduce-scatter.10.cloned.1.call-update) | async-done | bytes 524304 | tf_op jit(solution)/shard_map/reduce_scatter | solution.py:522
  409.0 1.6 fusion.28
  410.6 2.3 fusion.46
  413.2 36.6 %all-gather.23.cloned.1.call-done = bf16[2048,1024]{1,0:T(8,128)(2,1)} async-done(((bf16[256,1024]{1,0:T(8,128)(2,1)}), bf16[2048,1024]{1,0:T(8,128)(2,1)}) %all-gather.23.cloned.1.call-update) | async-done | bytes 4194320 | tf_op jit(solution)/shard_map/all_gather | solution.py:540
  449.8 4.4 convolution_convert_fusion.4.dag_ref
  454.2 43.3 %shard_map.366 = (bf16[2048,896]{1,0:T(8,128)(2,1)}, f32[8,512]{1,0:T(8,128)}) custom-call(s32[8]{0:T(128)} %copy-done.9, bf16[2048,256]{1,0:T(8,128)(2,1)} %convolution_convert_fusion.4.dag_ref, bf16[2048,256]{1,0:T(8,128)(2,1)} %copy-done.2, f32[2048,1024]{1,0:T(8,128)} %fusion.5.u_ref, f32[2048,256]{1,0:T(8,128)} %concatenate.34.table_ref, ...), custom_call_target="tpu_custom_call" | custom-call | tf_op jit(solution)/shard_map/pallas_call | solution.py:379
  497.5 8.2 convolution_convert_fusion.2
  505.8 1.1 copy-done.16
  507.0 4.4 convolution_convert_fusion
  511.6 9.9 %convert_dynamic-update-slice_fusion = bf16[1024,1920]{0,1:T(8,128)(2,1)} fusion(bf16[2048,896]{1,0:T(8,128)(2,1)} %get-tuple-element.68, bf16[2048,1024]{1,0:T(8,128)(2,1)} %all-gather.11.cloned.1.call-done, f32[1024]{0:T(1024)S(1)} %copy-done.29, f32[2048]{0:T(1024)S(1)} %add_rsqrt_fusion), kind=kOutput, calls=%fused_computation.29 | convolution fusion | flops 3767402496 | bytes 9711616 | tf_op jit(solution)/shard_map/dot_general | solution.py:25
  521.6 2.1 fusion.13
  524.2 2.1 fusion.12
  526.4 2.1 fusion.11
  528.5 1.1 copy-done.34
  529.6 2.1 fusion.18
  531.8 25.4 %reduce-scatter.12.cloned.1.call-done = bf16[256,1024]{1,0:T(8,128)(2,1)} async-done(((bf16[2048,1024]{1,0:T(8,128)(2,1)}), bf16[256,1024]{1,0:T(8,128)(2,1)}) %reduce-scatter.12.cloned.1.call-update) | async-done | bytes 524304 | tf_op jit(solution)/shard_map/reduce_scatter | solution.py:522
  557.2 1.4 fusion.34
  558.6 53.5 %reduce-scatter.8.cloned.1.call-done = bf16[256,1024]{1,0:T(8,128)(2,1)} async-done(((bf16[2048,1024]{1,0:T(8,128)(2,1)}), bf16[256,1024]{1,0:T(8,128)(2,1)}) %reduce-scatter.8.cloned.1.call-update) | async-done | bytes 524304 | tf_op jit(solution)/shard_map/reduce_scatter | solution.py:522
  612.1 3.2 fusion.23
  616.2 71.0 %reduce-scatter.14.cloned.1.call-done = bf16[256,1920]{0,1:T(8,128)(2,1)} async-done(((bf16[1024,1920]{0,1:T(8,128)(2,1)}), bf16[256,1920]{0,1:T(8,128)(2,1)}) %reduce-scatter.14.cloned.1.call-update) | async-done | bytes 983056 | tf_op jit(solution)/shard_map/reduce_scatter | solution.py:560
  689.0 41.4 %psum.14 = f32[9288]{0:T(1024)S(1)} all-reduce(f32[9288]{0:T(1024)S(1)} %concatenate.38), channel_id=1, replica_groups=mesh['fsdp'=4,'context'=4,'tensor'=2] {'fsdp','context','tensor'}, use_global_device_ids=true, to_apply=%region_16.17 | all-reduce | flops 9288 | bytes 74304 | tf_op jit(solution)/shard_map/psum | solution.py:593
  734.0 30.7 %all-gather.27.cloned.1.call-done = bf16[1024,1920]{0,1:T(8,128)(2,1)} async-done(((bf16[256,1920]{0,1:T(8,128)(2,1)}), bf16[1024,1920]{0,1:T(8,128)(2,1)}) %all-gather.27.cloned.1.call-update) | async-done | bytes 3932176 | tf_op jit(solution)/shard_map/all_gather | solution.py:561
  764.7 8.8 %reshape.259 = f32[4,256,1920]{1,0,2:T(4,128)} reshape(bf16[1024,1920]{0,1:T(8,128)(2,1)} %all-gather.27.cloned.1.call-done) | data formatting | bytes 11796480 | tf_op jit(solution)/shard_map/convert_element_type | solution.py:561
  773.5 3.7 slice_bitcast_fusion
  777.2 13.0 %reduce_sum.133 = f32[256,1920]{0,1:T(8,128)} reduce(f32[4,256,1920]{1,0,2:T(4,128)} %reshape.259, f32[]{:T(128)} %constant.119.clone.1), dimensions={0}, to_apply=%region_18.19 | reduce | flops 1474560 | bytes 9830404 | tf_op jit(solution)/shard_map/reduce_sum | solution.py:567
  790.3 1.7 slice.194
  791.9 3.2 fusion.47
  795.1 1.5 copy.122
  796.6 1.2 copy.141
  797.8 1.5 copy.123
  799.4 1.2 copy.142
  801.2 1.2 copy.143
  802.4 1.3 copy.135
  803.7 1.1 copy.128
  805.0 1.1 copy.129
  806.4 1.1 copy.131
  808.3 1.1 fusion.48
  811.8 1.8 copy.130
  (190 shorter events, 27.8 us)
Async XLA Ops:
  7.2 155.7 %copy-start = (bf16[256,1024]{1,0:T(8,128)(2,1)S(1)}, bf16[256,1024]{1,0:T(8,128)(2,1)}, u32[]{:S(2)}) copy-start(bf16[256,1024]{1,0:T(8,128)(2,1)} %param.46) | copy-start | bytes 1572868
  7.2 57.6 %all-gather.13.cloned.1.call-start = ((), (), s32[]{:S(2)}) async-start(), calls=%async_computation.6 | async-start | bytes 2293760 | tf_op jit(solution)/shard_map/all_gather | solution.py:479
  12.2 106.1 %all-gather.11.cloned.1.call-start = ((), (), s32[]{:S(2)}) async-start(), calls=%async_computation.5 | async-start | bytes 5242880 | tf_op jit(solution)/shard_map/all_gather | solution.py:509
  12.9 201.4 %reduce-scatter.6.cloned.1.call-start = ((), (), s32[]{:S(2)}) async-start(), calls=%async_computation.7 | async-start | bytes 4718592 | tf_op jit(solution)/shard_map/reduce_scatter | solution.py:522
  16.1 112.6 %copy-start.8 = (f32[8,256]{1,0:T(8,128)}, f32[8,256]{1,0:T(8,128)S(1)}, u32[]{:S(2)}) copy-start(f32[8,256]{1,0:T(8,128)S(1)} %scatter.14.heads_ref) | copy-start | bytes 24580
  24.1 6.4 copy-start.36
  24.1 6.5 copy-start.28
  25.4 31.1 %copy-start.31 = (f32[4,256]{1,0:T(4,128)S(1)}, f32[4,256]{1,0:T(4,128)}, u32[]{:S(2)}) copy-start(f32[4,256]{1,0:T(4,128)} %param.40) | copy-start | bytes 12292
  30.6 98.1 %copy-start.9 = (s32[8]{0:T(128)}, s32[8]{0:T(128)S(1)}, u32[]{:S(2)}) copy-start(s32[8]{0:T(128)S(1)} %select_reduce_fusion.slots_ref) | copy-start | bytes 100
  56.4 72.2 %copy-start.7 = (f32[4,512]{1,0:T(4,128)}, f32[4,512]{1,0:T(4,128)S(1)}, u32[]{:S(2)}) copy-start(f32[4,512]{1,0:T(4,128)S(1)} %pad_maximum_fusion.2.taps_ref) | copy-start | bytes 24580
  66.0 55.4 %slice-start.2 = ((bf16[1024,896]{1,0:T(8,128)(2,1)}), bf16[1024,768]{1,0:T(8,128)(2,1)S(1)}, s32[]{:S(2)}) async-start(bf16[1024,896]{1,0:T(8,128)(2,1)} %all-gather.13.cloned.1.call-done), calls=%async_computation.22 | async-start | bytes 3145728 | tf_op jit(solution)/shard_map/slice | solution.py:485
  66.1 55.4 %slice-start.3 = ((bf16[1024,896]{1,0:T(8,128)(2,1)}), bf16[1024,64]{1,0:T(8,128)(2,1)S(1)}, s32[]{:S(2)}) async-start(bf16[1024,896]{1,0:T(8,128)(2,1)} %all-gather.13.cloned.1.call-done), calls=%async_computation.23 | async-start | bytes 524288 | tf_op jit(solution)/shard_map/slice | solution.py:487
  66.1 55.4 %copy-start.29 = (f32[1024]{0:T(1024)S(1)}, f32[1024]{0:T(1024)}, u32[]{:S(2)}) copy-start(f32[1024]{0:T(1024)} %param.31) | copy-start | bytes 12292
  67.1 54.4 %copy-start.26 = (bf16[1024,192]{1,0:T(8,128)(2,1)S(1)}, bf16[1024,192]{1,0:T(8,128)(2,1)}, u32[]{:S(2)}) copy-start(bf16[1024,192]{1,0:T(8,128)(2,1)} %copy.113) | copy-start | bytes 1179652
  118.2 3.4 copy-start.14
  156.6 0.9 copy-start.4
  157.5 1.4 copy-start.5
  158.8 0.8 copy-start.6
  159.6 3.2 copy-start.2
  162.8 51.5 %copy-start.10 = (bf16[512,1024]{1,0:T(8,128)(2,1)S(1)}, bf16[512,1024]{1,0:T(8,128)(2,1)}, u32[]{:S(2)}) copy-start(bf16[512,1024]{1,0:T(8,128)(2,1)} %param.28) | copy-start | bytes 3145732
  162.9 52.8 %copy-start.27 = (f32[1024]{0:T(1024)S(1)}, f32[1024]{0:T(1024)}, u32[]{:S(2)}) copy-start(f32[1024]{0:T(1024)} %param.45) | copy-start | bytes 12292
  162.9 90.7 %all-gather.17.cloned.1.call-start = ((), (), s32[]{:S(2)}) async-start(), calls=%async_computation.9 | async-start | bytes 1966080 | tf_op jit(solution)/shard_map/all_gather | solution.py:481
  164.8 126.8 %all-gather.15.cloned.1.call-start = ((), (), s32[]{:S(2)}) async-start(), calls=%async_computation.8 | async-start | bytes 4718592 | tf_op jit(solution)/shard_map/all_gather | solution.py:528
  217.8 128.5 %all-gather.21.cloned.1.call-start = ((), (), s32[]{:S(2)}) async-start(), calls=%async_computation.12 | async-start | bytes 5242880 | tf_op jit(solution)/shard_map/all_gather | solution.py:510
  218.4 190.7 %reduce-scatter.10.cloned.1.call-start = ((), (), s32[]{:S(2)}) async-start(), calls=%async_computation.13 | async-start | bytes 4718592 | tf_op jit(solution)/shard_map/reduce_scatter | solution.py:522
  291.7 5.1 copy-start.32
  346.2 6.7 copy-start.21
  352.9 1.3 copy-start.19
  352.9 1.3 copy-start.22
  357.5 51.5 %copy-start.11 = (bf16[256,1024]{1,0:T(8,128)(2,1)S(1)}, bf16[256,1024]{1,0:T(8,128)(2,1)}, u32[]{:S(2)}) copy-start(bf16[256,1024]{1,0:T(8,128)(2,1)} %reduce-scatter.6.cloned.1.call-done) | copy-start | bytes 1572868
  357.5 53.1 %copy-start.13 = (bf16[512,1024]{1,0:T(8,128)(2,1)S(1)}, bf16[512,1024]{1,0:T(8,128)(2,1)}, u32[]{:S(2)}) copy-start(bf16[512,1024]{1,0:T(8,128)(2,1)} %param.49) | copy-start | bytes 3145732
  357.5 92.3 %all-gather.23.cloned.1.call-start = ((), (), s32[]{:S(2)}) async-start(), calls=%async_computation.14 | async-start | bytes 4718592 | tf_op jit(solution)/shard_map/all_gather | solution.py:540
  412.9 144.2 %reduce-scatter.12.cloned.1.call-start = ((), (), s32[]{:S(2)}) async-start(), calls=%async_computation.15 | async-start | bytes 4718592 | tf_op jit(solution)/shard_map/reduce_scatter | solution.py:522
  454.2 43.3 %copy-start.18 = (bf16[1024,896]{1,0:T(8,128)(2,1)S(1)}, bf16[1024,896]{1,0:T(8,128)(2,1)}, u32[]{:S(2)}) copy-start(bf16[1024,896]{1,0:T(8,128)(2,1)} %all-gather.13.cloned.1.call-done) | copy-start | bytes 5505028
  505.7 1.2 copy-start.16
  505.8 106.4 %reduce-scatter.8.cloned.1.call-start = ((), (), s32[]{:S(2)}) async-start(), calls=%async_computation.10 | async-start | bytes 4718592 | tf_op jit(solution)/shard_map/reduce_scatter | solution.py:522
  511.3 10.2 %copy-start.3 = (bf16[2048,256]{1,0:T(8,128)(2,1)S(1)}, bf16[2048,256]{1,0:T(8,128)(2,1)}, u32[]{:S(2)}) copy-start(bf16[2048,256]{1,0:T(8,128)(2,1)} %copy-done.2) | copy-start | bytes 3145732
  511.4 175.8 %reduce-scatter.14.cloned.1.call-start = ((), (), s32[]{:S(2)}) async-start(), calls=%async_computation.17 | async-start | bytes 4915200 | tf_op jit(solution)/shard_map/reduce_scatter | solution.py:560
  511.6 9.9 %copy-start.35 = (bf16[2048,1024]{1,0:T(8,128)(2,1)S(1)}, bf16[2048,1024]{1,0:T(8,128)(2,1)}, u32[]{:S(2)}) copy-start(bf16[2048,1024]{1,0:T(8,128)(2,1)} %all-gather.23.cloned.1.call-done) | copy-start | bytes 12582916
  521.5 2.1 copy-start.20
  521.5 2.7 copy-start.33
  524.2 2.1 copy-start.23
  526.4 2.1 copy-start.17
  526.4 3.3 copy-start.34
  531.7 80.4 %copy-start.12 = (bf16[256,1024]{1,0:T(8,128)(2,1)S(1)}, bf16[256,1024]{1,0:T(8,128)(2,1)}, u32[]{:S(2)}) copy-start(bf16[256,1024]{1,0:T(8,128)(2,1)} %reduce-scatter.10.cloned.1.call-done) | copy-start | bytes 1572868
  531.8 155.5 %copy-start.30 = (f32[8,512]{1,0:T(8,128)S(1)}, f32[8,512]{1,0:T(8,128)}, u32[]{:S(2)}) copy-start(f32[8,512]{1,0:T(8,128)} %get-tuple-element.69) | copy-start | bytes 49156
  531.8 202.2 %all-gather.19.cloned.1.call-start = ((), (), s32[]{:S(2)}) async-start(), calls=%async_computation.11 | async-start | bytes 1572864 | tf_op jit(solution)/shard_map/all_gather | solution.py:547
  615.4 118.6 %all-gather.25.cloned.1.call-start = ((), (), s32[]{:S(2)}) async-start(), calls=%async_computation.16 | async-start | bytes 1572864 | tf_op jit(solution)/shard_map/all_gather | solution.py:548
  616.1 148.6 %all-gather.27.cloned.1.call-start = ((), (), s32[]{:S(2)}) async-start(), calls=%async_computation.19 | async-start | bytes 4915200 | tf_op jit(solution)/shard_map/all_gather | solution.py:561
  687.2 124.6 %all-reduce.4.cloned.1.call-start = ((), (), s32[]{:S(2)}) async-start(), calls=%async_computation.18 | async-start | bytes 524288 | tf_op jit(solution)/shard_map/psum | solution.py:568
  801.2 3.6 copy-start.15
  803.7 3.8 slice-start.1
  805.0 6.1 slice-start
  805.0 8.5 %copy-start.24 = (bf16[512,1024]{1,0:T(8,128)(2,1)S(1)}, bf16[512,1024]{1,0:T(8,128)(2,1)}, u32[]{:S(2)}) copy-start(bf16[512,1024]{1,0:T(8,128)(2,1)} %all-gather.19.cloned.1.call-done) | copy-start | bytes 3145732
  806.3 8.2 copy-start.25
  806.3 9.2 %copy-start.1 = (bf16[256,1024]{1,0:T(8,128)(2,1)S(1)}, bf16[256,1024]{1,0:T(8,128)(2,1)}, u32[]{:S(2)}) copy-start(bf16[256,1024]{1,0:T(8,128)(2,1)} %param.46) | copy-start | bytes 1572868
Sparse Core Ops, SparseCore 0:
  12.3 52.4 all-gather.12
  66.6 51.5 all-gather.10
  163.0 51.3 reduce-scatter.5
  216.5 37.0 all-gather.16
  256.1 35.5 all-gather.14
  293.5 52.6 all-gather.20
  357.7 51.3 reduce-scatter.9
  413.1 36.6 all-gather.22
  505.9 51.2 reduce-scatter.11
  560.8 51.3 reduce-scatter.7
  614.5 72.6 reduce-scatter.13
  689.1 9.4 all-gather.18
  700.7 10.1 all-gather.24
  712.6 52.0 all-gather.26
  792.1 18.2 all-reduce.3

commit v2 on v1

--- a/solution.py
+++ b/solution.py
@@ -414,6 +414,344 @@
     )(slot_of, dag, ag, u, table, head_rows, taps, y, conv, states, states, keyval)
 
 
+MESH = pl.DeviceIdType.MESH
+
+
+class Place:
+    def __init__(self):
+        self.c = lax.axis_index("context")
+        self.t = lax.axis_index("tensor")
+        count = lax.axis_size("context")
+        self.chips = [
+            self.c,
+            self.c + 1 - 2 * (self.c % 2),
+            (self.c + count // 2) % count,
+            count - 1 - self.c,
+        ]
+
+    def slot(self, mask, sibling=False):
+        core = 1 - self.t if sibling else self.t
+        return self.chips[mask] * 2 + core
+
+    def target(self, mask):
+        if mask == 4:
+            return {"tensor": 1 - self.t}
+        return {"context": self.chips[mask]}
+
+    def greet(self, masks=(1, 2, 4)):
+        barrier = pltpu.get_barrier_semaphore()
+        for mask in masks:
+            pl.semaphore_signal(
+                barrier, inc=1, device_id=self.target(mask), device_id_type=MESH
+            )
+        pl.semaphore_wait(barrier, len(masks))
+
+
+class Wire:
+    def __init__(self, place, sems):
+        self.place = place
+        self.sems = sems
+        self.sent = []
+
+    def copy(self, source, target, index, mask):
+        return pltpu.make_async_remote_copy(
+            src_ref=source,
+            dst_ref=target,
+            send_sem=self.sems.at[0, index],
+            recv_sem=self.sems.at[1, index],
+            device_id=self.place.target(mask),
+            device_id_type=MESH,
+        )
+
+    def send(self, source, target, index, mask):
+        made = self.copy(source, target, index, mask)
+        made.start()
+        self.sent.append(made)
+
+    def arrive(self, target, index, mask):
+        self.copy(target, target, index, mask).wait_recv()
+
+    def finish(self):
+        for made in self.sent:
+            made.wait_send()
+        self.sent = []
+
+
+ROWS = HALF
+PART = HALF // 2
+TOP, END = pl.ds(0, PART), pl.ds(PART, PART)
+SCATTER_SEMS = 10
+GATHER_SEMS = 14
+
+
+def scatter_scratch(columns):
+    return [
+        pltpu.VMEM((4, ROWS, columns), BF16),
+        pltpu.VMEM((4, ROWS, columns), BF16),
+        pltpu.VMEM((6, PART, columns), BF16),
+        pltpu.VMEM((ROWS, columns), F32),
+        pltpu.SemaphoreType.DMA((2, SCATTER_SEMS)),
+    ]
+
+
+SCATTER_ORDER = (3, 1, 2, 0)
+
+
+class Scatter:
+    def __init__(self, place, scratch):
+        self.place = place
+        self.core_in, self.out, self.chip_in, self.kept, sems = scratch
+        self.wire = Wire(place, sems)
+
+    def to_core(self, mask, source):
+        index = SCATTER_ORDER.index(mask)
+        self.wire.send(source, self.core_in.at[index], index, 4)
+
+    def from_core(self, mask):
+        index = SCATTER_ORDER.index(mask)
+        self.wire.arrive(self.core_in.at[index], index, 4)
+        return self.core_in[index].astype(F32)
+
+    def first(self, mine, total, between=None):
+        wire, out, kept = self.wire, self.out, self.kept
+        both = mine(3) + self.from_core(3)
+        out[0] = both.astype(BF16)
+        wire.send(out.at[0, TOP], self.chip_in.at[0], 4, 1)
+        wire.send(out.at[0, END], self.chip_in.at[1], 5, 2)
+        both = mine(1) + self.from_core(1)
+        out[1] = both.astype(BF16)
+        wire.send(out.at[1, TOP], self.chip_in.at[2], 6, 1)
+        kept[END] = both[PART:]
+        both = mine(2) + self.from_core(2)
+        out[2] = both.astype(BF16)
+        wire.send(out.at[2, END], self.chip_in.at[3], 7, 2)
+        kept[TOP] = both[:PART]
+        total[...] = mine(0) + self.from_core(0)
+
+    def second(self):
+        wire, out, kept, came = self.wire, self.out, self.kept, self.chip_in
+        wire.arrive(came.at[0], 4, 1)
+        out[3, TOP] = (kept[TOP] + came[0].astype(F32)).astype(BF16)
+        wire.send(out.at[3, TOP], came.at[4], 8, 2)
+        wire.arrive(came.at[1], 5, 2)
+        out[3, END] = (kept[END] + came[1].astype(F32)).astype(BF16)
+        wire.send(out.at[3, END], came.at[5], 9, 1)
+
+    def last(self, total):
+        wire, came = self.wire, self.chip_in
+        wire.arrive(came.at[2], 6, 1)
+        wire.arrive(came.at[4], 8, 2)
+        total[TOP] += came[2].astype(F32) + came[4].astype(F32)
+        wire.arrive(came.at[3], 7, 2)
+        wire.arrive(came.at[5], 9, 1)
+        total[END] += came[3].astype(F32) + came[5].astype(F32)
+        wire.finish()
+
+
+class Gather:
+    def __init__(self, place, whole, sems):
+        self.place = place
+        self.whole = whole
+        self.wire = Wire(place, sems)
+
+    def rows(self, mask, sibling=False, half=None):
+        begin = self.place.slot(mask, sibling) * ROWS
+        if half is None:
+            return self.whole.at[pl.ds(pl.multiple_of(begin, ROWS), ROWS)]
+        return self.whole.at[pl.ds(pl.multiple_of(begin + half * PART, PART), PART)]
+
+    def start(self):
+        wire = self.wire
+        for half, mask, index in ((0, 1, 0), (1, 2, 1), (1, 1, 2), (0, 2, 3)):
+            wire.send(self.rows(0, half=half), self.rows(0, half=half), index, mask)
+        wire.send(self.rows(0), self.rows(0), 6, 4)
+
+    def relay(self):
+        wire = self.wire
+        wire.arrive(self.rows(1, half=0), 0, 1)
+        wire.send(self.rows(1, half=0), self.rows(1, half=0), 4, 2)
+        wire.arrive(self.rows(2, half=1), 1, 2)
+        wire.send(self.rows(2, half=1), self.rows(2, half=1), 5, 1)
+
+    def near(self):
+        wire = self.wire
+        wire.arrive(self.rows(1, half=1), 2, 1)
+        wire.send(self.rows(1), self.rows(1), 7, 4)
+        wire.arrive(self.rows(2, half=0), 3, 2)
+        wire.send(self.rows(2), self.rows(2), 8, 4)
+
+    def far(self):
+        wire = self.wire
+        wire.arrive(self.rows(3, half=0), 4, 2)
+        wire.arrive(self.rows(3, half=1), 5, 1)
+        wire.send(self.rows(3), self.rows(3), 9, 4)
+
+    def core(self, mask):
+        index = (6, 7, 8, 9)[mask]
+        self.wire.arrive(self.rows(mask, sibling=True), index, 4)
+
+    def finish(self):
+        self.wire.finish()
+
+
+def slot_rows(slot):
+    return pl.ds(pl.multiple_of(slot * ROWS, ROWS), ROWS)
+
+
+def norm_scale(values):
+    return lax.rsqrt(jnp.mean(values * values, axis=1, keepdims=True) + epsilon)
+
+
+def middle_kernel(
+    ag_ref, wout_ref, wffn_ref, x_ref, cot_ref, cot_all_ref, gain_ref,
+    nffn_ref, hidden_ref, dgu_ref, dm_ref, dag_ref, outp_ref, mixed_ref, dmixed_ref, dgain_ref, dw_ref,
+    part, *scratch,
+):
+    place = Place()
+    first = Scatter(place, scratch[0:5])
+    back = Scatter(place, scratch[5:10])
+    forth = Gather(place, nffn_ref, scratch[10])
+    home = Gather(place, dm_ref, scratch[11])
+    hid = hidden_ref.shape[1]
+    place.greet()
+
+    def block(mask, sibling=False):
+        return dot(ag_ref[slot_rows(place.slot(mask, sibling)), :], wout_ref[...], 1, 1)
+
+    for mask in SCATTER_ORDER:
+        rows = slot_rows(place.slot(mask, True))
+        part[rows, :] = block(mask, True).astype(BF16)
+        first.to_core(mask, part.at[rows])
+    first.first(block, mixed_ref)
+    first.second()
+    mixed_ref[...] += x_ref[...].astype(F32)
+    first.last(mixed_ref)
+    mixed = mixed_ref[...]
+    gain = gain_ref[...]
+    scale = norm_scale(mixed)
+    own = slot_rows(place.slot(0))
+    nffn_ref[own, :] = (mixed * scale * gain).astype(BF16)
+    forth.start()
+
+    def work(slot):
+        rows = slot_rows(slot)
+        normed = nffn_ref[rows, :]
+        gate_up = dot(normed, wffn_ref[:, : 2 * hid])
+        dhidden = dot(cot_all_ref[rows, :], wffn_ref[:, 2 * hid :]).astype(BF16).astype(F32)
+        gate, up = gate_up[:, :hid], gate_up[:, hid:]
+        sig = sigmoid(gate)
+        silu = gate * sig
+        dgate = dhidden * up * (sig * (1.0 + gate * (1.0 - sig)))
+        hidden_ref[rows, :] = (silu * up).astype(BF16)
+        dgu_ref[rows, :hid] = dgate.astype(BF16)
+        dgu_ref[rows, hid:] = (dhidden * silu).astype(BF16)
+        part[rows, :] = dot(dgu_ref[rows, :], wffn_ref[:, : 2 * hid], 1, 1).astype(BF16)
+
+    def hand_over(mask):
+        slot = place.slot(mask, True)
+        work(slot)
+        back.to_core(mask, part.at[slot_rows(slot)])
+
+    work(place.slot(0))
+    forth.relay()
+    forth.core(0)
+    hand_over(0)
+    forth.near()
+    forth.core(1)
+    hand_over(1)
+    forth.core(2)
+    hand_over(2)
+    work(place.slot(1))
+    forth.far()
+    work(place.slot(2))
+    forth.core(3)
+    hand_over(3)
+    work(place.slot(3))
+    forth.finish()
+
+    def ready(mask):
+        return part[slot_rows(place.slot(mask)), :].astype(F32)
+
+    back.first(ready, dmixed_ref)
+
+    def out_block(slot, carry):
+        rows = slot_rows(slot)
+        outp_ref[rows, :] = dot(hidden_ref[rows, :], wffn_ref[:, 2 * hid :], 1, 1).astype(BF16)
+        return carry
+
+    lax.fori_loop(0, 8, out_block, 0)
+    back.second()
+    dw_ref[:, : 2 * hid] = dot(nffn_ref[...], dgu_ref[...], 0, 0).astype(BF16)
+    back.last(dmixed_ref)
+    dnffn = dmixed_ref[...]
+    mixed = mixed_ref[...]
+    scale = norm_scale(mixed)
+    spread = dnffn * gain
+    pull = jnp.mean(spread * mixed, axis=1, keepdims=True)
+    dgain_ref[...] = jnp.broadcast_to(
+        jnp.sum(dnffn * mixed * scale, axis=0, keepdims=True), dgain_ref.shape
+    )
+    dmixed = cot_ref[...].astype(F32) + scale * (spread - mixed * (scale * scale * pull))
+    dmixed_ref[...] = dmixed
+    dm_ref[own, :] = dmixed.astype(BF16)
+    home.start()
+
+    def pull_back(slot):
+        rows = slot_rows(slot)
+        dag_ref[rows, :] = dot(dm_ref[rows, :], wout_ref[...]).astype(BF16)
+
+    pull_back(place.slot(0))
+    home.relay()
+    dw_ref[:, 2 * hid : 3 * hid] = dot(cot_all_ref[...], hidden_ref[...], 0, 0).astype(BF16)
+    home.core(0)
+    pull_back(place.slot(0, True))
+    home.near()
+    pull_back(place.slot(1))
+    pull_back(place.slot(2))
+    home.far()
+    pull_back(place.slot(3))
+    for mask in (1, 2, 3):
+        home.core(mask)
+        pull_back(place.slot(mask, True))
+    dw_ref[:, 3 * hid :] = dot(dm_ref[...], ag_ref[...], 0, 0).astype(BF16)
+    home.finish()
+
+
+def middle(ag, wout, wffn, x_own, cot_own, cot_all, gain):
+    count, model = cot_all.shape
+    hid = wffn.shape[1] // 3
+    columns = ag.shape[1]
+    vmem = pl.BlockSpec(memory_space=pltpu.VMEM)
+    shape = jax.ShapeDtypeStruct
+    return pl.pallas_call(
+        middle_kernel,
+        out_shape=(
+            shape((count, model), BF16),
+            shape((count, hid), BF16),
+            shape((count, 2 * hid), BF16),
+            shape((count, model), BF16),
+            shape((count, columns), BF16),
+            shape((count, model), BF16),
+            shape((ROWS, model), F32),
+            shape((ROWS, model), F32),
+            shape((8, model), F32),
+            shape((model, 3 * hid + columns), BF16),
+        ),
+        in_specs=[vmem] * 7,
+        out_specs=(vmem,) * 10,
+        scratch_shapes=[pltpu.VMEM((count, model), BF16)]
+        + scatter_scratch(model)
+        + scatter_scratch(model)
+        + [pltpu.SemaphoreType.DMA((2, GATHER_SEMS))] * 2,
+        compiler_params=pltpu.CompilerParams(
+            collective_id=1, has_side_effects=True, vmem_limit_bytes=60 << 20
+        ),
+        cost_estimate=pl.CostEstimate(
+            flops=20 * count * model * hid, bytes_accessed=40 << 20, transcendentals=count * hid
+        ),
+    )(ag, wout, wffn, x_own, cot_own, cot_all, gain.reshape(1, -1))
+
+
 GROUP = ("context", "tensor")
 
 
@@ -488,7 +826,6 @@
         ],
         axis=1,
     )
-    w_gate, w_up, w_down = wffn_all[:, :hid], wffn_all[:, hid : 2 * hid], wffn_all[:, 2 * hid :]
 
     order = deal[0]
     ids = jnp.arange(order.shape[0], dtype=jnp.int32)
@@ -510,8 +847,8 @@
     cot_all = lax.all_gather(cotangent, "context", axis=0, tiled=True)
     row_count = tokens.shape[0]
     half = row_count // 2
-    x_own = lax.dynamic_slice_in_dim(tokens, t * half, half, axis=0).astype(F32)
-    cot_own = lax.dynamic_slice_in_dim(cotangent, t * half, half, axis=0).astype(F32)
+    x_own = lax.dynamic_slice_in_dim(tokens, t * half, half, axis=0)
+    cot_own = lax.dynamic_slice_in_dim(cotangent, t * half, half, axis=0)
 
     xf = x_all.astype(F32)
     normed = (xf * inverse_rms(xf) * gain_mix).astype(BF16)
@@ -523,41 +860,24 @@
             values.astype(BF16), GROUP, scatter_dimension=0, tiled=True
         ).astype(F32)
 
-    mixed = x_own + scatter(low_dot(ag, wout_all, 1, 1))
-    nffn_own = (mixed * inverse_rms(mixed) * gain_ffn).astype(BF16)
-    nffn = lax.all_gather(nffn_own, GROUP, axis=0, tiled=True)
-    gate = low_dot(nffn, w_gate)
-    up = low_dot(nffn, w_up)
-    sig = sigmoid(gate)
-    hidden = (gate * sig * up).astype(BF16)
-    out_own = mixed + scatter(low_dot(hidden, w_down, 1, 1))
-    dhidden = low_dot(cot_all, w_down).astype(BF16).astype(F32)
-    dgate = (dhidden * up * (sig * (1.0 + gate * (1.0 - sig)))).astype(BF16)
-    dup = (dhidden * gate * sig).astype(BF16)
-    dnffn = scatter(low_dot(dgate, w_gate, 1, 1) + low_dot(dup, w_up, 1, 1))
-    dm_norm, dgain_ffn = norm_back(mixed, gain_ffn, dnffn)
-    dmixed = cot_own + dm_norm
-    dm_all = lax.all_gather(dmixed.astype(BF16), GROUP, axis=0, tiled=True)
-    dag = low_dot(dm_all, wout_all).astype(BF16)
+    nffn, hidden, dgu, dm_all, dag, out_part, mixed, dmixed, dgain_rows, dw_mid = middle(
+        ag, wout_all, wffn_all, x_own, cot_own, cot_all, gain_ffn
+    )
+    dgain_ffn = dgain_rows[0]
+    out_own = mixed + scatter(out_part)
     du, stats = mixer_backward(dag, ag, u, table, head_rows, taps, y, conv, states, keyval, slot_of)
     dnormed = scatter(low_dot(du, w_all, 1, 1))
-    dx_norm, dgain_mix = norm_back(x_own, gain_mix, dnormed)
+    dx_norm, dgain_mix = norm_back(x_own.astype(F32), gain_mix, dnormed)
     dx_own = dmixed + dx_norm
 
     mixed_out = lax.all_gather(out_own.astype(BF16), "tensor", axis=0, tiled=True)
     tokens_grad = lax.all_gather(dx_own.astype(BF16), "tensor", axis=0, tiled=True)
 
-    dw = jnp.concatenate(
-        [
-            low_dot(normed, du, 0, 0),
-            low_dot(dm_all, ag, 0, 0),
-            low_dot(nffn, dgate, 0, 0),
-            low_dot(nffn, dup, 0, 0),
-            low_dot(cot_all, hidden, 0, 0),
-        ],
-        axis=1,
-    ).astype(BF16)
-    dw = lax.psum_scatter(dw, "fsdp", scatter_dimension=0, tiled=True)
+    dw_mid = lax.psum_scatter(dw_mid, "fsdp", scatter_dimension=0, tiled=True)
+    dw = lax.psum_scatter(
+        low_dot(normed, du, 0, 0).astype(BF16), "fsdp", scatter_dimension=0, tiled=True
+    )
+    dw = jnp.concatenate([dw, dw_mid[:, 3 * hid :], dw_mid[:, : 3 * hid]], axis=1)
     dw_all = lax.all_gather(dw, "context", axis=0, tiled=False).astype(F32)
 
     def spread(begin, width):

time: 827 us -> 703 us (0.85)
  waiting for transfers between devices: 498 us -> 327 us
  Pallas kernels: 71.2 us -> 172 us
  matrix products: 65.6 us -> 24.7 us
    pallas_call x0 -> x1, Pallas kernels: none -> 99.8 us  [middle(): pl.pallas_call(middle_kernel, out_shape=(shape((count, model), BF16), sha...]
    reduce_scatter x4 -> x2, waiting for transfers between devices: 180 us -> 91.6 us  [scatter(): lax.psum_scatter(values.astype(BF16), GROUP, scatter_dimension=0, tiled=T...]
    all_gather x2 -> x0, waiting for transfers between devices: 74.7 us -> none  [the longest x1 38.1 us: per_device(): nffn = lax.all_gather(nffn_own, GROUP, axis=0, tiled=True)]
    dot_general x15 -> x3, matrix products: 65.6 us -> 24.7 us  [dot(): lax.dot_general(left, right, (((left_dim,), (right_dim,)), ((), ())), pre...]
    all_gather x1, waiting for transfers between devices: 34.6 us -> 0.01 us  [per_device(): wffn_all = lax.all_gather(mine_ffn, 'fsdp', axis=0, tiled=True)]
    psum x1, waiting for transfers between devices: 0.01 us -> 13.9 us  [per_device(): dbc = lax.psum(summed[:, 256:512], 'tensor')]
    reduce_scatter x1 -> x2, waiting for transfers between devices: 71 us -> 83.4 us  [the longest x1 44.1 us: per_device(): dw_mid = lax.psum_scatter(dw_mid, 'fsdp', scatter_dimension=0, tiled=True)]
    convert_element_type x1 -> x0, local copies, waits for them, and re-layouts: 8.81 us -> none  [per_device(): dw_all = lax.all_gather(dw, 'context', axis=0, tiled=False).astype(F32)]
  transfers between devices with their start and end apart: 15 -> 12, of which waited for: 12 -> 9; matrix products, arithmetic and copies ran while one was open for 11% -> 9% of each run, Pallas kernels for 0% -> 4%
where the time goes in v2:
time: 703 us; the launch traced here: 694 us
  waiting for transfers between devices  327 us (47%)
  Pallas kernels  172 us (24%)
  blocking collectives  64.7 us (9%)
  local copies, waits for them, and re-layouts  60.3 us (9%)
  other arithmetic  29.2 us (4%)
  matrix products  24.7 us (4%)
  between operations  15.2 us (2%)
    pallas_call x1, Pallas kernels, middle(): pl.pallas_call(middle_kernel, out_shape=(shape((count, model), BF16), sha...  99.8 us
    reduce_scatter x2, waiting for transfers between devices, scatter(): lax.psum_scatter(values.astype(BF16), GROUP, scatter_dimension=0, tiled=T...  91.6 us
    all_gather x1, waiting for transfers between devices, per_device(): x_all = lax.all_gather(tokens, 'context', axis=0, tiled=True)  52 us
    all_gather x1, waiting for transfers between devices, per_device(): cot_all = lax.all_gather(cotangent, 'context', axis=0, tiled=True)  50 us
    reduce_scatter x1, waiting for transfers between devices, per_device(): dw_mid = lax.psum_scatter(dw_mid, 'fsdp', scatter_dimension=0, tiled=True)  44.1 us
    pallas_call x1, Pallas kernels, mixer_backward(): pl.pallas_call(mixer_backward_kernel, out_shape=(jax.ShapeDtypeStruct((co...  43.5 us
    psum x1, blocking collectives, per_device(): joined = lax.psum(jnp.concatenate(small), ('fsdp', 'context', 'tensor'))  40 us
    reduce_scatter x1, waiting for transfers between devices, per_device(): lax.psum_scatter(low_dot(normed, du, 0, 0).astype(BF16), 'fsdp', scatter_...  39.2 us
  transfers between devices with their start and end apart: 12, of which 9 were waited for; matrix products, arithmetic and copies ran while one was open for 9% of the time, Pallas kernels for 4%

profile of v2, /device:TPU:0, one launch (start us, length us, event | category | flops | bytes accessed | tf_op | source)
XLA Modules:
  0.0 693.8 jit_solution(3272350619754722820)
XLA Ops:
  7.3 0.8 constant_dynamic-slice_fusion.9
  8.3 0.9 constant_dynamic-slice_fusion.11
  9.2 1.2 constant_dynamic-slice_fusion.10
  10.4 1.9 concatenate.31
  13.1 1.0 constant_dynamic-slice_fusion.3
  14.1 0.8 pad_maximum_fusion.1
  16.8 1.8 convert_reduce_fusion
  18.6 5.4 multiply_sine_fusion
  23.9 1.3 broadcast_in_dim.50
  25.2 4.3 concatenate.33.table_ref
  29.6 0.8 constant_dynamic-slice_fusion.8
  30.6 1.0 constant_dynamic-slice_fusion.7
  31.7 1.9 fusion.15
  33.6 1.9 constant_dynamic-slice_fusion.1.cot_ref
  35.5 24.7 %all_gather.29.wout_ref = bf16[1024,256]{1,0:T(8,128)(2,1)} all-gather(bf16[256,256]{1,0:T(8,128)(2,1)S(1)} %pad_maximum_fusion.2), channel_id=1, replica_groups=mesh['fsdp'=4,'context'=4,'tensor'=2] {'fsdp'}, dimensions={0}, use_global_device_ids=true | all-gather | bytes 655360 | tf_op jit(solution)/shard_map/all_gather | solution.py:818
  60.2 4.6 all-gather.11.cloned.1.call-done
  64.9 1.1 slice.183
  66.4 52.0 %all-gather.9.cloned.1.call-done = bf16[2048,1024]{1,0:T(8,128)(2,1)} async-done(((bf16[512,1024]{1,0:T(8,128)(2,1)}), bf16[2048,1024]{1,0:T(8,128)(2,1)}) %all-gather.9.cloned.1.call-update) | async-done | bytes 4194320 | tf_op jit(solution)/shard_map/all_gather | solution.py:846
  118.4 3.2 fusion
  121.8 7.0 %fusion.3.u_ref = f32[2048,1024]{1,0:T(8,128)} fusion(bf16[1024,64]{1,0:T(8,128)(2,1)S(1)} %slice-done.1, bf16[1024,192]{1,0:T(8,128)(2,1)S(1)} %copy.88, bf16[1024,768]{1,0:T(8,128)(2,1)S(1)} %slice-done, bf16[2048,1024]{1,0:T(8,128)(2,1)S(1)} %copy-done.11, f32[1024]{0:T(1024)S(1)} %copy-done.20, f32[2048]{0:T(1024)S(1)} %add_rsqrt_fusion), kind=kOutput, calls=%fused_computation.8 | convolution fusion | flops 4309647360 | bytes 14692352 | tf_op jit(solution)/shard_map/dot_general | solution.py:25
  128.8 28.2 %shard_map.365 = (bf16[2048,256]{1,0:T(8,128)(2,1)S(1)}, f32[2048,256]{1,0:T(8,128)S(1)}, f32[2048,512]{1,0:T(8,128)}, f32[1536,128]{1,0:T(8,128)S(1)}, bf16[2048,128]{1,0:T(8,128)(2,1)S(1)}) custom-call(s32[8]{0:T(128)S(1)} %select_reduce_fusion.slots_ref, f32[2048,1024]{1,0:T(8,128)} %fusion.3.u_ref, f32[2048,256]{1,0:T(8,128)} %concatenate.33.table_ref, ...), custom_call_target="tpu_custom_call" | custom-call | tf_op jit(solution)/shard_map/pallas_call | solution.py:332
  157.0 0.9 copy-done.2
  157.9 1.3 copy-done.3
  159.2 1.0 copy-done.4
  160.1 0.8 copy-done.5
  160.9 50.0 %all-gather.15.cloned.1.call-done.cot_all_ref = bf16[2048,1024]{1,0:T(8,128)(2,1)} async-done(((bf16[512,1024]{1,0:T(8,128)(2,1)}), bf16[2048,1024]{1,0:T(8,128)(2,1)}) %all-gather.15.cloned.1.call-update) | async-done | bytes 4194320 | tf_op jit(solution)/shard_map/all_gather | solution.py:847
  210.9 99.8 %shard_map.366 = (bf16[2048,1024]{1,0:T(8,128)(2,1)}, bf16[2048,256]{1,0:T(8,128)(2,1)}, bf16[2048,512]{1,0:T(8,128)(2,1)}, bf16[2048,1024]{1,0:T(8,128)(2,1)}, ...) custom-call(bf16[2048,256]{1,0:T(8,128)(2,1)} %copy-done.4, ...), custom_call_target="tpu_custom_call" | custom-call | flops 10737418240 | bytes 41943040 | tf_op jit(solution)/shard_map/pallas_call | solution.py:726
  310.8 43.5 %shard_map.367 = (bf16[2048,896]{1,0:T(8,128)(2,1)}, f32[8,512]{1,0:T(8,128)}) custom-call(s32[8]{0:T(128)} %copy-done.8, bf16[2048,256]{1,0:T(8,128)(2,1)} %get-tuple-element.73.dag_ref, bf16[2048,256]{1,0:T(8,128)(2,1)} %copy-done.4, f32[2048,1024]{1,0:T(8,128)} %fusion.3.u_ref, f32[2048,256]{1,0:T(8,128)} %concatenate.33.table_ref, f32[8,256]{1,0:T(8,128)} %copy-done.7, ...), custom_call_target="tpu_custom_call" | custom-call | tf_op jit(solution)/shard_map/pallas_call | solution.py:379
  354.3 8.2 %convolution_convert_fusion = bf16[2048,1024]{1,0:T(8,128)(2,1)} fusion(bf16[2048,896]{1,0:T(8,128)(2,1)} %get-tuple-element.78, bf16[1024,896]{1,0:T(8,128)(2,1)S(1)} %copy-done.13), kind=kOutput, calls=%fused_computation.7 | convolution fusion | flops 3760193536 | bytes 9699328 | tf_op jit(solution)/shard_map/dot_general | solution.py:25
  364.0 9.6 %convolution_convert_fusion.1 = bf16[1024,896]{1,0:T(8,128)(2,1)} fusion(bf16[2048,896]{1,0:T(8,128)(2,1)} %get-tuple-element.78, bf16[2048,1024]{1,0:T(8,128)(2,1)} %all-gather.9.cloned.1.call-done, f32[1024]{0:T(1024)S(1)} %copy-done.20, f32[2048]{0:T(1024)S(1)} %add_rsqrt_fusion), kind=kOutput, calls=%fused_computation.18 | convolution fusion | flops 3767402496 | bytes 9711616 | tf_op jit(solution)/shard_map/dot_general | solution.py:25
  373.9 40.4 %reduce-scatter.7.cloned.1.call-done = bf16[256,1024]{1,0:T(8,128)(2,1)} async-done(((bf16[2048,1024]{1,0:T(8,128)(2,1)}), bf16[256,1024]{1,0:T(8,128)(2,1)}) %reduce-scatter.7.cloned.1.call-update) | async-done | bytes 524304 | tf_op jit(solution)/shard_map/reduce_scatter | solution.py:859
  414.2 1.4 fusion.20
  415.6 2.2 fusion.14
  417.9 51.3 %reduce-scatter.5.cloned.1.call-done = bf16[256,1024]{1,0:T(8,128)(2,1)} async-done(((bf16[2048,1024]{1,0:T(8,128)(2,1)}), bf16[256,1024]{1,0:T(8,128)(2,1)}) %reduce-scatter.5.cloned.1.call-update) | async-done | bytes 524304 | tf_op jit(solution)/shard_map/reduce_scatter | solution.py:859
  469.2 2.0 add_convert_fusion
  471.2 44.1 %reduce-scatter.11.cloned.1.call-done = bf16[256,1024]{1,0:T(8,128)(2,1)} async-done(((bf16[1024,1024]{1,0:T(8,128)(2,1)}), bf16[256,1024]{1,0:T(8,128)(2,1)}) %reduce-scatter.11.cloned.1.call-update) | async-done | bytes 524304 | tf_op jit(solution)/shard_map/reduce_scatter | solution.py:876
  515.3 1.0 slice.187
  516.4 0.9 slice.186
  517.3 39.2 %reduce-scatter.9.cloned.1.call-done = bf16[256,896]{1,0:T(8,128)(2,1)} async-done(((bf16[1024,896]{1,0:T(8,128)(2,1)}), bf16[256,896]{1,0:T(8,128)(2,1)}) %reduce-scatter.9.cloned.1.call-update) | async-done | bytes 458768 | tf_op jit(solution)/shard_map/reduce_scatter | solution.py:877
  556.5 2.0 pad_maximum_fusion
  559.2 0.8 slice.156
  561.1 40.0 %psum.14 = f32[9288]{0:T(1024)S(1)} all-reduce(f32[9288]{0:T(1024)S(1)} %concatenate.37), channel_id=1, replica_groups=mesh['fsdp'=4,'context'=4,'tensor'=2] {'fsdp','context','tensor'}, use_global_device_ids=true, to_apply=%region_11.12 | all-reduce | flops 9288 | bytes 74304 | tf_op jit(solution)/shard_map/psum | solution.py:913
  604.8 29.4 %all-gather.21.cloned.1.call-done = bf16[1024,1920]{1,0:T(8,128)(2,1)} async-done(((bf16[256,1920]{1,0:T(8,128)(2,1)}), bf16[1024,1920]{1,0:T(8,128)(2,1)}) %all-gather.21.cloned.1.call-update) | async-done | bytes 3932176 | tf_op jit(solution)/shard_map/all_gather | solution.py:881
  634.2 2.6 bitcast_convert_fusion
  636.8 1.5 fusion.23
  638.3 1.9 copy-done.9
  640.2 1.8 slice_bitcast_fusion
  641.9 5.2 reduce_sum.99
  647.2 1.7 slice.193
  648.8 1.7 slice.189
  650.5 2.1 slice.194
  652.6 1.5 copy.106
  654.2 1.1 copy.101
  655.6 1.1 copy.102
  657.1 1.1 copy.103
  658.3 2.3 copy.111
  660.6 2.4 copy.112
  663.0 1.1 copy.113
  664.1 1.7 fusion.24
  666.0 0.8 copy.100
  667.0 0.8 copy.99
  668.7 13.9 %all-reduce.4.cloned.1.call-done = f32[256,256]{1,0:T(8,128)} async-done(((f32[256,256]{1,0:T(8,128)}), f32[256,256]{1,0:T(8,128)}) %all-reduce.4.cloned.1.call-update) | async-done | bytes 262160 | tf_op jit(solution)/shard_map/psum | solution.py:888
  682.5 2.3 copy.129
  684.9 1.0 copy.130
  (147 shorter events, 13.5 us)
Async XLA Ops:
  7.2 5.9 copy-start
  7.2 8.3 %copy-start.24 = (f32[12]{0:T(128)S(1)}, f32[12]{0:T(128)}, u32[]{:S(2)}) copy-start(f32[12]{0:T(128)} %param.41) | copy-start | bytes 148
  7.2 8.6 %copy-start.25 = (f32[12]{0:T(128)S(1)}, f32[12]{0:T(128)}, u32[]{:S(2)}) copy-start(f32[12]{0:T(128)} %param.42) | copy-start | bytes 148
  7.2 8.8 %copy-start.26 = (f32[12]{0:T(128)S(1)}, f32[12]{0:T(128)}, u32[]{:S(2)}) copy-start(f32[12]{0:T(128)} %param.43) | copy-start | bytes 148
  7.2 9.5 %copy-start.23 = (s32[1,2048]{1,0:T(1,128)S(1)}, s32[1,2048]{1,0:T(1,128)}, u32[]{:S(2)}) copy-start(s32[1,2048]{1,0:T(1,128)} %param.29) | copy-start | bytes 24580
  7.2 57.6 %all-gather.11.cloned.1.call-start = ((), (), s32[]{:S(2)}) async-start(), calls=%async_computation.5 | async-start | bytes 2293760 | tf_op jit(solution)/shard_map/all_gather | solution.py:817
  12.3 106.1 %all-gather.9.cloned.1.call-start = ((), (), s32[]{:S(2)}) async-start(), calls=%async_computation.4 | async-start | bytes 5242880 | tf_op jit(solution)/shard_map/all_gather | solution.py:846
  13.0 147.9 %all-gather.13.cloned.1.call-start = ((), (), s32[]{:S(2)}) async-start(), calls=%async_computation.6 | async-start | bytes 1966080 | tf_op jit(solution)/shard_map/all_gather | solution.py:819
  14.9 196.0 %all-gather.15.cloned.1.call-start = ((), (), s32[]{:S(2)}) async-start(), calls=%async_computation.7 | async-start | bytes 5242880 | tf_op jit(solution)/shard_map/all_gather | solution.py:847
  15.5 398.7 %reduce-scatter.7.cloned.1.call-start = ((), (), s32[]{:S(2)}) async-start(), calls=%async_computation.10 | async-start | bytes 4718592 | tf_op jit(solution)/shard_map/reduce_scatter | solution.py:859
  16.7 112.0 %copy-start.7 = (f32[8,256]{1,0:T(8,128)}, f32[8,256]{1,0:T(8,128)S(1)}, u32[]{:S(2)}) copy-start(f32[8,256]{1,0:T(8,128)S(1)} %scatter.14.heads_ref) | copy-start | bytes 24580
  23.9 6.4 copy-start.27
  23.9 6.5 copy-start.19
  25.2 35.0 %copy-start.22 = (f32[4,256]{1,0:T(4,128)S(1)}, f32[4,256]{1,0:T(4,128)}, u32[]{:S(2)}) copy-start(f32[4,256]{1,0:T(4,128)} %param.40) | copy-start | bytes 12292
  30.4 98.3 %copy-start.8 = (s32[8]{0:T(128)}, s32[8]{0:T(128)S(1)}, u32[]{:S(2)}) copy-start(s32[8]{0:T(128)S(1)} %select_reduce_fusion.slots_ref) | copy-start | bytes 100
  60.2 68.6 %copy-start.6 = (f32[4,512]{1,0:T(4,128)}, f32[4,512]{1,0:T(4,128)S(1)}, u32[]{:S(2)}) copy-start(f32[4,512]{1,0:T(4,128)S(1)} %pad_maximum_fusion.3.taps_ref) | copy-start | bytes 24580
  66.1 55.4 %slice-start = ((bf16[1024,896]{1,0:T(8,128)(2,1)}), bf16[1024,768]{1,0:T(8,128)(2,1)S(1)}, s32[]{:S(2)}) async-start(bf16[1024,896]{1,0:T(8,128)(2,1)} %all-gather.11.cloned.1.call-done), calls=%async_computation.16 | async-start | bytes 3145728 | tf_op jit(solution)/shard_map/slice | solution.py:823
  66.2 55.4 %slice-start.1 = ((bf16[1024,896]{1,0:T(8,128)(2,1)}), bf16[1024,64]{1,0:T(8,128)(2,1)S(1)}, s32[]{:S(2)}) async-start(bf16[1024,896]{1,0:T(8,128)(2,1)} %all-gather.11.cloned.1.call-done), calls=%async_computation.17 | async-start | bytes 524288 | tf_op jit(solution)/shard_map/slice | solution.py:825
  66.2 55.4 %copy-start.20 = (f32[1024]{0:T(1024)S(1)}, f32[1024]{0:T(1024)}, u32[]{:S(2)}) copy-start(f32[1024]{0:T(1024)} %param.31) | copy-start | bytes 12292
  118.4 3.4 copy-start.11
  157.0 0.9 copy-start.2
  157.8 1.3 copy-start.3
  159.1 1.0 copy-start.4
  160.1 0.8 copy-start.5
  310.8 43.6 %copy-start.13 = (bf16[1024,896]{1,0:T(8,128)(2,1)S(1)}, bf16[1024,896]{1,0:T(8,128)(2,1)}, u32[]{:S(2)}) copy-start(bf16[1024,896]{1,0:T(8,128)(2,1)} %all-gather.11.cloned.1.call-done) | copy-start | bytes 5505028
  362.6 106.6 %reduce-scatter.5.cloned.1.call-start = ((), (), s32[]{:S(2)}) async-start(), calls=%async_computation.8 | async-start | bytes 4718592 | tf_op jit(solution)/shard_map/reduce_scatter | solution.py:859
  363.2 152.2 %reduce-scatter.11.cloned.1.call-start = ((), (), s32[]{:S(2)}) async-start(), calls=%async_computation.13 | async-start | bytes 2621440 | tf_op jit(solution)/shard_map/reduce_scatter | solution.py:876
  363.9 50.3 %copy-start.10 = (bf16[256,1024]{1,0:T(8,128)(2,1)S(1)}, bf16[256,1024]{1,0:T(8,128)(2,1)}, u32[]{:S(2)}) copy-start(bf16[256,1024]{1,0:T(8,128)(2,1)} %get-tuple-element.148.x_ref) | copy-start | bytes 1572868
  363.9 51.7 %copy-start.17 = (f32[256,1024]{1,0:T(8,128)S(1)}, f32[256,1024]{1,0:T(8,128)}, u32[]{:S(2)}) copy-start(f32[256,1024]{1,0:T(8,128)} %get-tuple-element.72) | copy-start | bytes 3145732
  363.9 192.6 %reduce-scatter.9.cloned.1.call-start = ((), (), s32[]{:S(2)}) async-start(), calls=%async_computation.12 | async-start | bytes 2293760 | tf_op jit(solution)/shard_map/reduce_scatter | solution.py:877
  373.5 95.6 %copy-start.16 = (f32[256,1024]{1,0:T(8,128)S(1)}, f32[256,1024]{1,0:T(8,128)}, u32[]{:S(2)}) copy-start(f32[256,1024]{1,0:T(8,128)} %get-tuple-element.70) | copy-start | bytes 3145732
  373.6 231.2 %all-gather.19.cloned.1.call-start = ((), (), s32[]{:S(2)}) async-start(), calls=%async_computation.11 | async-start | bytes 1572864 | tf_op jit(solution)/shard_map/all_gather | solution.py:874
  417.8 140.8 %copy-start.21 = (f32[8,512]{1,0:T(8,128)S(1)}, f32[8,512]{1,0:T(8,128)}, u32[]{:S(2)}) copy-start(f32[8,512]{1,0:T(8,128)} %get-tuple-element.80) | copy-start | bytes 49156
  417.9 186.9 %all-gather.17.cloned.1.call-start = ((), (), s32[]{:S(2)}) async-start(), calls=%async_computation.9 | async-start | bytes 1572864 | tf_op jit(solution)/shard_map/all_gather | solution.py:873
  471.2 163.0 %all-gather.21.cloned.1.call-start = ((), (), s32[]{:S(2)}) async-start(), calls=%async_computation.15 | async-start | bytes 4915200 | tf_op jit(solution)/shard_map/all_gather | solution.py:881
  558.6 124.0 %all-reduce.4.cloned.1.call-start = ((), (), s32[]{:S(2)}) async-start(), calls=%async_computation.14 | async-start | bytes 524288 | tf_op jit(solution)/shard_map/psum | solution.py:888
  636.8 3.4 copy-start.9
  656.8 6.2 copy-start.12
  660.6 7.3 %copy-start.14 = (f32[4,256,3]{2,1,0:T(8,128)S(1)}, f32[4,256,3]{2,1,0:T(8,128)}, u32[]{:S(2)}) copy-start(f32[4,256,3]{2,1,0:T(8,128)} %slice.194) | copy-start | bytes 36868
  664.1 20.7 %copy-start.15 = (bf16[512,1024]{1,0:T(8,128)(2,1)S(1)}, bf16[512,1024]{1,0:T(8,128)(2,1)}, u32[]{:S(2)}) copy-start(bf16[512,1024]{1,0:T(8,128)(2,1)} %all-gather.19.cloned.1.call-done) | copy-start | bytes 3145732
  664.1 22.4 %copy-start.1 = (bf16[256,1024]{1,0:T(8,128)(2,1)S(1)}, bf16[256,1024]{1,0:T(8,128)(2,1)}, u32[]{:S(2)}) copy-start(bf16[256,1024]{1,0:T(8,128)(2,1)} %param.46) | copy-start | bytes 1572868
  682.5 3.3 copy-start.18
Sparse Core Ops, SparseCore 0:
  12.4 52.4 all-gather.10
  66.7 51.5 all-gather.8
  120.5 37.0 all-gather.12
  159.3 51.5 all-gather.14
  362.7 51.4 reduce-scatter.6
  417.8 51.3 reduce-scatter.4
  471.5 43.8 reduce-scatter.10
  517.8 38.7 reduce-scatter.8
  558.7 8.2 all-gather.18
  569.0 10.1 all-gather.16
  581.9 52.2 all-gather.20
  664.3 18.2 all-reduce.3

commit v3 on v2

--- a/solution.py
+++ b/solution.py
@@ -438,13 +438,14 @@
             return {"tensor": 1 - self.t}
         return {"context": self.chips[mask]}
 
-    def greet(self, masks=(1, 2, 4)):
+    def greet(self, line=None):
         barrier = pltpu.get_barrier_semaphore()
-        for mask in masks:
-            pl.semaphore_signal(
-                barrier, inc=1, device_id=self.target(mask), device_id_type=MESH
-            )
-        pl.semaphore_wait(barrier, len(masks))
+        targets = [self.target(mask) for mask in (1, 2, 4)]
+        if line is not None:
+            targets += [line.target(step) for step in range(1, line.count)]
+        for target in targets:
+            pl.semaphore_signal(barrier, inc=1, device_id=target, device_id_type=MESH)
+        pl.semaphore_wait(barrier, len(targets))
 
 
 class Wire:
@@ -549,22 +550,27 @@
 
 
 class Gather:
-    def __init__(self, place, whole, sems):
+    def __init__(self, place, whole, sems, rows=ROWS, cores=True):
         self.place = place
         self.whole = whole
+        self.size = rows
+        self.cores = cores
         self.wire = Wire(place, sems)
 
     def rows(self, mask, sibling=False, half=None):
-        begin = self.place.slot(mask, sibling) * ROWS
+        place, size = self.place, self.size
+        block = place.slot(mask, sibling) if self.cores else place.chips[mask]
+        begin = block * size
         if half is None:
-            return self.whole.at[pl.ds(pl.multiple_of(begin, ROWS), ROWS)]
-        return self.whole.at[pl.ds(pl.multiple_of(begin + half * PART, PART), PART)]
-
-    def start(self):
+            return self.whole.at[pl.ds(pl.multiple_of(begin, size), size)]
+        return self.whole.at[pl.ds(pl.multiple_of(begin + half * (size // 2), size // 2), size // 2)]
+
+    def start(self, core=True):
         wire = self.wire
         for half, mask, index in ((0, 1, 0), (1, 2, 1), (1, 1, 2), (0, 2, 3)):
             wire.send(self.rows(0, half=half), self.rows(0, half=half), index, mask)
-        wire.send(self.rows(0), self.rows(0), 6, 4)
+        if self.cores and core:
+            wire.send(self.rows(0), self.rows(0), 6, 4)
 
     def relay(self):
         wire = self.wire
@@ -576,15 +582,18 @@
     def near(self):
         wire = self.wire
         wire.arrive(self.rows(1, half=1), 2, 1)
-        wire.send(self.rows(1), self.rows(1), 7, 4)
+        if self.cores:
+            wire.send(self.rows(1), self.rows(1), 7, 4)
         wire.arrive(self.rows(2, half=0), 3, 2)
-        wire.send(self.rows(2), self.rows(2), 8, 4)
+        if self.cores:
+            wire.send(self.rows(2), self.rows(2), 8, 4)
 
     def far(self):
         wire = self.wire
         wire.arrive(self.rows(3, half=0), 4, 2)
         wire.arrive(self.rows(3, half=1), 5, 1)
-        wire.send(self.rows(3), self.rows(3), 9, 4)
+        if self.cores:
+            wire.send(self.rows(3), self.rows(3), 9, 4)
 
     def core(self, mask):
         index = (6, 7, 8, 9)[mask]
@@ -592,6 +601,25 @@
 
     def finish(self):
         self.wire.finish()
+
+
+class Line:
+    def __init__(self):
+        self.f = lax.axis_index("fsdp")
+        self.count = lax.axis_size("fsdp")
+
+    def target(self, step):
+        return {"fsdp": (self.f + step) % self.count}
+
+    def copy(self, source, target, sems, step):
+        return pltpu.make_async_remote_copy(
+            src_ref=source,
+            dst_ref=target,
+            send_sem=sems.at[0, step],
+            recv_sem=sems.at[1, step],
+            device_id=self.target(step),
+            device_id_type=MESH,
+        )
 
 
 def slot_rows(slot):
@@ -752,6 +780,228 @@
     )(ag, wout, wffn, x_own, cot_own, cot_all, gain.reshape(1, -1))
 
 
+def ending_kernel(
+    du_ref, w_ref, normed_ref, x_ref, dmixed_ref, gain_ref, mixed_ref, outp_ref, mid_ref, stats_ref,
+    dgain_ref,
+    grad_ref, out_ref, last_ref, mids_ref, small_ref,
+    total, part, dw, arrived, bc_out, bc_in, small_in, *scratch,
+):
+    place = Place()
+    line = Line()
+    back = Scatter(place, scratch[0:5])
+    final = Scatter(place, scratch[5:10])
+    share = mid_ref.shape[0]
+    last_all = Gather(place, last_ref, scratch[10], share, False)
+    mid_all = Gather(place, mids_ref, scratch[11], share, False)
+    small_rows = small_in.shape[1]
+    small_all = Gather(place, small_ref, scratch[12], small_rows)
+    line_sems, small_sems, pair_sems = scratch[13], scratch[14], scratch[15]
+    pair = Wire(place, pair_sems)
+    place.greet(line)
+    sent = []
+
+    chunk = dw.shape[0] // 4
+    for k in range(4):
+        dw[k * chunk : (k + 1) * chunk, :] = dot(
+            normed_ref[:, k * chunk : (k + 1) * chunk], du_ref[...], 0, 0
+        ).astype(BF16)
+    for step in range(1, line.count):
+        rows = pl.ds(pl.multiple_of((line.f + step) % line.count * share, share), share)
+        made = line.copy(dw.at[rows], arrived.at[step], line_sems, step)
+        made.start()
+        sent.append(made)
+
+    def block(mask, sibling=False):
+        return dot(du_ref[slot_rows(place.slot(mask, sibling)), :], w_ref[...], 1, 1)
+
+    for mask in SCATTER_ORDER:
+        rows = slot_rows(place.slot(mask, True))
+        part[rows, :] = block(mask, True).astype(BF16)
+        back.to_core(mask, part.at[rows])
+    back.first(block, total)
+    mids_ref[pl.ds(pl.multiple_of(place.c * share, share), share), :] = mid_ref[...]
+    mid_all.start()
+    for mask in SCATTER_ORDER:
+        final.to_core(mask, outp_ref.at[slot_rows(place.slot(mask, True))])
+    back.second()
+    mid_all.relay()
+    back.last(total)
+    dnormed = total[...]
+    x = x_ref[...].astype(F32)
+    gain = gain_ref[...]
+    scale = norm_scale(x)
+    spread = dnormed * gain
+    pull = jnp.mean(spread * x, axis=1, keepdims=True)
+    grad = dmixed_ref[...] + scale * (spread - x * (scale * scale * pull))
+    half = pl.ds(pl.multiple_of(place.t * ROWS, ROWS), ROWS)
+    grad_ref[half, :] = grad.astype(BF16)
+    pair.send(grad_ref.at[half], grad_ref.at[half], 0, 4)
+    small_in[0] = jnp.zeros(small_in.shape[1:], F32)
+    small_in[0, 0:1, :] = jnp.sum(dnormed * x * scale, axis=0, keepdims=True)
+    small_in[0, 1:2, :] = dgain_ref[0:1, :]
+    small_in[0, 8:16, : stats_ref.shape[1]] = stats_ref[...]
+    for step in range(1, line.count):
+        made = line.copy(small_in.at[0], small_in.at[step], small_sems, step)
+        made.start()
+        sent.append(made)
+
+    def ready(mask):
+        return outp_ref[slot_rows(place.slot(mask)), :].astype(F32)
+
+    final.first(ready, total)
+    mid_all.near()
+    final.second()
+    total[...] += mixed_ref[...]
+    mid_all.far()
+    final.last(total)
+    out_ref[half, :] = total[...].astype(BF16)
+    pair.send(out_ref.at[half], out_ref.at[half], 1, 4)
+
+    for step in range(1, line.count):
+        line.copy(small_in.at[0], small_in.at[step], small_sems, step).wait_recv()
+    summed = small_in[line.f % line.count]
+    for other in range(1, line.count):
+        summed = summed + small_in[(line.f + line.count - other) % line.count]
+    mine = pl.ds(pl.multiple_of(place.slot(0) * small_rows, small_rows), small_rows)
+    small_ref[mine, :] = summed
+    small_all.start()
+
+    own = pl.ds(pl.multiple_of(line.f * share, share), share)
+    for step in range(1, line.count):
+        line.copy(arrived.at[step], arrived.at[step], line_sems, step).wait_recv()
+    sums = dw[own, :].astype(F32)
+    for step in range(1, line.count):
+        sums = sums + arrived[step].astype(F32)
+    here = pl.ds(pl.multiple_of(place.c * share, share), share)
+    bc_out[...] = sums[:, 256:512].astype(BF16)
+    pair.send(bc_out, bc_in, 2, 4)
+    last_ref[here, 0:256] = sums[:, 0:256].astype(BF16)
+    last_ref[here, 512:] = sums[:, 512:].astype(BF16)
+    small_all.relay()
+    pair.arrive(bc_in, 2, 4)
+    last_ref[here, 256:512] = (bc_out[...].astype(F32) + bc_in[...].astype(F32)).astype(BF16)
+    last_all.start()
+    small_all.near()
+    last_all.relay()
+    small_all.far()
+    last_all.near()
+    last_all.far()
+    for mask in range(4):
+        small_all.core(mask)
+    other = pl.ds(pl.multiple_of((1 - place.t) * ROWS, ROWS), ROWS)
+    pair.arrive(grad_ref.at[other], 0, 4)
+    pair.arrive(out_ref.at[other], 1, 4)
+    for made in sent:
+        made.wait_send()
+    pair.finish()
+    mid_all.finish()
+    small_all.finish()
+    last_all.finish()
+
+
+def ending(du, w, normed, x_own, dmixed, gain, mixed, outp, mid, stats, dgain, fsdp):
+    count, model = normed.shape
+    share = mid.shape[0]
+    columns = w.shape[1]
+    chips = lax.axis_size("context")
+    vmem = pl.BlockSpec(memory_space=pltpu.VMEM)
+    shape = jax.ShapeDtypeStruct
+    dma = pltpu.SemaphoreType.DMA
+    return pl.pallas_call(
+        ending_kernel,
+        out_shape=(
+            shape((2 * ROWS, model), BF16),
+            shape((2 * ROWS, model), BF16),
+            shape((chips * share, columns), BF16),
+            shape((chips * share, mid.shape[1]), BF16),
+            shape((2 * chips * 16, model), F32),
+        ),
+        in_specs=[vmem] * 11,
+        out_specs=(vmem,) * 5,
+        scratch_shapes=[
+            pltpu.VMEM((ROWS, model), F32),
+            pltpu.VMEM((count, model), BF16),
+            pltpu.VMEM((model, columns), BF16),
+            pltpu.VMEM((fsdp, share, columns), BF16),
+            pltpu.VMEM((share, 256), BF16),
+            pltpu.VMEM((share, 256), BF16),
+            pltpu.VMEM((fsdp, 16, model), F32),
+        ]
+        + scatter_scratch(model)
+        + scatter_scratch(model)
+        + [dma((2, GATHER_SEMS))] * 3
+        + [dma((2, fsdp)), dma((2, fsdp)), dma((2, 3))],
+        compiler_params=pltpu.CompilerParams(
+            collective_id=2, has_side_effects=True, vmem_limit_bytes=60 << 20
+        ),
+        cost_estimate=pl.CostEstimate(
+            flops=4 * count * model * columns, bytes_accessed=30 << 20, transcendentals=0
+        ),
+    )(du, w, normed, x_own, dmixed, gain.reshape(1, -1), mixed, outp, mid, stats, dgain)
+
+
+def assemble_kernel(
+    last_ref, mid_ref, dx_ref, out_in_ref,
+    out_ref, grad_ref, query_ref, keyval_ref, attn_ref, gate_ref, x_ref, bc_ref, step_ref, ssm_ref,
+    ffn_gate_ref, ffn_up_ref, ffn_down_ref,
+):
+    chips = last_ref.shape[0]
+    heads = step_ref.shape[1] // chips
+    inner = heads * SSM_DIM
+    hid = ffn_gate_ref.shape[1] // chips
+
+    def spread(source, begin, width):
+        return jnp.concatenate(
+            [source[k, :, begin : begin + width].astype(F32) for k in range(chips)], axis=1
+        )
+
+    def summed(begin, end):
+        total = last_ref[0, :, begin:end].astype(F32)
+        for k in range(1, chips):
+            total = total + last_ref[k, :, begin:end].astype(F32)
+        return total
+
+    out_ref[...] = out_in_ref[...]
+    grad_ref[...] = dx_ref[...]
+    x_ref[...] = spread(last_ref, 0, inner)
+    query_ref[...] = spread(last_ref, inner, HEAD_DIM)
+    bc_ref[...] = summed(256, 512)
+    gate_ref[...] = spread(last_ref, 512, inner)
+    both = summed(640, 896)
+    keyval_ref[...] = both[:, HEAD_DIM : 3 * HEAD_DIM]
+    step_ref[...] = spread(last_ref, 896 - HEAD_DIM, heads)
+    ffn_gate_ref[...] = spread(mid_ref, 0, hid)
+    ffn_up_ref[...] = spread(mid_ref, hid, hid)
+    ffn_down_ref[...] = spread(mid_ref, 2 * hid, hid)
+    ssm_ref[...] = spread(mid_ref, 3 * hid, inner)
+    attn_ref[...] = spread(mid_ref, 3 * hid + inner, HEAD_DIM)
+
+
+def assemble(last, mid, dx, out, widths):
+    chips = lax.axis_size("context")
+    share = last.shape[0] // chips
+    turns = 2
+    rows = share // turns
+    shape = jax.ShapeDtypeStruct
+    block = lambda height, width: pl.BlockSpec((height, width), lambda i: (i, 0))
+    slab = lambda width: pl.BlockSpec((chips, rows, width), lambda i: (0, i, 0))
+    token_rows = dx.shape[0] // turns
+    model = dx.shape[1]
+    return pl.pallas_call(
+        assemble_kernel,
+        grid=(turns,),
+        out_shape=(shape(out.shape, BF16), shape(dx.shape, BF16))
+        + tuple(shape((share, width), F32) for width in widths),
+        in_specs=[
+            slab(last.shape[1]), slab(mid.shape[1]), block(token_rows, model),
+            block(token_rows, model),
+        ],
+        out_specs=(block(token_rows, model), block(token_rows, model))
+        + tuple(block(rows, width) for width in widths),
+        compiler_params=pltpu.CompilerParams(vmem_limit_bytes=40 << 20),
+    )(last.reshape(chips, share, -1), mid.reshape(chips, share, -1), dx, out)
+
+
 GROUP = ("context", "tensor")
 
 
@@ -855,92 +1105,43 @@
     u = low_dot(normed, w_wide)
     ag, y, conv, states, keyval = mixer_forward(u, table, head_rows, taps, slot_of)
 
-    def scatter(values):
-        return lax.psum_scatter(
-            values.astype(BF16), GROUP, scatter_dimension=0, tiled=True
-        ).astype(F32)
-
     nffn, hidden, dgu, dm_all, dag, out_part, mixed, dmixed, dgain_rows, dw_mid = middle(
         ag, wout_all, wffn_all, x_own, cot_own, cot_all, gain_ffn
     )
-    dgain_ffn = dgain_rows[0]
-    out_own = mixed + scatter(out_part)
     du, stats = mixer_backward(dag, ag, u, table, head_rows, taps, y, conv, states, keyval, slot_of)
-    dnormed = scatter(low_dot(du, w_all, 1, 1))
-    dx_norm, dgain_mix = norm_back(x_own.astype(F32), gain_mix, dnormed)
-    dx_own = dmixed + dx_norm
-
-    mixed_out = lax.all_gather(out_own.astype(BF16), "tensor", axis=0, tiled=True)
-    tokens_grad = lax.all_gather(dx_own.astype(BF16), "tensor", axis=0, tiled=True)
-
     dw_mid = lax.psum_scatter(dw_mid, "fsdp", scatter_dimension=0, tiled=True)
-    dw = lax.psum_scatter(
-        low_dot(normed, du, 0, 0).astype(BF16), "fsdp", scatter_dimension=0, tiled=True
-    )
-    dw = jnp.concatenate([dw, dw_mid[:, 3 * hid :], dw_mid[:, : 3 * hid]], axis=1)
-    dw_all = lax.all_gather(dw, "context", axis=0, tiled=False).astype(F32)
-
-    def spread(begin, width):
-        piece = dw_all[:, :, begin : begin + width]
-        return piece.transpose(1, 0, 2).reshape(piece.shape[1], -1)
-
-    summed = jnp.sum(dw_all, axis=0)
-    dbc = lax.psum(summed[:, 256:512], "tensor")
-    dkv = summed[:, 768 - HEAD_DIM : 768 + HEAD_DIM]
-
-    def place(values, full, axis_start):
-        zero = jnp.zeros(full, F32)
-        return lax.dynamic_update_slice(zero, values, axis_start).reshape(-1)
-
-    total_heads = skip.shape[0] * lax.axis_size("tensor")
-    at_head = t * skip.shape[0] + c * heads
-
-    def head_sum(row):
-        return jnp.sum(row[:inner].reshape(heads, SSM_DIM), axis=1)
-
-    x_width = conv_x.shape[1] * lax.axis_size("tensor")
-    small = [
-        dgain_mix,
-        dgain_ffn,
-        place(stats[0:CONV, :inner], (CONV, x_width), (0, t * conv_x.shape[1] + c * inner)),
-        stats[0:CONV, 256:512].reshape(-1),
-        place(stats[5, :inner].reshape(heads, SSM_DIM)[:, 0], (total_heads,), (at_head,)),
-        place(head_sum(stats[6]), (total_heads,), (at_head,)),
-        place(head_sum(stats[4]), (total_heads,), (at_head,)),
-    ]
-    small[4] = place(head_sum(stats[5]), (total_heads,), (at_head,))
-    sizes = [s.shape[0] for s in small]
-    joined = lax.psum(jnp.concatenate(small), ("fsdp", "context", "tensor"))
-    pieces = []
-    at = 0
-    for size in sizes:
-        pieces.append(joined[at : at + size])
-        at += size
-
-    def own(values, width, axis):
-        return lax.dynamic_slice_in_dim(values, t * width, width, axis=axis)
-
+    dx, out, last, mids, small = ending(
+        du, w_all, normed, x_own, dmixed, gain_mix, mixed, out_part, dw_mid, stats, dgain_rows,
+        lax.axis_size("fsdp"),
+    )
+    cores = lax.axis_size("tensor")
+    weights = (
+        w_query, w_keyval, w_attn_out, w_gate_z, w_in_x, w_bc, w_step, w_ssm_out, w_ffn_gate,
+        w_ffn_up, w_ffn_down,
+    )
+    grads = assemble(last, mids, dx, out, [w.shape[1] for w in weights])
+    small = small.reshape(ctx, cores, 16, -1)
+    everywhere = jnp.sum(small[:, :, 0:2] , axis=(0, 1))
+    dconv_bc = jnp.sum(small[:, :, 8 : 8 + CONV, 256:512], axis=(0, 1))
+    own = lax.dynamic_index_in_dim(small, t, axis=1, keepdims=False)
+    dconv_x = own[:, 8 : 8 + CONV, :inner].transpose(1, 0, 2).reshape(CONV, -1)
+    by_head = own[:, 12:15, :inner].reshape(ctx, 3, heads, SSM_DIM)
+    dskip = jnp.sum(by_head[:, 0], axis=2).reshape(-1)
+    dbias = jnp.sum(by_head[:, 1], axis=2).reshape(-1)
+    ddecay = jnp.sum(by_head[:, 2], axis=2).reshape(-1)
     return (
-        mixed_out,
-        tokens_grad,
-        pieces[0],
-        spread(inner, qd),
-        dkv,
-        spread(896 + inner, qd),
-        spread(512, inner),
-        spread(0, inner),
-        dbc,
-        spread(at_step, heads),
-        own(pieces[2].reshape(CONV, x_width), conv_x.shape[1], 1),
-        pieces[3].reshape(CONV, -1),
-        own(pieces[4], skip.shape[0], 0),
-        own(pieces[5], skip.shape[0], 0),
-        own(pieces[6], skip.shape[0], 0),
-        spread(896, inner),
-        pieces[1],
-        spread(1152, hid),
-        spread(1152 + hid, hid),
-        spread(1152 + 2 * hid, hid),
+        grads[0],
+        grads[1],
+        everywhere[0],
+        *grads[2:9],
+        dconv_x,
+        dconv_bc,
+        dbias,
+        ddecay,
+        dskip,
+        grads[9],
+        everywhere[1],
+        *grads[10:13],
     )
 
 

time: 703 us -> 476 us (0.68)
  waiting for transfers between devices: 327 us -> 106 us
  Pallas kernels: 172 us -> 268 us
  blocking collectives: 64.7 us -> 24.9 us
  local copies, waits for them, and re-layouts: 60.3 us -> 36.5 us
  matrix products: 24.7 us -> 7.23 us
  other arithmetic: 29.2 us -> 15 us
    reduce_scatter x3 -> x0, waiting for transfers between devices: 131 us -> none  [the longest x2 91.6 us: scatter(): lax.psum_scatter(values.astype(BF16), GROUP, scatter_dimension=0, tiled=T...]
    pallas_call x0 -> x2, Pallas kernels: none -> 96.9 us  [the longest x1 93 us: ending(): pl.pallas_call(ending_kernel, out_shape=(shape((2 * ROWS, model), BF16),...]
    reduce_scatter x1, waiting for transfers between devices: 44.1 us -> 1.09 us  [per_device(): dw_mid = lax.psum_scatter(dw_mid, 'fsdp', scatter_dimension=0, tiled=True)]
    psum x1 -> x0, blocking collectives: 40 us -> none  [per_device(): joined = lax.psum(jnp.concatenate(small), ('fsdp', 'context', 'tensor'))]
    all_gather x3 -> x0, waiting for transfers between devices: 29.4 us -> none  [the longest x1 29.4 us: per_device(): dw_all = lax.all_gather(dw, 'context', axis=0, tiled=False).astype(F32)]
    dot_general x3 -> x1, matrix products: 24.7 us -> 7.23 us  [dot(): lax.dot_general(left, right, (((left_dim,), (right_dim,)), ((), ())), pre...]
    psum x1 -> x0, waiting for transfers between devices: 13.9 us -> none  [per_device(): dbc = lax.psum(summed[:, 256:512], 'tensor')]
    slice x13 -> x3, local copies, waits for them, and re-layouts: 12 us -> 0.62 us  [the longest x1 0.61 us: per_device(): everywhere[1]]
  transfers between devices with their start and end apart: 12 -> 5, of which waited for: 9 -> 4; matrix products, arithmetic and copies ran while one was open for 9% -> 7% of each run, Pallas kernels for 4% -> 15%
where the time goes in v3:
time: 476 us; the launch traced here: 472 us
  Pallas kernels  268 us (56%)
  waiting for transfers between devices  106 us (22%)
  local copies, waits for them, and re-layouts  36.5 us (8%)
  blocking collectives  24.9 us (5%)
  other arithmetic  15 us (3%)
  between operations  14.3 us (3%)
  matrix products  7.23 us (2%)
    pallas_call x1, Pallas kernels, middle(): pl.pallas_call(middle_kernel, out_shape=(shape((count, model), BF16), sha...  99.8 us
    pallas_call x1, Pallas kernels, ending(): pl.pallas_call(ending_kernel, out_shape=(shape((2 * ROWS, model), BF16),...  93 us
    all_gather x1, waiting for transfers between devices, per_device(): x_all = lax.all_gather(tokens, 'context', axis=0, tiled=True)  52 us
    all_gather x1, waiting for transfers between devices, per_device(): cot_all = lax.all_gather(cotangent, 'context', axis=0, tiled=True)  46.7 us
    pallas_call x1, Pallas kernels, mixer_backward(): pl.pallas_call(mixer_backward_kernel, out_shape=(jax.ShapeDtypeStruct((co...  43.2 us
    pallas_call x1, Pallas kernels, mixer_forward(): pl.pallas_call(mixer_forward_kernel, out_shape=(jax.ShapeDtypeStruct((cou...  28 us
    all_gather x1, blocking collectives, per_device(): wout_all = lax.all_gather(mine_out, 'fsdp', axis=0, tiled=True)  24.9 us
    unnamed x48, local copies, waits for them, and re-layouts  12.6 us
  transfers between devices with their start and end apart: 5, of which 4 were waited for; matrix products, arithmetic and copies ran while one was open for 7% of the time, Pallas kernels for 15%

profile of v3, /device:TPU:0, one launch (start us, length us, event | category | flops | bytes accessed | tf_op | source)
XLA Modules:
  0.0 471.6 jit_solution(18165927896363184946)
XLA Ops:
  7.3 0.8 constant_dynamic-slice_fusion.8
  8.1 0.1 copy.72
  8.3 0.9 constant_dynamic-slice_fusion.10
  9.2 1.2 constant_dynamic-slice_fusion.9
  10.4 1.9 concatenate.25
  12.3 0.7 all-gather.5.cloned.1.call-update
  13.1 1.0 constant_dynamic-slice_fusion.2
  14.1 0.8 pad_maximum_fusion
  15.0 0.5 all-gather.11.cloned.1.call-update
  15.6 0.1 dynamic_slice.53
  15.9 0.1 reshape.190
  16.0 0.1 reshape.189
  16.2 0.1 reshape.188
  16.3 0.1 pad.22.clone
  16.4 0.1 scatter.11
  16.5 0.2 scatter.14.heads_ref
  16.7 1.8 convert_reduce_fusion
  18.6 5.4 %multiply_sine_fusion = (f32[2048,32]{1,0:T(8,128)S(1)}, f32[2048,32]{1,0:T(8,128)}, f32[2048,32]{1,0:T(8,128)S(1)}) fusion(f32[2048]{0:T(1024)S(1)} %subtract_convert_fusion, f32[32]{0:T(128)S(1)} %multiply_power_fusion), kind=kLoop, calls=%fused_computation.12 | loop fusion | flops 131072 | bytes 794752 | tf_op jit(solution)/shard_map/sin | solution.py:1031
  23.9 1.3 broadcast_in_dim.45
  25.2 4.3 concatenate.27.table_ref
  29.5 0.8 constant_dynamic-slice_fusion.7
  30.3 0.1 select_reduce_fusion.slots_ref
  30.4 0.1 constant_dynamic-slice_fusion.5
  30.5 1.0 constant_dynamic-slice_fusion.6
  31.6 0.1 pad_maximum_fusion.1
  31.7 1.9 constant_dynamic-slice_fusion.1.x_ref
  33.6 1.9 constant_dynamic-slice_fusion.cot_ref
  35.4 24.9 %all_gather.17.wout_ref = bf16[1024,256]{1,0:T(8,128)(2,1)} all-gather(bf16[256,256]{1,0:T(8,128)(2,1)S(1)} %pad_maximum_fusion.1), channel_id=1, replica_groups=mesh['fsdp'=4,'context'=4,'tensor'=2] {'fsdp'}, dimensions={0}, use_global_device_ids=true | all-gather | bytes 655360 | tf_op jit(solution)/shard_map/all_gather | solution.py:1068
  60.3 4.5 all-gather.7.cloned.1.call-done.w_ref
  64.9 1.1 slice.106
  66.0 0.1 copy.65
  66.2 0.2 copy.66
  66.4 52.0 %all-gather.5.cloned.1.call-done = bf16[2048,1024]{1,0:T(8,128)(2,1)} async-done(((bf16[512,1024]{1,0:T(8,128)(2,1)}), bf16[2048,1024]{1,0:T(8,128)(2,1)}) %all-gather.5.cloned.1.call-update) | async-done | bytes 4194320 | tf_op jit(solution)/shard_map/all_gather | solution.py:1096
  118.3 3.2 fusion
  121.6 0.2 copy-done.13
  121.8 1.1 fusion.2.normed_ref
  122.9 2.0 copy-done.14
  124.9 7.2 %fusion.3.u_ref = f32[2048,1024]{1,0:T(8,128)} fusion(bf16[2048,1024]{1,0:T(8,128)(2,1)S(1)} %fusion.2.normed_ref, bf16[1024,64]{1,0:T(8,128)(2,1)S(1)} %slice-done, bf16[1024,192]{1,0:T(8,128)(2,1)S(1)} %copy.66, bf16[1024,768]{1,0:T(8,128)(2,1)S(1)} %slice-done.1), kind=kOutput, calls=%fused_computation.6 | convolution fusion | flops 4301258752 | bytes 14680064 | tf_op jit(solution)/shard_map/dot_general | solution.py:25
  132.1 28.0 %shard_map.365 = (bf16[2048,256]{1,0:T(8,128)(2,1)S(1)}, f32[2048,256]{1,0:T(8,128)S(1)}, f32[2048,512]{1,0:T(8,128)}, f32[1536,128]{1,0:T(8,128)S(1)}, bf16[2048,128]{1,0:T(8,128)(2,1)S(1)}) custom-call(s32[8]{0:T(128)S(1)} %select_reduce_fusion.slots_ref, f32[2048,1024]{1,0:T(8,128)} %fusion.3.u_ref, f32[2048,256]{1,0:T(8,128)} %concatenate.27.table_ref, ...), custom_call_target="tpu_custom_call" | custom-call | tf_op jit(solution)/shard_map/pallas_call | solution.py:332
  160.2 0.9 copy-done.2
  161.0 1.4 copy-done.4
  162.4 1.0 copy-done.8
  163.4 0.8 copy-done.9
  164.2 46.7 %all-gather.11.cloned.1.call-done.cot_all_ref = bf16[2048,1024]{1,0:T(8,128)(2,1)} async-done(((bf16[512,1024]{1,0:T(8,128)(2,1)}), bf16[2048,1024]{1,0:T(8,128)(2,1)}) %all-gather.11.cloned.1.call-update) | async-done | bytes 4194320 | tf_op jit(solution)/shard_map/all_gather | solution.py:1097
  210.9 99.8 %shard_map.366 = (bf16[2048,1024]{1,0:T(8,128)(2,1)}, bf16[2048,256]{1,0:T(8,128)(2,1)}, bf16[2048,512]{1,0:T(8,128)(2,1)}, bf16[2048,1024]{1,0:T(8,128)(2,1)}, ...) custom-call(bf16[2048,256]{1,0:T(8,128)(2,1)} %copy-done.8, ...), custom_call_target="tpu_custom_call" | custom-call | flops 10737418240 | bytes 41943040 | tf_op jit(solution)/shard_map/pallas_call | solution.py:754
  310.8 43.2 %shard_map.367 = (bf16[2048,896]{1,0:T(8,128)(2,1)}, f32[8,512]{1,0:T(8,128)}) custom-call(s32[8]{0:T(128)} %copy-done.12, bf16[2048,256]{1,0:T(8,128)(2,1)} %get-tuple-element.88.dag_ref, bf16[2048,256]{1,0:T(8,128)(2,1)} %copy-done.8, f32[2048,1024]{1,0:T(8,128)} %fusion.3.u_ref, f32[2048,256]{1,0:T(8,128)} %concatenate.27.table_ref, f32[8,256]{1,0:T(8,128)} %copy-done.11, ...), custom_call_target="tpu_custom_call" | custom-call | tf_op jit(solution)/shard_map/pallas_call | solution.py:379
  354.0 1.1 reduce-scatter.2.cloned.1.call-done.mid_ref
  355.1 93.0 %shard_map.368 = (bf16[512,1024]{1,0:T(8,128)(2,1)}, bf16[512,1024]{1,0:T(8,128)(2,1)}, bf16[1024,896]{1,0:T(8,128)(2,1)}, bf16[1024,1024]{1,0:T(8,128)(2,1)}, f32[128,1024]{1,0:T(8,128)}) custom-call(bf16[2048,896]{1,0:T(8,128)(2,1)} %get-tuple-element.93.du_ref, bf16[1024,896]{1,0:T(8,128)(2,1)} %all-gather.7.cloned.1.call-done.w_ref, ...), custom_call_target="tpu_custom_call" | custom-call | flops 7516192768 | bytes 31457280 | tf_op jit(solution)/shard_map/pallas_call | solution.py:910
  448.1 1.4 slice_reduce_fusion.1
  449.5 1.0 slice_reduce_fusion
  450.5 1.0 dynamic-slice_bitcast_fusion
  451.5 0.6 fusion.11
  452.1 0.7 reshape.195
  452.8 0.1 reshape.196
  452.9 0.1 slice_reduce_fusion.2
  453.0 0.6 reshape.199
  453.6 0.6 reshape.198
  454.2 0.6 reshape.197
  454.8 1.6 copy-done.3
  456.4 1.5 copy-done.5
  457.9 1.2 copy-done.6
  459.1 1.2 copy-done.7
  460.3 3.9 shard_map.369
  464.2 0.7 copy.71
  (67 shorter events, 0.9 us)
Async XLA Ops:
  7.2 5.9 %copy-start = (bf16[256,1024]{1,0:T(8,128)(2,1)S(1)}, bf16[256,1024]{1,0:T(8,128)(2,1)}, u32[]{:S(2)}) copy-start(bf16[256,1024]{1,0:T(8,128)(2,1)} %param.46) | copy-start | bytes 1572868
  7.2 8.3 %copy-start.19 = (f32[12]{0:T(128)S(1)}, f32[12]{0:T(128)}, u32[]{:S(2)}) copy-start(f32[12]{0:T(128)} %param.41) | copy-start | bytes 148
  7.2 8.4 %copy-start.20 = (f32[12]{0:T(128)S(1)}, f32[12]{0:T(128)}, u32[]{:S(2)}) copy-start(f32[12]{0:T(128)} %param.42) | copy-start | bytes 148
  7.2 8.5 %copy-start.21 = (f32[12]{0:T(128)S(1)}, f32[12]{0:T(128)}, u32[]{:S(2)}) copy-start(f32[12]{0:T(128)} %param.43) | copy-start | bytes 148
  7.2 9.5 %copy-start.18 = (s32[1,2048]{1,0:T(1,128)S(1)}, s32[1,2048]{1,0:T(1,128)}, u32[]{:S(2)}) copy-start(s32[1,2048]{1,0:T(1,128)} %param.29) | copy-start | bytes 24580
  7.2 57.6 %all-gather.7.cloned.1.call-start = ((), (), s32[]{:S(2)}) async-start(), calls=%async_computation.2 | async-start | bytes 2293760 | tf_op jit(solution)/shard_map/all_gather | solution.py:1067
  12.3 106.1 %all-gather.5.cloned.1.call-start = ((), (), s32[]{:S(2)}) async-start(), calls=%async_computation.1 | async-start | bytes 5242880 | tf_op jit(solution)/shard_map/all_gather | solution.py:1096
  13.0 151.2 %all-gather.9.cloned.1.call-start = ((), (), s32[]{:S(2)}) async-start(), calls=%async_computation.3 | async-start | bytes 1966080 | tf_op jit(solution)/shard_map/all_gather | solution.py:1069
  14.9 196.0 %all-gather.11.cloned.1.call-start = ((), (), s32[]{:S(2)}) async-start(), calls=%async_computation.4 | async-start | bytes 5242880 | tf_op jit(solution)/shard_map/all_gather | solution.py:1097
  15.5 339.6 %reduce-scatter.2.cloned.1.call-start = ((), (), s32[]{:S(2)}) async-start(), calls=%async_computation.5 | async-start | bytes 2621440 | tf_op jit(solution)/shard_map/reduce_scatter | solution.py:1112
  16.7 115.4 %copy-start.11 = (f32[8,256]{1,0:T(8,128)}, f32[8,256]{1,0:T(8,128)S(1)}, u32[]{:S(2)}) copy-start(f32[8,256]{1,0:T(8,128)S(1)} %scatter.14.heads_ref) | copy-start | bytes 24580
  23.9 6.4 %copy-start.22 = (s32[1,8]{1,0:T(1,128)S(1)}, s32[1,8]{1,0:T(1,128)}, u32[]{:S(2)}) copy-start(s32[1,8]{1,0:T(1,128)} %param.30) | copy-start | bytes 100
  23.9 6.5 %copy-start.15 = (bf16[256,256]{1,0:T(8,128)(2,1)S(1)}, bf16[256,256]{1,0:T(8,128)(2,1)}, u32[]{:S(2)}) copy-start(bf16[256,256]{1,0:T(8,128)(2,1)} %param.34) | copy-start | bytes 393220
  25.2 35.1 %copy-start.17 = (f32[4,256]{1,0:T(4,128)S(1)}, f32[4,256]{1,0:T(4,128)}, u32[]{:S(2)}) copy-start(f32[4,256]{1,0:T(4,128)} %param.40) | copy-start | bytes 12292
  30.4 101.7 %copy-start.12 = (s32[8]{0:T(128)}, s32[8]{0:T(128)S(1)}, u32[]{:S(2)}) copy-start(s32[8]{0:T(128)S(1)} %select_reduce_fusion.slots_ref) | copy-start | bytes 100
  60.3 71.8 %copy-start.10 = (f32[4,512]{1,0:T(4,128)}, f32[4,512]{1,0:T(4,128)S(1)}, u32[]{:S(2)}) copy-start(f32[4,512]{1,0:T(4,128)S(1)} %pad_maximum_fusion.2.taps_ref) | copy-start | bytes 24580
  66.1 55.4 %copy-start.16 = (f32[1024]{0:T(1024)S(1)}, f32[1024]{0:T(1024)}, u32[]{:S(2)}) copy-start(f32[1024]{0:T(1024)} %param.31) | copy-start | bytes 12292
  118.3 3.4 copy-start.13
  121.8 3.1 slice-start
  121.8 3.1 slice-start.1
  122.9 2.0 copy-start.14
  160.2 0.9 copy-start.2
  161.0 1.4 copy-start.4
  162.4 1.0 copy-start.8
  163.4 0.8 copy-start.9
  355.1 109.8 %copy-start.1 = (bf16[256,1024]{1,0:T(8,128)(2,1)S(1)}, bf16[256,1024]{1,0:T(8,128)(2,1)}, u32[]{:S(2)}) copy-start(bf16[256,1024]{1,0:T(8,128)(2,1)} %param.46) | copy-start | bytes 1572868
  454.8 1.6 copy-start.3
  456.4 1.5 copy-start.5
  457.9 1.2 copy-start.6
  459.1 1.2 copy-start.7
Sparse Core Ops, SparseCore 0:
  12.4 52.4 all-gather.6
  66.7 51.5 all-gather.4
  120.5 37.0 all-gather.8
  159.3 51.5 all-gather.10
  310.9 44.1 reduce-scatter.1

commit v4 on v3

--- a/solution.py
+++ b/solution.py
@@ -1,4 +1,4 @@
-import functools
+import math
 
 import jax
 import jax.numpy as jnp
@@ -622,6 +622,216 @@
         )
 
 
+class LineGather:
+    def __init__(self, line, whole, sems):
+        self.line = line
+        self.whole = whole
+        self.sems = sems
+        self.size = whole.shape[0] // line.count
+
+    def rows(self, block):
+        return self.whole.at[pl.ds(pl.multiple_of(block * self.size, self.size), self.size)]
+
+    def copy(self, block, way, step):
+        toward = self.line.f + 1 if way == 0 else self.line.f - 1
+        return pltpu.make_async_remote_copy(
+            src_ref=self.rows(block),
+            dst_ref=self.rows(block),
+            send_sem=self.sems.at[way, 0, step],
+            recv_sem=self.sems.at[way, 1, step],
+            device_id={"fsdp": toward},
+            device_id_type=MESH,
+        )
+
+    def step(self, number, arrive=True):
+        f, last = self.line.f, self.line.count - 1
+        for way in (0, 1):
+            block = f - number if way == 0 else f + number
+            there = block >= 0 if way == 0 else block <= last
+            goes_on = f < last if way == 0 else f > 0
+
+            @pl.when(there)
+            def _():
+                if number > 0:
+                    self.copy(block, way, number).wait_recv()
+
+                @pl.when(goes_on)
+                def _():
+                    self.copy(block, way, number + 1).start()
+
+    def finish(self):
+        f, last = self.line.f, self.line.count - 1
+        for number in range(self.line.count - 1):
+            for way in (0, 1):
+                block = f - number if way == 0 else f + number
+                there = block >= 0 if way == 0 else block <= last
+                goes_on = f < last if way == 0 else f > 0
+
+                @pl.when(there & goes_on)
+                def _():
+                    self.copy(block, way, number + 1).wait_send()
+
+
+def line_sems(count):
+    return pltpu.SemaphoreType.DMA((2, 2, count + 1))
+
+
+def opening_kernel(
+    tokens_ref, cot_ref, in_x_ref, query_ref, bc_ref, gate_ref, keyval_ref, step_ref, ssm_ref, attn_ref,
+    gain_ref, segments_ref,
+    normed_ref, u_ref, w_ref, wout_ref, cot_all_ref, table_ref,
+    x_all, wide, x_sems, cot_sems, w_sems, out_sems,
+):
+    place = Place()
+    line = Line()
+    rows_x = Gather(place, x_all, x_sems)
+    rows_cot = Gather(place, cot_all_ref, cot_sems)
+    weights = LineGather(line, w_ref, w_sems)
+    weights_out = LineGather(line, wout_ref, out_sems)
+    chips = lax.axis_size("context")
+    share = in_x_ref.shape[0]
+    heads = step_ref.shape[1] // chips
+    inner = heads * SSM_DIM
+    chip_rows = pl.ds(pl.multiple_of(place.c * 2 * ROWS, 2 * ROWS), 2 * ROWS)
+    place.greet(line)
+    x_all[chip_rows, :] = tokens_ref[...]
+    rows_x.start(core=False)
+    mine = pl.ds(pl.multiple_of(line.f * share, share), share)
+    for k in range(chips):
+
+        @pl.when(place.c == k)
+        def _():
+            inner_part = slice(k * inner, (k + 1) * inner)
+            head_part = slice(k * HEAD_DIM, (k + 1) * HEAD_DIM)
+            w_ref[mine, 0:256] = jnp.concatenate(
+                [in_x_ref[:, inner_part], query_ref[:, head_part]], axis=1
+            )
+            w_ref[mine, 512:768] = jnp.concatenate(
+                [gate_ref[:, inner_part], keyval_ref[:, :HEAD_DIM]], axis=1
+            )
+            none = jnp.zeros((share, HEAD_DIM - heads), F32)
+            steps = step_ref[:, k * heads : (k + 1) * heads].astype(F32)
+            w_ref[mine, 768:896] = jnp.concatenate(
+                [keyval_ref[:, HEAD_DIM:].astype(F32), steps, none], axis=1
+            ).astype(BF16)
+            wout_ref[mine, :] = jnp.concatenate(
+                [ssm_ref[:, inner_part], attn_ref[:, head_part]], axis=1
+            )
+
+    w_ref[mine, 256:512] = bc_ref[...]
+    weights.step(0)
+
+    def norm(slot):
+        rows = slot_rows(slot)
+        x = x_all[rows, :].astype(F32)
+        normed_ref[rows, :] = (x * norm_scale(x) * gain_ref[...]).astype(BF16)
+
+    cot_all_ref[chip_rows, :] = cot_ref[...]
+    norm(place.slot(0))
+    norm(place.slot(0, True))
+    rows_x.relay()
+    rows_cot.start(core=False)
+    weights.step(1)
+
+    numbers = segments_ref[...]
+    bounds = [
+        jnp.sum(jnp.where(numbers < k, 1.0, 0.0), axis=1, keepdims=True) for k in (1, 2)
+    ]
+    count = table_ref.shape[0]
+    lane = lax.broadcasted_iota(jnp.int32, (8, 128), 1)[0:1]
+    power = -(lane % (HEAD_DIM // 2)).astype(F32) / (HEAD_DIM // 2)
+    freqs = jnp.exp(power * math.log(10000.0))
+    phase = jnp.where(lane < HEAD_DIM, math.pi / 2, 0.0)
+    sign = jnp.where((lane >= HEAD_DIM) & (lane < HEAD_DIM + HEAD_DIM // 2), -1.0, 1.0)
+
+    def angles(block, carry):
+        row = lax.broadcasted_iota(jnp.int32, (ROWS, 128), 0) + block * ROWS
+        row = row.astype(F32)
+        start = jnp.where(row >= bounds[0], bounds[0], 0.0)
+        start = jnp.where(row >= bounds[1], bounds[1], start)
+        pos = row - start
+        here = slot_rows(block)
+        table_ref[here, 0:128] = jnp.sin(pos * freqs + phase) * sign
+        table_ref[here, 128:256] = pos
+        return carry
+
+    lax.fori_loop(0, count // ROWS, angles, 0)
+    rows_x.near()
+    norm(place.slot(1))
+    norm(place.slot(2))
+    rows_x.far()
+    norm(place.slot(3))
+    rows_cot.relay()
+    for mask in (1, 2, 3):
+        rows_x.core(mask)
+        norm(place.slot(mask, True))
+    for number in range(2, line.count):
+        weights.step(number)
+    weights_out.step(0)
+    rows_cot.near()
+    wide[:, 0:768] = w_ref[:, 0:768]
+    row, column = iotas(HEAD_DIM, inner)
+    copies = jnp.where(column // SSM_DIM == row, 1.0, 0.0).astype(BF16)
+    wide[:, 768:1024] = jnp.concatenate(
+        [dot(w_ref[:, 896 - HEAD_DIM : 896], copies), w_ref[:, 768 : 768 + HEAD_DIM].astype(F32)],
+        axis=1,
+    ).astype(BF16)
+
+    def project(slot, carry):
+        rows = slot_rows(slot)
+        u_ref[rows, :] = dot(normed_ref[rows, :], wide[...])
+        return carry
+
+    lax.fori_loop(0, 4, project, 0)
+    weights_out.step(1)
+    rows_cot.far()
+    lax.fori_loop(4, 8, project, 0)
+    for number in range(2, line.count):
+        weights_out.step(number)
+    for mask in (1, 2, 3):
+        rows_cot.core(mask)
+    rows_x.finish()
+    rows_cot.finish()
+    weights.finish()
+    weights_out.finish()
+
+
+def opening(tokens, cotangent, weights, gain, segments):
+    fsdp = lax.axis_size("fsdp")
+    model = tokens.shape[1]
+    count = segments.shape[1]
+    vmem = pl.BlockSpec(memory_space=pltpu.VMEM)
+    shape = jax.ShapeDtypeStruct
+    dma = pltpu.SemaphoreType.DMA
+    return pl.pallas_call(
+        opening_kernel,
+        out_shape=(
+            shape((count, model), BF16),
+            shape((count, 1024), F32),
+            shape((model, 896), BF16),
+            shape((model, 256), BF16),
+            shape((count, model), BF16),
+            shape((count, 256), F32),
+        ),
+        in_specs=[vmem] * 12,
+        out_specs=(vmem,) * 6,
+        scratch_shapes=[
+            pltpu.VMEM((count, model), BF16),
+            pltpu.VMEM((model, 1024), BF16),
+            dma((2, GATHER_SEMS)),
+            dma((2, GATHER_SEMS)),
+            line_sems(fsdp),
+            line_sems(fsdp),
+        ],
+        compiler_params=pltpu.CompilerParams(
+            collective_id=3, has_side_effects=True, vmem_limit_bytes=60 << 20
+        ),
+        cost_estimate=pl.CostEstimate(
+            flops=2 * count * model * 1024, bytes_accessed=30 << 20, transcendentals=count * 128
+        ),
+    )(tokens, cotangent, *weights, gain.reshape(1, -1), segments)
+
+
 def slot_rows(slot):
     return pl.ds(pl.multiple_of(slot * ROWS, ROWS), ROWS)
 
@@ -631,9 +841,9 @@
 
 
 def middle_kernel(
-    ag_ref, wout_ref, wffn_ref, x_ref, cot_ref, cot_all_ref, gain_ref,
+    ag_ref, wout_ref, gate_ref, up_ref, down_ref, x_ref, cot_ref, cot_all_ref, gain_ref,
     nffn_ref, hidden_ref, dgu_ref, dm_ref, dag_ref, outp_ref, mixed_ref, dmixed_ref, dgain_ref, dw_ref,
-    part, *scratch,
+    part, wffn_ref, *scratch,
 ):
     place = Place()
     first = Scatter(place, scratch[0:5])
@@ -641,7 +851,15 @@
     forth = Gather(place, nffn_ref, scratch[10])
     home = Gather(place, dm_ref, scratch[11])
     hid = hidden_ref.shape[1]
-    place.greet()
+    line = Line()
+    weights = LineGather(line, wffn_ref, scratch[12])
+    share = gate_ref.shape[0]
+    place.greet(line)
+    mine = pl.ds(pl.multiple_of(line.f * share, share), share)
+    lanes = pl.ds(pl.multiple_of(place.c * hid, hid), hid)
+    for k, source in enumerate((gate_ref, up_ref, down_ref)):
+        wffn_ref[mine, k * hid : (k + 1) * hid] = source[:, lanes]
+    weights.step(0)
 
     def block(mask, sibling=False):
         return dot(ag_ref[slot_rows(place.slot(mask, sibling)), :], wout_ref[...], 1, 1)
@@ -651,6 +869,7 @@
         part[rows, :] = block(mask, True).astype(BF16)
         first.to_core(mask, part.at[rows])
     first.first(block, mixed_ref)
+    weights.step(1)
     first.second()
     mixed_ref[...] += x_ref[...].astype(F32)
     first.last(mixed_ref)
@@ -660,6 +879,8 @@
     own = slot_rows(place.slot(0))
     nffn_ref[own, :] = (mixed * scale * gain).astype(BF16)
     forth.start()
+    for number in range(2, line.count):
+        weights.step(number)
 
     def work(slot):
         rows = slot_rows(slot)
@@ -743,11 +964,12 @@
         pull_back(place.slot(mask, True))
     dw_ref[:, 3 * hid :] = dot(dm_ref[...], ag_ref[...], 0, 0).astype(BF16)
     home.finish()
-
-
-def middle(ag, wout, wffn, x_own, cot_own, cot_all, gain):
+    weights.finish()
+
+
+def middle(ag, wout, weights, x_own, cot_own, cot_all, gain):
     count, model = cot_all.shape
-    hid = wffn.shape[1] // 3
+    hid = weights[0].shape[1] // lax.axis_size("context")
     columns = ag.shape[1]
     vmem = pl.BlockSpec(memory_space=pltpu.VMEM)
     shape = jax.ShapeDtypeStruct
@@ -765,19 +987,20 @@
             shape((8, model), F32),
             shape((model, 3 * hid + columns), BF16),
         ),
-        in_specs=[vmem] * 7,
+        in_specs=[vmem] * 9,
         out_specs=(vmem,) * 10,
-        scratch_shapes=[pltpu.VMEM((count, model), BF16)]
+        scratch_shapes=[pltpu.VMEM((count, model), BF16), pltpu.VMEM((model, 3 * hid), BF16)]
         + scatter_scratch(model)
         + scatter_scratch(model)
-        + [pltpu.SemaphoreType.DMA((2, GATHER_SEMS))] * 2,
+        + [pltpu.SemaphoreType.DMA((2, GATHER_SEMS))] * 2
+        + [line_sems(lax.axis_size("fsdp"))],
         compiler_params=pltpu.CompilerParams(
             collective_id=1, has_side_effects=True, vmem_limit_bytes=60 << 20
         ),
         cost_estimate=pl.CostEstimate(
             flops=20 * count * model * hid, bytes_accessed=40 << 20, transcendentals=count * hid
         ),
-    )(ag, wout, wffn, x_own, cot_own, cot_all, gain.reshape(1, -1))
+    )(ag, wout, *weights, x_own, cot_own, cot_all, gain.reshape(1, -1))
 
 
 def ending_kernel(
@@ -1002,38 +1225,6 @@
     )(last.reshape(chips, share, -1), mid.reshape(chips, share, -1), dx, out)
 
 
-GROUP = ("context", "tensor")
-
-
-def low_dot(left, right, left_dim=1, right_dim=0):
-    return dot(left.astype(BF16), right.astype(BF16), left_dim, right_dim)
-
-
-def inverse_rms(values):
-    return lax.rsqrt(jnp.mean(values * values, axis=-1, keepdims=True) + epsilon)
-
-
-def norm_back(values, gain, grad):
-    scale = inverse_rms(values)
-    pull = jnp.mean(grad * gain * values, axis=-1, keepdims=True)
-    gain_grad = jnp.sum(grad * values * scale, axis=0)
-    return scale * (grad * gain - values * scale * scale * pull), gain_grad
-
-
-def stream_table(segment_ids):
-    count = segment_ids.shape[0]
-    order = jnp.arange(count, dtype=jnp.int32)
-    starts = jnp.sum((segment_ids[None, :] < segment_ids[:, None]).astype(jnp.int32), axis=1)
-    pos = (order - starts).astype(F32)
-    half = HEAD_DIM // 2
-    freqs = 10000.0 ** (-jnp.arange(half, dtype=F32) / half)
-    angles = pos[:, None] * freqs[None, :]
-    cosine, sine = jnp.cos(angles), jnp.sin(angles)
-    return jnp.concatenate(
-        [cosine, cosine, -sine, sine, jnp.broadcast_to(pos[:, None], (count, 128))], axis=1
-    )
-
-
 def per_device(
     tokens, segments, deal, gain_mix, w_query, w_keyval, w_attn_out, w_gate_z, w_in_x, w_bc, w_step,
     conv_x, conv_bc, step_bias, decay_log, skip, w_ssm_out, gain_ffn, w_ffn_gate, w_ffn_up,
@@ -1045,42 +1236,13 @@
     heads = skip.shape[0] // ctx
     inner = heads * SSM_DIM
     qd = w_query.shape[1] // ctx
-    hid = w_ffn_gate.shape[1] // ctx
-    ddt = cotangent.dtype
 
     def part(array, width):
         return lax.dynamic_slice_in_dim(array, c * width, width, axis=1)
-
-    keys_w, values_w = w_keyval[:, :HEAD_DIM], w_keyval[:, HEAD_DIM:]
-    pad = HEAD_DIM - heads
-    mine = jnp.concatenate(
-        [
-            part(w_in_x, inner), part(w_query, qd), w_bc, part(w_gate_z, inner), keys_w, values_w,
-            jnp.pad(part(w_step, heads), ((0, 0), (0, pad))),
-        ],
-        axis=1,
-    )
-    mine_out = jnp.concatenate([part(w_ssm_out, inner), part(w_attn_out, qd)], axis=1)
-    mine_ffn = jnp.concatenate(
-        [part(w_ffn_gate, hid), part(w_ffn_up, hid), part(w_ffn_down, hid)], axis=1
-    )
-    w_all = lax.all_gather(mine, "fsdp", axis=0, tiled=True)
-    wout_all = lax.all_gather(mine_out, "fsdp", axis=0, tiled=True)
-    wffn_all = lax.all_gather(mine_ffn, "fsdp", axis=0, tiled=True)
-    at_step = 896 - HEAD_DIM
-    w_wide = jnp.concatenate(
-        [
-            w_all[:, :768],
-            jnp.repeat(w_all[:, at_step : at_step + heads], SSM_DIM, axis=1),
-            w_all[:, 768 : 768 + HEAD_DIM],
-        ],
-        axis=1,
-    )
 
     order = deal[0]
     ids = jnp.arange(order.shape[0], dtype=jnp.int32)
     slot_of = jnp.sum(jnp.where(order[None, :] == ids[:, None], ids[None, :], 0), axis=1)
-    table = stream_table(segments[0])
 
     def lanes(values):
         return jnp.repeat(lax.dynamic_slice_in_dim(values, c * heads, heads), SSM_DIM)
@@ -1093,20 +1255,22 @@
         [part(conv_x, inner), jnp.zeros((CONV, qd), F32), conv_bc], axis=1
     )
 
-    x_all = lax.all_gather(tokens, "context", axis=0, tiled=True)
-    cot_all = lax.all_gather(cotangent, "context", axis=0, tiled=True)
     row_count = tokens.shape[0]
     half = row_count // 2
     x_own = lax.dynamic_slice_in_dim(tokens, t * half, half, axis=0)
     cot_own = lax.dynamic_slice_in_dim(cotangent, t * half, half, axis=0)
 
-    xf = x_all.astype(F32)
-    normed = (xf * inverse_rms(xf) * gain_mix).astype(BF16)
-    u = low_dot(normed, w_wide)
+    normed, u, w_all, wout_all, cot_all, table = opening(
+        tokens,
+        cotangent,
+        (w_in_x, w_query, w_bc, w_gate_z, w_keyval, w_step, w_ssm_out, w_attn_out),
+        gain_mix,
+        segments,
+    )
     ag, y, conv, states, keyval = mixer_forward(u, table, head_rows, taps, slot_of)
 
     nffn, hidden, dgu, dm_all, dag, out_part, mixed, dmixed, dgain_rows, dw_mid = middle(
-        ag, wout_all, wffn_all, x_own, cot_own, cot_all, gain_ffn
+        ag, wout_all, (w_ffn_gate, w_ffn_up, w_ffn_down), x_own, cot_own, cot_all, gain_ffn
     )
     du, stats = mixer_backward(dag, ag, u, table, head_rows, taps, y, conv, states, keyval, slot_of)
     dw_mid = lax.psum_scatter(dw_mid, "fsdp", scatter_dimension=0, tiled=True)

time: 476 us -> 380 us (0.80)
  waiting for transfers between devices: 106 us -> 0.04 us
  Pallas kernels: 268 us -> 333 us
  blocking collectives: 24.9 us -> 0 us
  local copies, waits for them, and re-layouts: 36.5 us -> 21.3 us
  other arithmetic: 15 us -> 3.98 us
  matrix products: 7.23 us -> 0 us
    all_gather x4 -> x0, waiting for transfers between devices: 103 us -> none  [the longest x1 52 us: per_device(): x_all = lax.all_gather(tokens, 'context', axis=0, tiled=True)]
    pallas_call x0 -> x1, Pallas kernels: none -> 64.7 us  [opening(): pl.pallas_call(opening_kernel, out_shape=(shape((count, model), BF16), sh...]
    all_gather x1 -> x0, blocking collectives: 24.9 us -> none  [per_device(): wout_all = lax.all_gather(mine_out, 'fsdp', axis=0, tiled=True)]
    dot_general x1 -> x0, matrix products: 7.23 us -> none  [dot(): lax.dot_general(left, right, (((left_dim,), (right_dim,)), ((), ())), pre...]
    concatenate x2 -> x0, local copies, waits for them, and re-layouts: 6.16 us -> none  [the longest x1 4.3 us: stream_table(): jnp.concatenate([cosine, cosine, -sine, sine, jnp.broadcast_to(pos[:, Non...]
    dynamic_slice x8 -> x1, local copies, waits for them, and re-layouts: 5.84 us -> 0.07 us  [part(): return lax.dynamic_slice_in_dim(array, c * width, width, axis=1)]
    sin x1 -> x0, other arithmetic: 5.37 us -> none  [stream_table(): cosine, sine = (jnp.cos(angles), jnp.sin(angles))]
    reduce_sum x2 -> x0, other arithmetic: 5.02 us -> none  [the longest x1 3.22 us: inverse_rms(): jnp.mean(values * values, axis=-1, keepdims=True) + epsilon]
  transfers between devices with their start and end apart: 5 -> 1, of which waited for: 4 -> 0; matrix products, arithmetic and copies ran while one was open for 7% -> 0% of each run, Pallas kernels for 15% -> 12%
where the time goes in v4:
time: 380 us; the launch traced here: 373 us
  Pallas kernels  333 us (88%)
  local copies, waits for them, and re-layouts  21.3 us (6%)
  between operations  14.7 us (4%)
  other arithmetic  3.98 us (1%)
    pallas_call x1, Pallas kernels, middle(): pl.pallas_call(middle_kernel, out_shape=(shape((count, model), BF16), sha...  100 us
    pallas_call x1, Pallas kernels, ending(): pl.pallas_call(ending_kernel, out_shape=(shape((2 * ROWS, model), BF16),...  93.4 us
    pallas_call x1, Pallas kernels, opening(): pl.pallas_call(opening_kernel, out_shape=(shape((count, model), BF16), sh...  64.7 us
    pallas_call x1, Pallas kernels, mixer_backward(): pl.pallas_call(mixer_backward_kernel, out_shape=(jax.ShapeDtypeStruct((co...  43.3 us
    pallas_call x1, Pallas kernels, mixer_forward(): pl.pallas_call(mixer_forward_kernel, out_shape=(jax.ShapeDtypeStruct((cou...  27.9 us
    unnamed x28, local copies, waits for them, and re-layouts  11.7 us
  transfers between devices with their start and end apart: 1, of which 0 were waited for; matrix products, arithmetic and copies ran while one was open for 0% of the time, Pallas kernels for 12%

profile of v4, /device:TPU:0, one launch (start us, length us, event | category | flops | bytes accessed | tf_op | source)
XLA Modules:
  0.0 373.3 jit_solution(16533313956794897824)
XLA Ops:
  7.2 0.0 copy-start
  7.2 0.0 reduce-scatter.2.cloned.1.call-start
  7.3 0.8 select_reduce_fusion.slots_ref
  8.0 0.0 copy-start.12
  8.0 0.7 dynamic_slice.22
  8.8 0.7 dynamic_slice.23
  9.5 0.7 dynamic_slice.24
  10.2 0.1 broadcast_in_dim.31
  10.3 0.1 reshape.167
  10.4 0.1 broadcast_in_dim.30
  10.5 0.1 reshape.166
  10.5 0.1 broadcast_in_dim.29
  10.6 0.1 reshape.165
  10.7 1.4 copy.53.step_ref
  12.1 0.1 pad.12.clone
  12.2 0.0 copy-done
  12.2 0.1 constant_dynamic-slice_fusion.2
  12.3 0.7 pad_maximum_fusion.taps_ref
  13.0 0.0 copy-start.10
  13.0 0.2 scatter.11
  13.2 0.2 scatter.14.heads_ref
  13.4 0.0 copy-start.11
  13.4 2.2 constant_dynamic-slice_fusion
  15.6 64.7 %shard_map.365 = (bf16[2048,1024]{1,0:T(8,128)(2,1)}, f32[2048,1024]{1,0:T(8,128)}, bf16[1024,896]{1,0:T(8,128)(2,1)}, bf16[1024,256]{1,0:T(8,128)(2,1)}, bf16[2...) custom-call(bf16[512,1024]{1,0:T(8,128)(2,1)} %tokens_ref.1, bf16[512,1024]{1,0:T(8,128)(2,1)} %cot_ref.1, ...), custom_call_target="tpu_custom_call" | custom-call | flops 4294967296 | bytes 31457280 | tf_op jit(solution)/shard_map/pallas_call | solution.py:806
  80.3 0.0 copy-done.12
  80.3 0.0 copy-done.10
  80.3 0.0 copy-done.11
  80.3 27.9 %shard_map.366 = (bf16[2048,256]{1,0:T(8,128)(2,1)S(1)}, f32[2048,256]{1,0:T(8,128)S(1)}, f32[2048,512]{1,0:T(8,128)}, f32[1536,128]{1,0:T(8,128)S(1)}, bf16[2048,128]{1,0:T(8,128)(2,1)S(1)}) custom-call(s32[8]{0:T(128)S(1)} %select_reduce_fusion.slots_ref, f32[2048,1024]{1,0:T(8,128)} %get-tuple-element.93.u_ref, f32[2048,256]{1,0:T(8,128)} %get-tuple-element.94.table_ref, ...), custom_call_target="tpu_custom_call" | custom-call | tf_op jit(solution)/shard_map/pallas_call | solution.py:332
  108.3 0.0 copy-start.2
  108.3 0.9 copy-done.2
  109.1 0.0 copy-start.4
  109.1 1.4 copy-done.4
  110.5 0.0 copy-start.8
  110.5 1.0 copy-done.8
  111.5 0.0 copy-start.9
  111.5 0.8 copy-done.9
  112.3 100.1 %shard_map.367 = (bf16[2048,1024]{1,0:T(8,128)(2,1)}, bf16[2048,256]{1,0:T(8,128)(2,1)}, bf16[2048,512]{1,0:T(8,128)(2,1)}, bf16[2048,1024]{1,0:T(8,128)(2,1)}, ...) custom-call(bf16[2048,256]{1,0:T(8,128)(2,1)} %copy-done.8, ...), custom_call_target="tpu_custom_call" | custom-call | flops 10737418240 | bytes 41943040 | tf_op jit(solution)/shard_map/pallas_call | solution.py:976
  212.4 0.0 reduce-scatter.2.cloned.1.call-update
  212.4 43.3 %shard_map.368 = (bf16[2048,896]{1,0:T(8,128)(2,1)}, f32[8,512]{1,0:T(8,128)}) custom-call(s32[8]{0:T(128)} %copy-done.12, bf16[2048,256]{1,0:T(8,128)(2,1)} %get-tuple-element.98.dag_ref, bf16[2048,256]{1,0:T(8,128)(2,1)} %copy-done.8, f32[2048,1024]{1,0:T(8,128)} %get-tuple-element.93.u_ref, f32[2048,256]{1,0:T(8,128)} %get-tuple-element.94.table_ref, ...), custom_call_target="tpu_custom_call" | custom-call | tf_op jit(solution)/shard_map/pallas_call | solution.py:379
  255.7 0.0 reduce-scatter.2.cloned.1.call-done.mid_ref
  255.8 0.0 copy-start.1
  255.8 93.4 %shard_map.369 = (bf16[512,1024]{1,0:T(8,128)(2,1)}, bf16[512,1024]{1,0:T(8,128)(2,1)}, bf16[1024,896]{1,0:T(8,128)(2,1)}, bf16[1024,1024]{1,0:T(8,128)(2,1)}, f32[128,1024]{1,0:T(8,128)}) custom-call(bf16[2048,896]{1,0:T(8,128)(2,1)} %get-tuple-element.103.du_ref, bf16[1024,896]{1,0:T(8,128)(2,1)} %get-tuple-element.104.w_ref, ...), custom_call_target="tpu_custom_call" | custom-call | flops 7516192768 | bytes 31457280 | tf_op jit(solution)/shard_map/pallas_call | solution.py:1133
  349.2 1.4 slice_reduce_fusion.1
  350.6 1.0 slice_reduce_fusion
  351.6 1.0 dynamic-slice_bitcast_fusion
  352.6 0.6 fusion
  353.2 0.7 reshape.172
  353.9 0.1 reshape.173
  354.0 0.1 slice_reduce_fusion.2
  354.1 0.6 reshape.176
  354.7 0.6 reshape.175
  355.3 0.6 reshape.174
  355.9 0.0 copy-start.3
  355.9 1.6 copy-done.3
  357.5 0.0 copy-start.5
  357.5 1.5 copy-done.5
  359.0 0.0 copy-start.6
  359.0 1.2 copy-done.6
  360.2 0.0 copy-start.7
  360.2 1.2 copy-done.7
  361.4 3.9 %shard_map.370 = (bf16[512,1024]{1,0:T(8,128)(2,1)}, bf16[512,1024]{1,0:T(8,128)(2,1)}, f32[256,256]{1,0:T(8,128)}, f32[256,128]{1,0:T(8,128)}, f32[256,256]{1,0...) custom-call(bf16[4,256,896]{2,1,0:T(8,128)(2,1)S(1)} %bitcast.17, ...), custom_call_target="tpu_custom_call" | custom-call | tf_op jit(solution)/shard_map/pallas_call | solution.py:1213
  365.3 0.7 copy.57
  366.0 0.0 copy-done.1
  (6 shorter events, 0.0 us)
Async XLA Ops:
  7.2 5.0 %copy-start = (f32[4,768]{1,0:T(4,128)S(1)}, f32[4,768]{1,0:T(4,128)}, u32[]{:S(2)}) copy-start(f32[4,768]{1,0:T(4,128)} %param.39) | copy-start | bytes 36868
  7.2 248.6 %reduce-scatter.2.cloned.1.call-start = ((), (), s32[]{:S(2)}) async-start(), calls=%async_computation.1 | async-start | bytes 2621440 | tf_op jit(solution)/shard_map/reduce_scatter | solution.py:1276
  8.0 72.3 %copy-start.12 = (s32[8]{0:T(128)}, s32[8]{0:T(128)S(1)}, u32[]{:S(2)}) copy-start(s32[8]{0:T(128)S(1)} %select_reduce_fusion.slots_ref) | copy-start | bytes 100
  13.0 67.3 %copy-start.10 = (f32[4,512]{1,0:T(4,128)}, f32[4,512]{1,0:T(4,128)S(1)}, u32[]{:S(2)}) copy-start(f32[4,512]{1,0:T(4,128)S(1)} %pad_maximum_fusion.taps_ref) | copy-start | bytes 24580
  13.4 66.9 %copy-start.11 = (f32[8,256]{1,0:T(8,128)}, f32[8,256]{1,0:T(8,128)S(1)}, u32[]{:S(2)}) copy-start(f32[8,256]{1,0:T(8,128)S(1)} %scatter.14.heads_ref) | copy-start | bytes 24580
  108.3 0.9 copy-start.2
  109.1 1.4 copy-start.4
  110.5 1.0 copy-start.8
  111.5 0.8 copy-start.9
  255.8 110.3 %copy-start.1 = (f32[4,768]{1,0:T(4,128)S(1)}, f32[4,768]{1,0:T(4,128)}, u32[]{:S(2)}) copy-start(f32[4,768]{1,0:T(4,128)} %param.39) | copy-start | bytes 36868
  355.9 1.6 copy-start.3
  357.5 1.5 copy-start.5
  359.0 1.2 copy-start.6
  360.2 1.2 copy-start.7
Sparse Core Ops, SparseCore 0:
  212.5 43.1 reduce-scatter.1

commit v5 on v4

--- a/solution.py
+++ b/solution.py
@@ -1,3 +1,4 @@
+import functools
 import math
 
 import jax
@@ -102,8 +103,8 @@
 
 
 def mixer_forward_kernel(
-    slots_ref, u_ref, table_ref, heads_ref, taps_ref, ag_ref, y_ref, conv_ref, state_in_ref, kv_ref,
-    ext, state, keyval,
+    order_ref, u_ref, normed_ref, table_ref, heads_ref, taps_ref, ag_ref, y_ref, conv_ref, state_in_ref,
+    kv_ref, kept_ref, ordered_ref, ext, state, keyval,
 ):
     block = pl.program_id(0)
     heads = state.shape[0] // SSM_DIM
@@ -173,37 +174,25 @@
     y_pure = jnp.concatenate(parts, axis=1) + factor * dot(ssm_c, held.astype(BF16), 1, 1)
     tailed = (tails * stepped_low.astype(F32)).astype(BF16)
     state[...] = state_scale(last_row, carry_last, heads) * held + dot(tailed, ssm_b, 0, 0)
-    y_ref[:, :inner] = y_pure
-    y_ref[:, inner : inner + HEAD_DIM] = jnp.broadcast_to(
-        highest + jnp.log(total), (rows, HEAD_DIM)
+    y_ref[:, 0:256] = jnp.concatenate(
+        [y_pure, jnp.broadcast_to(highest + jnp.log(total), (rows, HEAD_DIM))], axis=1
     )
+    y_ref[:, 256:512] = jnp.concatenate([u_ref[:, 768 : 768 + inner], attended], axis=1)
+    ordered_ref[...] = normed_ref[...]
+    kept_ref[...] = u_ref[:, 0:768].astype(BF16)
     y_full = y_pure + heads_ref[2:3, :inner] * x_f
     gate = u_ref[:, 512 : 512 + inner].astype(F32)
     gated = y_full * (gate * sigmoid(gate))
     ag_ref[...] = jnp.concatenate([gated, attended], axis=1).astype(BF16)
 
 
-def mixer_backward_kernel(
-    slots_ref, dag_ref, ag_ref, u_ref, table_ref, heads_ref, taps_ref, y_ref, conv_ref, state_in_ref,
-    state_out_ref, kv_ref, du_ref, stats_ref, dext, dpos, dstate, dkey_t, dvalue_t,
+def backward_block(
+    block, first_turn, dag, table_ref, heads_ref, taps_ref, y_ref, conv_ref, kept_ref, state_in_ref,
+    state_out, kv_ref, stats_ref, dext, dpos, dstate, dkey_t, dvalue_t,
 ):
-    turn = pl.program_id(0)
-    blocks = pl.num_programs(0)
-    block = blocks - 1 - turn
     heads = dstate.shape[0] // SSM_DIM
     inner = heads * SSM_DIM
-    rows = u_ref.shape[0]
-    width = dext.shape[1]
-
-    @pl.when(turn == 0)
-    def _():
-        dext[rows : rows + 8, :] = jnp.zeros((8, width), F32)
-        dpos[rows : rows + 8, :] = jnp.full((8, dpos.shape[1]), -1.0, F32)
-        dstate[...] = jnp.zeros(dstate.shape, F32)
-        dkey_t[...] = jnp.zeros(dkey_t.shape, F32)
-        dvalue_t[...] = jnp.zeros(dvalue_t.shape, F32)
-        stats_ref[...] = jnp.zeros(stats_ref.shape, F32)
-
+    rows = dag.shape[0]
     lane_pos = table_ref[:, 128:256]
     cosine = table_ref[:, 0:64]
     sine = table_ref[:, 64:128]
@@ -215,13 +204,13 @@
     values = window[:, HEAD_DIM:]
     query = conv_ref[:, inner : inner + HEAD_DIM] * 0.125
     query_low = query.astype(BF16)
-    datt = dag_ref[:, inner : inner + HEAD_DIM]
+    datt = dag[:, inner : inner + HEAD_DIM]
     datt_f = datt.astype(F32)
     lse = y_ref[:, inner : inner + 1]
     scores = dot(query_low, keys, 1, 1)
     allowed_all = window_mask(lane_pos, offset, rows, span)
     probs = jnp.exp(jnp.where(allowed_all, scores, masked) - lse)
-    inward = jnp.sum(datt_f * ag_ref[:, inner : inner + HEAD_DIM].astype(F32), axis=1, keepdims=True)
+    inward = jnp.sum(datt_f * y_ref[:, 256 + inner : 256 + inner + HEAD_DIM], axis=1, keepdims=True)
     dscores = (probs * (dot(datt, values, 1, 1) - inward)).astype(BF16)
     dquery = dot(dscores, keys) * 0.125
     dkey_t[:, pl.ds(begin, span)] += dot(query.T.astype(BF16), dscores)
@@ -240,15 +229,15 @@
     ssm_c = act[:, 384:512].astype(BF16)
     x_f = ssm_x.astype(F32)
     raw, step, rate, totals, last_row, carry_last, factor, tails = block_decays(
-        u_ref[:, 768 : 768 + inner].astype(F32), heads_ref, lane_pos, heads
+        y_ref[:, 256 : 256 + inner], heads_ref, lane_pos, heads
     )
     totals_t = totals.T
     allowed = local_mask(lane_pos, rows)
     cross = dot(ssm_c, ssm_b, 1, 1)
-    gate = u_ref[:, 512 : 512 + inner].astype(F32)
+    gate = kept_ref[:, 512 : 512 + inner].astype(F32)
     sig = sigmoid(gate)
     y_pure = y_ref[:, :inner]
-    dgated = dag_ref[:, :inner].astype(F32)
+    dgated = dag[:, :inner].astype(F32)
     skip = heads_ref[2:3, :inner]
     dy = dgated * (gate * sig)
     dgate = dgated * (y_pure + skip * x_f) * (sig * (1.0 + gate * (1.0 - sig)))
@@ -278,12 +267,12 @@
     dtotals = dy_r * y_pure - stepped_r * dstep_x - tailed.astype(F32) * from_state
     dstep_x = dstep_x + tails * from_state
     end_term = dot(
-        jnp.ones((8, STATE), F32), dheld_low.astype(F32) * state_out_ref[...], 1, 1, exact
+        jnp.ones((8, STATE), F32), dheld_low.astype(F32) * state_out[...], 1, 1, exact
     )[0:1]
-    end_term = jnp.where(turn == 0, jnp.zeros_like(end_term), end_term)
     row, col = iotas(rows, rows)
     upper = jnp.where(col >= row, 1.0, 0.0).astype(F32)
     drate = -(dot(upper, dtotals, precision=exact) + end_term)
+    state_out[...] = state_in_ref[...]
     dstate[...] = state_scale(last_row, carry_last, heads) * dheld + dot(dfactored, ssm_c, 0, 0)
     dssm_x = step * dstep_x + skip * dy
     dstep = x_f * dstep_x + jnp.exp(heads_ref[1:2, :inner]) * drate
@@ -292,7 +281,7 @@
     dconv = jnp.concatenate([dssm_x, none, dssm_b, dssm_c], axis=1) * dact
     dext[0:rows, :] = dconv
     dpos[0:rows, :] = lane_pos
-    u = u_ref[:, :width].astype(F32)
+    u = kept_ref[:, 0:512].astype(F32)
     du = dconv * taps_ref[CONV - 1 : CONV, :]
     stats_ref[CONV - 1 : CONV, :] += jnp.sum(dconv * u, axis=0, keepdims=True)
     for ahead in range(1, CONV):
@@ -314,45 +303,59 @@
     dstep_all = jnp.zeros((rows, HEAD_DIM), F32)
     for h in range(heads):
         dstep_all = jnp.where(lane == h, summed[h], dstep_all)
-    du_ref[:, 0:256] = jnp.concatenate([du[:, :inner], dquery], axis=1).astype(BF16)
-    du_ref[:, 256:512] = du[:, 256:512].astype(BF16)
-    du_ref[:, 512:768] = jnp.concatenate([dgate, dkey], axis=1).astype(BF16)
-    du_ref[:, 768:896] = jnp.concatenate([dvalue, dstep_all], axis=1).astype(BF16)
-
-
-def mixer_forward(u, table, head_rows, taps, slot_of):
+    return (
+        jnp.concatenate([du[:, :inner], dquery], axis=1).astype(BF16),
+        du[:, 256:512].astype(BF16),
+        jnp.concatenate([dgate, dkey], axis=1).astype(BF16),
+        jnp.concatenate([dvalue, dstep_all], axis=1).astype(BF16),
+    )
+
+
+def slot_holding(order, block):
+    slot = 0
+    for k in range(1, order.shape[0]):
+        slot = slot + jnp.where(order[k] == block, k, 0)
+    return slot
+
+
+def mixer_forward(u, normed_t, table, head_rows, taps, slot_of):
     count = u.shape[0]
     blocks = count // HALF
     heads = 3
     inner = heads * SSM_DIM
     width = taps.shape[1]
-    at_slot = lambda i, slots: (slots[i], 0)
+    at_slot = lambda i, order: (slot_holding(order, i), 0)
     in_order = lambda i, slots: (i, 0)
     whole = lambda i, slots: (0, 0)
     return pl.pallas_call(
         mixer_forward_kernel,
         out_shape=(
             jax.ShapeDtypeStruct((count, inner + HEAD_DIM), BF16),
-            jax.ShapeDtypeStruct((count, inner + HEAD_DIM), F32),
+            jax.ShapeDtypeStruct((count, 512), F32),
             jax.ShapeDtypeStruct((count, width), F32),
             jax.ShapeDtypeStruct((blocks * inner, STATE), F32),
             jax.ShapeDtypeStruct((count, 2 * HEAD_DIM), BF16),
+            jax.ShapeDtypeStruct((count, 768), BF16),
+            jax.ShapeDtypeStruct(normed_t.shape, BF16),
         ),
         grid_spec=pltpu.PrefetchScalarGridSpec(
             num_scalar_prefetch=1,
             grid=(blocks,),
             in_specs=[
                 pl.BlockSpec((HALF, u.shape[1]), at_slot),
+                pl.BlockSpec((normed_t.shape[0], HALF), lambda i, order: at_slot(i, order)[::-1]),
                 pl.BlockSpec((HALF, table.shape[1]), in_order),
                 pl.BlockSpec(head_rows.shape, whole),
                 pl.BlockSpec(taps.shape, whole),
             ],
             out_specs=(
                 pl.BlockSpec((HALF, inner + HEAD_DIM), at_slot),
-                pl.BlockSpec((HALF, inner + HEAD_DIM), in_order),
+                pl.BlockSpec((HALF, 512), in_order),
                 pl.BlockSpec((HALF, width), in_order),
                 pl.BlockSpec((inner, STATE), in_order),
                 pl.BlockSpec((HALF, 2 * HEAD_DIM), in_order),
+                pl.BlockSpec((HALF, 768), in_order),
+                pl.BlockSpec((normed_t.shape[0], HALF), lambda i, order: (0, i)),
             ),
             scratch_shapes=[
                 pltpu.VMEM((8 + HALF, width), F32),
@@ -360,58 +363,8 @@
                 pltpu.VMEM((count, 2 * HEAD_DIM), BF16),
             ],
         ),
-        compiler_params=pltpu.CompilerParams(vmem_limit_bytes=48 << 20),
-    )(slot_of, u, table, head_rows, taps)
-
-
-def mixer_backward(dag, ag, u, table, head_rows, taps, y, conv, states, keyval, slot_of):
-    count = u.shape[0]
-    blocks = count // HALF
-    heads = 3
-    inner = heads * SSM_DIM
-    width = taps.shape[1]
-    last = blocks - 1
-    at_slot = lambda i, slots: (slots[last - i], 0)
-    in_order = lambda i, slots: (last - i, 0)
-    after = lambda i, slots: (jnp.minimum(last - i + 1, last), 0)
-    whole = lambda i, slots: (0, 0)
-    columns = inner + HEAD_DIM
-    return pl.pallas_call(
-        mixer_backward_kernel,
-        out_shape=(
-            jax.ShapeDtypeStruct((count, 896), BF16),
-            jax.ShapeDtypeStruct((8, width), F32),
-        ),
-        grid_spec=pltpu.PrefetchScalarGridSpec(
-            num_scalar_prefetch=1,
-            grid=(blocks,),
-            in_specs=[
-                pl.BlockSpec((HALF, columns), at_slot),
-                pl.BlockSpec((HALF, columns), at_slot),
-                pl.BlockSpec((HALF, u.shape[1]), at_slot),
-                pl.BlockSpec((HALF, table.shape[1]), in_order),
-                pl.BlockSpec(head_rows.shape, whole),
-                pl.BlockSpec(taps.shape, whole),
-                pl.BlockSpec((HALF, columns), in_order),
-                pl.BlockSpec((HALF, width), in_order),
-                pl.BlockSpec((inner, STATE), in_order),
-                pl.BlockSpec((inner, STATE), after),
-                pl.BlockSpec((count, 2 * HEAD_DIM), whole),
-            ],
-            out_specs=(
-                pl.BlockSpec((HALF, 896), at_slot),
-                pl.BlockSpec((8, width), whole),
-            ),
-            scratch_shapes=[
-                pltpu.VMEM((HALF + 8, width), F32),
-                pltpu.VMEM((HALF + 8, 128), F32),
-                pltpu.VMEM((inner, STATE), F32),
-                pltpu.VMEM((HEAD_DIM, count), F32),
-                pltpu.VMEM((HEAD_DIM, count), F32),
-            ],
-        ),
-        compiler_params=pltpu.CompilerParams(vmem_limit_bytes=56 << 20),
-    )(slot_of, dag, ag, u, table, head_rows, taps, y, conv, states, states, keyval)
+        compiler_params=pltpu.CompilerParams(vmem_limit_bytes=60 << 20),
+    )(slot_of, u, normed_t, table, head_rows, taps)
 
 
 MESH = pl.DeviceIdType.MESH
@@ -438,14 +391,17 @@
             return {"tensor": 1 - self.t}
         return {"context": self.chips[mask]}
 
-    def greet(self, line=None):
+    def hello(self, line=None):
         barrier = pltpu.get_barrier_semaphore()
         targets = [self.target(mask) for mask in (1, 2, 4)]
         if line is not None:
             targets += [line.target(step) for step in range(1, line.count)]
         for target in targets:
             pl.semaphore_signal(barrier, inc=1, device_id=target, device_id_type=MESH)
-        pl.semaphore_wait(barrier, len(targets))
+        return len(targets)
+
+    def greet(self, line=None):
+        pl.semaphore_wait(pltpu.get_barrier_semaphore(), self.hello(line))
 
 
 class Wire:
@@ -465,8 +421,12 @@
         )
 
     def send(self, source, target, index, mask):
-        made = self.copy(source, target, index, mask)
-        made.start()
+        def made():
+            here = source() if callable(source) else source
+            there = target() if callable(target) else target
+            return self.copy(here, there, index, mask)
+
+        made().start()
         self.sent.append(made)
 
     def arrive(self, target, index, mask):
@@ -474,7 +434,7 @@
 
     def finish(self):
         for made in self.sent:
-            made.wait_send()
+            made().wait_send()
         self.sent = []
 
 
@@ -517,15 +477,15 @@
         wire, out, kept = self.wire, self.out, self.kept
         both = mine(3) + self.from_core(3)
         out[0] = both.astype(BF16)
-        wire.send(out.at[0, TOP], self.chip_in.at[0], 4, 1)
-        wire.send(out.at[0, END], self.chip_in.at[1], 5, 2)
+        wire.send(lambda: out.at[0, TOP], lambda: self.chip_in.at[0], 4, 1)
+        wire.send(lambda: out.at[0, END], lambda: self.chip_in.at[1], 5, 2)
         both = mine(1) + self.from_core(1)
         out[1] = both.astype(BF16)
-        wire.send(out.at[1, TOP], self.chip_in.at[2], 6, 1)
+        wire.send(lambda: out.at[1, TOP], lambda: self.chip_in.at[2], 6, 1)
         kept[END] = both[PART:]
         both = mine(2) + self.from_core(2)
         out[2] = both.astype(BF16)
-        wire.send(out.at[2, END], self.chip_in.at[3], 7, 2)
+        wire.send(lambda: out.at[2, END], lambda: self.chip_in.at[3], 7, 2)
         kept[TOP] = both[:PART]
         total[...] = mine(0) + self.from_core(0)
 
@@ -533,10 +493,10 @@
         wire, out, kept, came = self.wire, self.out, self.kept, self.chip_in
         wire.arrive(came.at[0], 4, 1)
         out[3, TOP] = (kept[TOP] + came[0].astype(F32)).astype(BF16)
-        wire.send(out.at[3, TOP], came.at[4], 8, 2)
+        wire.send(lambda: out.at[3, TOP], lambda: came.at[4], 8, 2)
         wire.arrive(came.at[1], 5, 2)
         out[3, END] = (kept[END] + came[1].astype(F32)).astype(BF16)
-        wire.send(out.at[3, END], came.at[5], 9, 1)
+        wire.send(lambda: out.at[3, END], lambda: came.at[5], 9, 1)
 
     def last(self, total):
         wire, came = self.wire, self.chip_in
@@ -565,35 +525,39 @@
             return self.whole.at[pl.ds(pl.multiple_of(begin, size), size)]
         return self.whole.at[pl.ds(pl.multiple_of(begin + half * (size // 2), size // 2), size // 2)]
 
+    def both(self, mask, sibling=False, half=None):
+        block = functools.partial(self.rows, mask, sibling, half)
+        return block, block
+
     def start(self, core=True):
         wire = self.wire
         for half, mask, index in ((0, 1, 0), (1, 2, 1), (1, 1, 2), (0, 2, 3)):
-            wire.send(self.rows(0, half=half), self.rows(0, half=half), index, mask)
+            wire.send(*self.both(0, half=half), index, mask)
         if self.cores and core:
-            wire.send(self.rows(0), self.rows(0), 6, 4)
+            wire.send(*self.both(0), 6, 4)
 
     def relay(self):
         wire = self.wire
         wire.arrive(self.rows(1, half=0), 0, 1)
-        wire.send(self.rows(1, half=0), self.rows(1, half=0), 4, 2)
+        wire.send(*self.both(1, half=0), 4, 2)
         wire.arrive(self.rows(2, half=1), 1, 2)
-        wire.send(self.rows(2, half=1), self.rows(2, half=1), 5, 1)
+        wire.send(*self.both(2, half=1), 5, 1)
 
     def near(self):
         wire = self.wire
         wire.arrive(self.rows(1, half=1), 2, 1)
         if self.cores:
-            wire.send(self.rows(1), self.rows(1), 7, 4)
+            wire.send(*self.both(1), 7, 4)
         wire.arrive(self.rows(2, half=0), 3, 2)
         if self.cores:
-            wire.send(self.rows(2), self.rows(2), 8, 4)
+            wire.send(*self.both(2), 8, 4)
 
     def far(self):
         wire = self.wire
         wire.arrive(self.rows(3, half=0), 4, 2)
         wire.arrive(self.rows(3, half=1), 5, 1)
         if self.cores:
-            wire.send(self.rows(3), self.rows(3), 9, 4)
+            wire.send(*self.both(3), 9, 4)
 
     def core(self, mask):
         index = (6, 7, 8, 9)[mask]
@@ -678,66 +642,90 @@
 
 def opening_kernel(
     tokens_ref, cot_ref, in_x_ref, query_ref, bc_ref, gate_ref, keyval_ref, step_ref, ssm_ref, attn_ref,
-    gain_ref, segments_ref,
-    normed_ref, u_ref, w_ref, wout_ref, cot_all_ref, table_ref,
-    x_all, wide, x_sems, cot_sems, w_sems, out_sems,
+    gain_ref, segments_ref, conv_x_ref, conv_bc_ref, bias_ref, decay_ref, skip_ref,
+    normed_t_out, u_out, w_out, wout_out, cot_out, table_out, heads_ref, taps_ref,
+    x_all, cot_all, normed, normed_t, u, weights_all, wout_all, table, wide,
+    x_sems, cot_sems, w_sems, out_sems, local_sems, block_sems,
 ):
     place = Place()
     line = Line()
     rows_x = Gather(place, x_all, x_sems)
-    rows_cot = Gather(place, cot_all_ref, cot_sems)
-    weights = LineGather(line, w_ref, w_sems)
-    weights_out = LineGather(line, wout_ref, out_sems)
+    rows_cot = Gather(place, cot_all, cot_sems)
+    weights = LineGather(line, weights_all, w_sems)
+    weights_out = LineGather(line, wout_all, out_sems)
     chips = lax.axis_size("context")
     share = in_x_ref.shape[0]
-    heads = step_ref.shape[1] // chips
+    heads = step_ref.shape[0] // chips
     inner = heads * SSM_DIM
     chip_rows = pl.ds(pl.multiple_of(place.c * 2 * ROWS, 2 * ROWS), 2 * ROWS)
-    place.greet(line)
-    x_all[chip_rows, :] = tokens_ref[...]
-    rows_x.start(core=False)
+    waiting = []
+
+    def local(source, target, sem):
+        made = pltpu.make_async_copy(source, target, sem)
+        made.start()
+        waiting.append(made)
+        return made
+
+    greetings = place.hello(line)
+    own_x = pltpu.make_async_copy(tokens_ref, x_all.at[chip_rows], local_sems.at[0])
+    own_x.start()
+    own_cot = pltpu.make_async_copy(cot_ref, cot_all.at[chip_rows], local_sems.at[1])
+    own_cot.start()
     mine = pl.ds(pl.multiple_of(line.f * share, share), share)
+    heads_ref[...] = jnp.zeros(heads_ref.shape, F32)
+    taps_ref[...] = jnp.zeros(taps_ref.shape, F32)
     for k in range(chips):
 
         @pl.when(place.c == k)
         def _():
             inner_part = slice(k * inner, (k + 1) * inner)
             head_part = slice(k * HEAD_DIM, (k + 1) * HEAD_DIM)
-            w_ref[mine, 0:256] = jnp.concatenate(
+            weights_all[mine, 0:256] = jnp.concatenate(
                 [in_x_ref[:, inner_part], query_ref[:, head_part]], axis=1
             )
-            w_ref[mine, 512:768] = jnp.concatenate(
+            weights_all[mine, 512:768] = jnp.concatenate(
                 [gate_ref[:, inner_part], keyval_ref[:, :HEAD_DIM]], axis=1
             )
-            none = jnp.zeros((share, HEAD_DIM - heads), F32)
-            steps = step_ref[:, k * heads : (k + 1) * heads].astype(F32)
-            w_ref[mine, 768:896] = jnp.concatenate(
-                [keyval_ref[:, HEAD_DIM:].astype(F32), steps, none], axis=1
-            ).astype(BF16)
-            wout_ref[mine, :] = jnp.concatenate(
+            wout_all[mine, :] = jnp.concatenate(
                 [ssm_ref[:, inner_part], attn_ref[:, head_part]], axis=1
             )
-
-    w_ref[mine, 256:512] = bc_ref[...]
+            taps_ref[0:CONV, :inner] = conv_x_ref[:, inner_part]
+            for h in range(heads):
+                lane = slice(k * heads + h, k * heads + h + 1)
+                for row, source in enumerate((bias_ref, decay_ref, skip_ref)):
+                    heads_ref[row : row + 1, h * SSM_DIM : (h + 1) * SSM_DIM] = jnp.broadcast_to(
+                        source[:, lane], (1, SSM_DIM)
+                    )
+
+    taps_ref[0:CONV, 256:512] = conv_bc_ref[...]
+    head, column = iotas(step_ref.shape[0], HEAD_DIM)
+    chosen = (head == column + place.c * heads) & (column < heads)
+    steps = dot(step_ref[...], jnp.where(chosen, 1.0, 0.0).astype(BF16), 0, 0)
+    weights_all[mine, 768:896] = jnp.concatenate(
+        [keyval_ref[:, HEAD_DIM:].astype(F32), steps], axis=1
+    ).astype(BF16)
+    weights_all[mine, 256:512] = bc_ref[...]
+    own_x.wait()
+    own_cot.wait()
+    pl.semaphore_wait(pltpu.get_barrier_semaphore(), greetings)
     weights.step(0)
+    rows_x.start(core=False)
 
     def norm(slot):
         rows = slot_rows(slot)
         x = x_all[rows, :].astype(F32)
-        normed_ref[rows, :] = (x * norm_scale(x) * gain_ref[...]).astype(BF16)
-
-    cot_all_ref[chip_rows, :] = cot_ref[...]
+        normed[rows, :] = (x * norm_scale(x) * gain_ref[...]).astype(BF16)
+        columns = pl.ds(pl.multiple_of(slot * ROWS, ROWS), ROWS)
+        normed_t[:, columns] = normed[rows, :].T
+
     norm(place.slot(0))
     norm(place.slot(0, True))
-    rows_x.relay()
-    rows_cot.start(core=False)
-    weights.step(1)
 
     numbers = segments_ref[...]
     bounds = [
         jnp.sum(jnp.where(numbers < k, 1.0, 0.0), axis=1, keepdims=True) for k in (1, 2)
     ]
-    count = table_ref.shape[0]
+    count = table.shape[0]
     lane = lax.broadcasted_iota(jnp.int32, (8, 128), 1)[0:1]
     power = -(lane % (HEAD_DIM // 2)).astype(F32) / (HEAD_DIM // 2)
     freqs = jnp.exp(power * math.log(10000.0))
@@ -751,77 +739,102 @@
         start = jnp.where(row >= bounds[1], bounds[1], start)
         pos = row - start
         here = slot_rows(block)
-        table_ref[here, 0:128] = jnp.sin(pos * freqs + phase) * sign
-        table_ref[here, 128:256] = pos
+        table[here, 0:128] = jnp.sin(pos * freqs + phase) * sign
+        table[here, 128:256] = pos
         return carry
 
-    lax.fori_loop(0, count // ROWS, angles, 0)
+    blocks = count // ROWS
+    rows_x.relay()
+    rows_cot.start(core=False)
+    lax.fori_loop(0, blocks // 2, angles, 0)
+    weights.step(1)
+    lax.fori_loop(blocks // 2, blocks, angles, 0)
+    local(table, table_out, local_sems.at[2])
     rows_x.near()
     norm(place.slot(1))
     norm(place.slot(2))
+    rows_cot.relay()
+    for number in range(2, line.count - 1):
+        weights.step(number)
     rows_x.far()
     norm(place.slot(3))
-    rows_cot.relay()
     for mask in (1, 2, 3):
         rows_x.core(mask)
         norm(place.slot(mask, True))
-    for number in range(2, line.count):
-        weights.step(number)
     weights_out.step(0)
     rows_cot.near()
-    wide[:, 0:768] = w_ref[:, 0:768]
+    weights.step(line.count - 1)
+    local(weights_all, w_out, local_sems.at[3])
+    local(normed_t, normed_t_out, local_sems.at[6])
+    wide[:, 0:768] = weights_all[:, 0:768]
     row, column = iotas(HEAD_DIM, inner)
     copies = jnp.where(column // SSM_DIM == row, 1.0, 0.0).astype(BF16)
     wide[:, 768:1024] = jnp.concatenate(
-        [dot(w_ref[:, 896 - HEAD_DIM : 896], copies), w_ref[:, 768 : 768 + HEAD_DIM].astype(F32)],
+        [
+            dot(weights_all[:, 896 - HEAD_DIM : 896], copies),
+            weights_all[:, 768 : 768 + HEAD_DIM].astype(F32),
+        ],
         axis=1,
     ).astype(BF16)
 
-    def project(slot, carry):
-        rows = slot_rows(slot)
-        u_ref[rows, :] = dot(normed_ref[rows, :], wide[...])
-        return carry
-
-    lax.fori_loop(0, 4, project, 0)
+    def project(slot):
+        rows = pl.ds(slot * ROWS, ROWS)
+        u[rows, :] = dot(normed[rows, :], wide[...])
+        local(u.at[rows], u_out.at[rows], block_sems.at[0, slot])
+
+    for slot in range(blocks // 2):
+        project(slot)
     weights_out.step(1)
     rows_cot.far()
-    lax.fori_loop(4, 8, project, 0)
+    for slot in range(blocks // 2, blocks):
+        project(slot)
     for number in range(2, line.count):
         weights_out.step(number)
+    local(wout_all, wout_out, local_sems.at[4])
     for mask in (1, 2, 3):
         rows_cot.core(mask)
+    local(cot_all, cot_out, local_sems.at[5])
+    for made in waiting:
+        made.wait()
     rows_x.finish()
     rows_cot.finish()
     weights.finish()
     weights_out.finish()
 
 
-def opening(tokens, cotangent, weights, gain, segments):
+def opening(tokens, cotangent, weights, gain, segments, taps, by_head):
     fsdp = lax.axis_size("fsdp")
     model = tokens.shape[1]
     count = segments.shape[1]
+    blocks = count // ROWS
     vmem = pl.BlockSpec(memory_space=pltpu.VMEM)
+    hbm = pl.BlockSpec(memory_space=pl.ANY)
     shape = jax.ShapeDtypeStruct
     dma = pltpu.SemaphoreType.DMA
+    buffers = [
+        ((model, count), BF16),
+        ((count, 1024), F32),
+        ((model, 896), BF16),
+        ((model, 256), BF16),
+        ((count, model), BF16),
+        ((count, 256), F32),
+    ]
+    kept = [buffers[k] for k in (0, 1, 2, 3, 5)]
     return pl.pallas_call(
         opening_kernel,
-        out_shape=(
-            shape((count, model), BF16),
-            shape((count, 1024), F32),
-            shape((model, 896), BF16),
-            shape((model, 256), BF16),
-            shape((count, model), BF16),
-            shape((count, 256), F32),
-        ),
-        in_specs=[vmem] * 12,
-        out_specs=(vmem,) * 6,
-        scratch_shapes=[
-            pltpu.VMEM((count, model), BF16),
+        out_shape=tuple(shape(*one) for one in buffers) + (shape((8, 256), F32), shape((8, 512), F32)),
+        in_specs=[hbm] * 2 + [vmem] * 15,
+        out_specs=(hbm,) * 6 + (vmem,) * 2,
+        scratch_shapes=[pltpu.VMEM((count, model), BF16)] * 3
+        + [pltpu.VMEM(*one) for one in kept]
+        + [
             pltpu.VMEM((model, 1024), BF16),
             dma((2, GATHER_SEMS)),
             dma((2, GATHER_SEMS)),
             line_sems(fsdp),
             line_sems(fsdp),
+            dma((7,)),
+            dma((1, blocks)),
         ],
         compiler_params=pltpu.CompilerParams(
             collective_id=3, has_side_effects=True, vmem_limit_bytes=60 << 20
@@ -829,7 +842,10 @@
         cost_estimate=pl.CostEstimate(
             flops=2 * count * model * 1024, bytes_accessed=30 << 20, transcendentals=count * 128
         ),
-    )(tokens, cotangent, *weights, gain.reshape(1, -1), segments)
+    )(
+        tokens, cotangent, *weights, gain.reshape(1, -1), segments, *taps,
+        *[one.reshape(1, -1) for one in by_head],
+    )
 
 
 def slot_rows(slot):
@@ -842,8 +858,8 @@
 
 def middle_kernel(
     ag_ref, wout_ref, gate_ref, up_ref, down_ref, x_ref, cot_ref, cot_all_ref, gain_ref,
-    nffn_ref, hidden_ref, dgu_ref, dm_ref, dag_ref, outp_ref, mixed_ref, dmixed_ref, dgain_ref, dw_ref,
-    part, wffn_ref, *scratch,
+    hidden_ref, dag_ref, mixed_ref, dmixed_ref, dgain_ref, down_all_ref, ffn_ref, dout_ref,
+    nffn_ref, dgu_ref, dm_ref, dw_ref, arrived, part, wffn_ref, *scratch,
 ):
     place = Place()
     first = Scatter(place, scratch[0:5])
@@ -871,7 +887,8 @@
     first.first(block, mixed_ref)
     weights.step(1)
     first.second()
-    mixed_ref[...] += x_ref[...].astype(F32)
+    half = pl.ds(pl.multiple_of(place.t * ROWS, ROWS), ROWS)
+    mixed_ref[...] += x_ref[half, :].astype(F32)
     first.last(mixed_ref)
     mixed = mixed_ref[...]
     gain = gain_ref[...]
@@ -923,14 +940,11 @@
 
     back.first(ready, dmixed_ref)
 
-    def out_block(slot, carry):
-        rows = slot_rows(slot)
-        outp_ref[rows, :] = dot(hidden_ref[rows, :], wffn_ref[:, 2 * hid :], 1, 1).astype(BF16)
-        return carry
-
-    lax.fori_loop(0, 8, out_block, 0)
     back.second()
-    dw_ref[:, : 2 * hid] = dot(nffn_ref[...], dgu_ref[...], 0, 0).astype(BF16)
+    chunk = dw_ref.shape[0] // 4
+    for k in range(4):
+        rows = slice(k * chunk, (k + 1) * chunk)
+        dw_ref[rows, : 2 * hid] = dot(nffn_ref[:, rows], dgu_ref[...], 0, 0).astype(BF16)
     back.last(dmixed_ref)
     dnffn = dmixed_ref[...]
     mixed = mixed_ref[...]
@@ -940,7 +954,7 @@
     dgain_ref[...] = jnp.broadcast_to(
         jnp.sum(dnffn * mixed * scale, axis=0, keepdims=True), dgain_ref.shape
     )
-    dmixed = cot_ref[...].astype(F32) + scale * (spread - mixed * (scale * scale * pull))
+    dmixed = cot_ref[half, :].astype(F32) + scale * (spread - mixed * (scale * scale * pull))
     dmixed_ref[...] = dmixed
     dm_ref[own, :] = dmixed.astype(BF16)
     home.start()
@@ -951,7 +965,15 @@
 
     pull_back(place.slot(0))
     home.relay()
-    dw_ref[:, 2 * hid : 3 * hid] = dot(cot_all_ref[...], hidden_ref[...], 0, 0).astype(BF16)
+    for k in range(4):
+        rows = slice(k * chunk, (k + 1) * chunk)
+        dw_ref[rows, 2 * hid :] = dot(cot_all_ref[:, rows], hidden_ref[...], 0, 0).astype(BF16)
+    line_sent = []
+    for step in range(1, line.count):
+        rows = pl.ds(pl.multiple_of((line.f + step) % line.count * share, share), share)
+        made = line.copy(dw_ref.at[rows], arrived.at[step], scratch[13], step)
+        made.start()
+        line_sent.append(made)
     home.core(0)
     pull_back(place.slot(0, True))
     home.near()
@@ -962,7 +984,15 @@
     for mask in (1, 2, 3):
         home.core(mask)
         pull_back(place.slot(mask, True))
-    dw_ref[:, 3 * hid :] = dot(dm_ref[...], ag_ref[...], 0, 0).astype(BF16)
+    dout_ref[...] = dot(dm_ref[...], ag_ref[...], 0, 0).astype(BF16)
+    down_all_ref[...] = wffn_ref[:, 2 * hid :]
+    sums = dw_ref[mine, :].astype(F32)
+    for step in range(1, line.count):
+        line.copy(arrived.at[step], arrived.at[step], scratch[13], step).wait_recv()
+        sums = sums + arrived[step].astype(F32)
+    ffn_ref[...] = sums.astype(BF16)
+    for made in line_sent:
+        made.wait_send()
     home.finish()
     weights.finish()
 
@@ -976,24 +1006,30 @@
     return pl.pallas_call(
         middle_kernel,
         out_shape=(
-            shape((count, model), BF16),
             shape((count, hid), BF16),
-            shape((count, 2 * hid), BF16),
-            shape((count, model), BF16),
             shape((count, columns), BF16),
-            shape((count, model), BF16),
             shape((ROWS, model), F32),
             shape((ROWS, model), F32),
             shape((8, model), F32),
-            shape((model, 3 * hid + columns), BF16),
+            shape((model, hid), BF16),
+            shape((weights[0].shape[0], 3 * hid), BF16),
+            shape((model, columns), BF16),
         ),
         in_specs=[vmem] * 9,
-        out_specs=(vmem,) * 10,
-        scratch_shapes=[pltpu.VMEM((count, model), BF16), pltpu.VMEM((model, 3 * hid), BF16)]
+        out_specs=(vmem,) * 8,
+        scratch_shapes=[
+            pltpu.VMEM((count, model), BF16),
+            pltpu.VMEM((count, 2 * hid), BF16),
+            pltpu.VMEM((count, model), BF16),
+            pltpu.VMEM((model, 3 * hid), BF16),
+            pltpu.VMEM((lax.axis_size("fsdp"), weights[0].shape[0], 3 * hid), BF16),
+            pltpu.VMEM((count, model), BF16),
+            pltpu.VMEM((model, 3 * hid), BF16),
+        ]
         + scatter_scratch(model)
         + scatter_scratch(model)
         + [pltpu.SemaphoreType.DMA((2, GATHER_SEMS))] * 2
-        + [line_sems(lax.axis_size("fsdp"))],
+        + [line_sems(lax.axis_size("fsdp")), pltpu.SemaphoreType.DMA((2, lax.axis_size("fsdp")))],
         compiler_params=pltpu.CompilerParams(
             collective_id=1, has_side_effects=True, vmem_limit_bytes=60 << 20
         ),
@@ -1003,83 +1039,178 @@
     )(ag, wout, *weights, x_own, cot_own, cot_all, gain.reshape(1, -1))
 
 
-def ending_kernel(
-    du_ref, w_ref, normed_ref, x_ref, dmixed_ref, gain_ref, mixed_ref, outp_ref, mid_ref, stats_ref,
-    dgain_ref,
-    grad_ref, out_ref, last_ref, mids_ref, small_ref,
-    total, part, dw, arrived, bc_out, bc_in, small_in, *scratch,
+BACK_INPUTS = 5
+
+
+def closing_kernel(
+    pick_ref, dag_ref, kv_ref, heads_ref, taps_ref, dmixed_ref, mixed_ref, tokens_ref, gain_ref, ffn_ref,
+    dgain_ref, dout_ref, table_hbm, y_hbm, conv_hbm, kept_hbm, states_hbm, normed_t_hbm, w_hbm,
+    hidden_hbm, down_hbm,
+    grad_ref, out_ref, last_ref, mids_ref, outs_ref, small_ref,
+    table, y, conv, kept, states, normed_t, w, hidden, down,
+    du, dw_sum, dw, arrived, arrived_out, total, part, bc_out, bc_in, small_in,
+    stats, dext, dpos, dstate, state_out, dkey_t, dvalue_t, *scratch,
 ):
     place = Place()
     line = Line()
     back = Scatter(place, scratch[0:5])
     final = Scatter(place, scratch[5:10])
-    share = mid_ref.shape[0]
+    share = ffn_ref.shape[0]
     last_all = Gather(place, last_ref, scratch[10], share, False)
     mid_all = Gather(place, mids_ref, scratch[11], share, False)
+    out_all = Gather(place, outs_ref, scratch[12], share, False)
     small_rows = small_in.shape[1]
-    small_all = Gather(place, small_ref, scratch[12], small_rows)
-    line_sems, small_sems, pair_sems = scratch[13], scratch[14], scratch[15]
+    small_all = Gather(place, small_ref, scratch[13], small_rows)
+    line_sems_, small_sems, out_sems, pair_sems, load_sems, block_sems = scratch[14:20]
     pair = Wire(place, pair_sems)
-    place.greet(line)
+    greetings = place.hello(line)
     sent = []
-
-    chunk = dw.shape[0] // 4
-    for k in range(4):
-        dw[k * chunk : (k + 1) * chunk, :] = dot(
-            normed_ref[:, k * chunk : (k + 1) * chunk], du_ref[...], 0, 0
-        ).astype(BF16)
+    loads = [
+        pltpu.make_async_copy(source, target, load_sems.at[k])
+        for k, (source, target) in enumerate(
+            ((hidden_hbm, hidden), (down_hbm, down), (normed_t_hbm, normed_t), (w_hbm, w))
+        )
+    ]
+    blocks = du.shape[0] // ROWS
+    streams = ((table_hbm, table), (y_hbm, y), (conv_hbm, conv), (kept_hbm, kept), (states_hbm, states))
+
+    def fetch(block, buffer):
+        copies = []
+        for k, (source, target) in enumerate(streams):
+            size = target.shape[1]
+            begin = pl.multiple_of(block * size, size)
+            copies.append(
+                pltpu.make_async_copy(
+                    source.at[pl.ds(begin, size)], target.at[buffer], block_sems.at[buffer, k]
+                )
+            )
+        return copies
+
+    for made in fetch(blocks - 1, 0) + loads:
+        made.start()
+    mids_ref[pl.ds(pl.multiple_of(place.c * share, share), share), :] = ffn_ref[...]
+    width = dext.shape[1]
+    dext[ROWS : ROWS + 8, :] = jnp.zeros((8, width), F32)
+    dpos[ROWS : ROWS + 8, :] = jnp.full((8, dpos.shape[1]), -1.0, F32)
+    for ref in (dstate, state_out, dkey_t, dvalue_t, stats, dw_sum):
+        ref[...] = jnp.zeros(ref.shape, F32)
+    pl.semaphore_wait(pltpu.get_barrier_semaphore(), greetings)
+
     for step in range(1, line.count):
         rows = pl.ds(pl.multiple_of((line.f + step) % line.count * share, share), share)
-        made = line.copy(dw.at[rows], arrived.at[step], line_sems, step)
+        made = line.copy(dout_ref.at[rows], arrived_out.at[step], out_sems, step)
         made.start()
         sent.append(made)
-
-    def block(mask, sibling=False):
-        return dot(du_ref[slot_rows(place.slot(mask, sibling)), :], w_ref[...], 1, 1)
-
-    for mask in SCATTER_ORDER:
-        rows = slot_rows(place.slot(mask, True))
-        part[rows, :] = block(mask, True).astype(BF16)
-        back.to_core(mask, part.at[rows])
-    back.first(block, total)
-    mids_ref[pl.ds(pl.multiple_of(place.c * share, share), share), :] = mid_ref[...]
+    for made in loads:
+        made.wait()
+
+    def out_block(mask, sibling=False):
+        return dot(hidden[slot_rows(place.slot(mask, sibling)), :], down[...], 1, 1)
+
+    for k, mask in enumerate(SCATTER_ORDER):
+        part[k] = out_block(mask, True).astype(BF16)
+        final.to_core(mask, part.at[k])
     mid_all.start()
-    for mask in SCATTER_ORDER:
-        final.to_core(mask, outp_ref.at[slot_rows(place.slot(mask, True))])
+    here = pl.ds(pl.multiple_of(place.c * share, share), share)
+    own = pl.ds(pl.multiple_of(line.f * share, share), share)
+    half = pl.ds(pl.multiple_of(place.t * ROWS, ROWS), ROWS)
+
+    def my_half(ref):
+        return lambda: ref.at[pl.ds(pl.multiple_of(place.t * ROWS, ROWS), ROWS)]
+
+    def collect_out():
+        sums = dout_ref[own, :].astype(F32)
+        for step in range(1, line.count):
+            line.copy(arrived_out.at[step], arrived_out.at[step], out_sems, step).wait_recv()
+            sums = sums + arrived_out[step].astype(F32)
+        outs_ref[here, :] = sums.astype(BF16)
+        out_all.start()
+
+    def finish_out():
+        total[...] += mixed_ref[...]
+        final.last(total)
+        out_ref[half, :] = total[...].astype(BF16)
+        pair.send(my_half(out_ref), my_half(out_ref), 1, 4)
+
+    def picked(source, row):
+        marks = pick_ref[pl.ds(pl.multiple_of(row * 8, 8), 8), 0:1].astype(BF16)
+        found = source[0:ROWS, :] * marks[0:1]
+        for k in range(1, blocks):
+            found = found + source[k * ROWS : (k + 1) * ROWS, :] * marks[k : k + 1]
+        return found
+
+    events = {
+        0: (lambda: final.first(out_block, total), mid_all.relay),
+        1: (final.second, mid_all.near, collect_out),
+        2: (mid_all.far, finish_out, out_all.relay),
+        3: (out_all.near,),
+        4: (out_all.far,),
+    }
+
+    def turn(number, carry):
+        block = blocks - 1 - number
+        buffer = number % 2
+        for made in fetch(block, buffer):
+            made.wait()
+
+        @pl.when(number < blocks - 1)
+        def _():
+            for made in fetch(block - 1, 1 - buffer):
+                made.start()
+
+        dag = picked(dag_ref, block)
+        pieces = backward_block(
+            block, number, dag, table.at[buffer], heads_ref, taps_ref, y.at[buffer],
+            conv.at[buffer], kept.at[buffer], states.at[buffer], state_out, kv_ref, stats, dext, dpos,
+            dstate, dkey_t, dvalue_t,
+        )
+        grads = jnp.concatenate(pieces, axis=1)
+        du[slot_rows(block), :] = grads
+        dw_sum[...] += dot(normed_t[:, slot_rows(block)], grads)
+        for when, actions in events.items():
+
+            @pl.when(number == when)
+            def _():
+                for action in actions:
+                    action()
+
+        return carry
+
+    lax.fori_loop(0, blocks, turn, 0)
+
+    dw[...] = dw_sum[...].astype(BF16)
+    for step in range(1, line.count):
+        rows = pl.ds(pl.multiple_of((line.f + step) % line.count * share, share), share)
+        made = line.copy(dw.at[rows], arrived.at[step], line_sems_, step)
+        made.start()
+        sent.append(made)
+
+    def block_of(mask, sibling=False):
+        return dot(picked(du, place.slot(mask, sibling) + blocks), w[...], 1, 1)
+
+    for k, mask in enumerate(SCATTER_ORDER):
+        part[k] = block_of(mask, True).astype(BF16)
+        back.to_core(mask, part.at[k])
+    back.first(block_of, total)
     back.second()
-    mid_all.relay()
     back.last(total)
     dnormed = total[...]
-    x = x_ref[...].astype(F32)
+    x = tokens_ref[half, :].astype(F32)
     gain = gain_ref[...]
     scale = norm_scale(x)
     spread = dnormed * gain
     pull = jnp.mean(spread * x, axis=1, keepdims=True)
     grad = dmixed_ref[...] + scale * (spread - x * (scale * scale * pull))
-    half = pl.ds(pl.multiple_of(place.t * ROWS, ROWS), ROWS)
     grad_ref[half, :] = grad.astype(BF16)
     pair.send(grad_ref.at[half], grad_ref.at[half], 0, 4)
     small_in[0] = jnp.zeros(small_in.shape[1:], F32)
     small_in[0, 0:1, :] = jnp.sum(dnormed * x * scale, axis=0, keepdims=True)
     small_in[0, 1:2, :] = dgain_ref[0:1, :]
-    small_in[0, 8:16, : stats_ref.shape[1]] = stats_ref[...]
+    small_in[0, 8:16, :width] = stats[...]
     for step in range(1, line.count):
         made = line.copy(small_in.at[0], small_in.at[step], small_sems, step)
         made.start()
         sent.append(made)
-
-    def ready(mask):
-        return outp_ref[slot_rows(place.slot(mask)), :].astype(F32)
-
-    final.first(ready, total)
-    mid_all.near()
-    final.second()
-    total[...] += mixed_ref[...]
-    mid_all.far()
-    final.last(total)
-    out_ref[half, :] = total[...].astype(BF16)
-    pair.send(out_ref.at[half], out_ref.at[half], 1, 4)
-
     for step in range(1, line.count):
         line.copy(small_in.at[0], small_in.at[step], small_sems, step).wait_recv()
     summed = small_in[line.f % line.count]
@@ -1088,25 +1219,22 @@
     mine = pl.ds(pl.multiple_of(place.slot(0) * small_rows, small_rows), small_rows)
     small_ref[mine, :] = summed
     small_all.start()
-
-    own = pl.ds(pl.multiple_of(line.f * share, share), share)
-    for step in range(1, line.count):
-        line.copy(arrived.at[step], arrived.at[step], line_sems, step).wait_recv()
+    small_all.relay()
+    small_all.near()
+    small_all.far()
+
     sums = dw[own, :].astype(F32)
     for step in range(1, line.count):
+        line.copy(arrived.at[step], arrived.at[step], line_sems_, step).wait_recv()
         sums = sums + arrived[step].astype(F32)
-    here = pl.ds(pl.multiple_of(place.c * share, share), share)
     bc_out[...] = sums[:, 256:512].astype(BF16)
     pair.send(bc_out, bc_in, 2, 4)
     last_ref[here, 0:256] = sums[:, 0:256].astype(BF16)
     last_ref[here, 512:] = sums[:, 512:].astype(BF16)
-    small_all.relay()
     pair.arrive(bc_in, 2, 4)
     last_ref[here, 256:512] = (bc_out[...].astype(F32) + bc_in[...].astype(F32)).astype(BF16)
     last_all.start()
-    small_all.near()
     last_all.relay()
-    small_all.far()
     last_all.near()
     last_all.far()
     for mask in range(4):
@@ -1118,55 +1246,76 @@
         made.wait_send()
     pair.finish()
     mid_all.finish()
+    out_all.finish()
     small_all.finish()
     last_all.finish()
 
 
-def ending(du, w, normed, x_own, dmixed, gain, mixed, outp, mid, stats, dgain, fsdp):
-    count, model = normed.shape
-    share = mid.shape[0]
+def closing(small_inputs, streams, loads, fsdp):
+    tokens, ffn, dout = small_inputs[7], small_inputs[9], small_inputs[11]
+    normed_t, w, hidden, down = loads
+    model, count = normed_t.shape
+    share = ffn.shape[0]
     columns = w.shape[1]
     chips = lax.axis_size("context")
+    blocks = count // ROWS
     vmem = pl.BlockSpec(memory_space=pltpu.VMEM)
+    hbm = pl.BlockSpec(memory_space=pl.ANY)
     shape = jax.ShapeDtypeStruct
     dma = pltpu.SemaphoreType.DMA
+    space = pltpu.VMEM
+    inner = streams[4].shape[0] // blocks
     return pl.pallas_call(
-        ending_kernel,
+        closing_kernel,
         out_shape=(
             shape((2 * ROWS, model), BF16),
             shape((2 * ROWS, model), BF16),
             shape((chips * share, columns), BF16),
-            shape((chips * share, mid.shape[1]), BF16),
+            shape((chips * share, ffn.shape[1]), BF16),
+            shape((chips * share, dout.shape[1]), BF16),
             shape((2 * chips * 16, model), F32),
         ),
-        in_specs=[vmem] * 11,
-        out_specs=(vmem,) * 5,
-        scratch_shapes=[
-            pltpu.VMEM((ROWS, model), F32),
-            pltpu.VMEM((count, model), BF16),
-            pltpu.VMEM((model, columns), BF16),
-            pltpu.VMEM((fsdp, share, columns), BF16),
-            pltpu.VMEM((share, 256), BF16),
-            pltpu.VMEM((share, 256), BF16),
-            pltpu.VMEM((fsdp, 16, model), F32),
+        in_specs=[vmem] * 12 + [hbm] * 9,
+        out_specs=(vmem,) * 6,
+        scratch_shapes=[space((2, one.shape[0] // blocks, one.shape[1]), one.dtype) for one in streams]
+        + [space(one.shape, one.dtype) for one in loads]
+        + [
+            space((count, columns), BF16),
+            space((model, columns), F32),
+            space((model, columns), BF16),
+            space((fsdp, share, columns), BF16),
+            space((fsdp, share, dout.shape[1]), BF16),
+            space((ROWS, model), F32),
+            space((4, ROWS, model), BF16),
+            space((share, 256), BF16),
+            space((share, 256), BF16),
+            space((fsdp, 16, model), F32),
+            space((8, 512), F32),
+            space((ROWS + 8, 512), F32),
+            space((ROWS + 8, 128), F32),
+            space((inner, STATE), F32),
+            space((inner, STATE), F32),
+            space((HEAD_DIM, count), F32),
+            space((HEAD_DIM, count), F32),
         ]
         + scatter_scratch(model)
         + scatter_scratch(model)
-        + [dma((2, GATHER_SEMS))] * 3
-        + [dma((2, fsdp)), dma((2, fsdp)), dma((2, 3))],
+        + [dma((2, GATHER_SEMS))] * 4
+        + [dma((2, fsdp)), dma((2, fsdp)), dma((2, fsdp)), dma((2, 3)), dma((4,)), dma((2, BACK_INPUTS))],
         compiler_params=pltpu.CompilerParams(
-            collective_id=2, has_side_effects=True, vmem_limit_bytes=60 << 20
+            collective_id=2, has_side_effects=True, vmem_limit_bytes=61 << 20
         ),
         cost_estimate=pl.CostEstimate(
             flops=4 * count * model * columns, bytes_accessed=30 << 20, transcendentals=0
         ),
-    )(du, w, normed, x_own, dmixed, gain.reshape(1, -1), mixed, outp, mid, stats, dgain)
+    )(*small_inputs, *streams, *loads)
 
 
 def assemble_kernel(
-    last_ref, mid_ref, dx_ref, out_in_ref,
+    last_ref, mid_ref, outs_ref, dx_ref, out_in_ref, small_ref,
     out_ref, grad_ref, query_ref, keyval_ref, attn_ref, gate_ref, x_ref, bc_ref, step_ref, ssm_ref,
-    ffn_gate_ref, ffn_up_ref, ffn_down_ref,
+    ffn_gate_ref, ffn_up_ref, ffn_down_ref, gain_ref, gain_ffn_ref, conv_x_ref, conv_bc_ref,
+    bias_ref, decay_ref, skip_ref,
 ):
     chips = last_ref.shape[0]
     heads = step_ref.shape[1] // chips
@@ -1196,33 +1345,65 @@
     ffn_gate_ref[...] = spread(mid_ref, 0, hid)
     ffn_up_ref[...] = spread(mid_ref, hid, hid)
     ffn_down_ref[...] = spread(mid_ref, 2 * hid, hid)
-    ssm_ref[...] = spread(mid_ref, 3 * hid, inner)
-    attn_ref[...] = spread(mid_ref, 3 * hid + inner, HEAD_DIM)
-
-
-def assemble(last, mid, dx, out, widths):
+    ssm_ref[...] = spread(outs_ref, 0, inner)
+    attn_ref[...] = spread(outs_ref, inner, HEAD_DIM)
+
+    @pl.when(pl.program_id(0) == 0)
+    def _():
+        everywhere = small_ref[0:16, :]
+        for k in range(1, small_ref.shape[0] // 16):
+            everywhere = everywhere + small_ref[16 * k : 16 * k + 16, :]
+        gain_ref[...] = everywhere[0:1]
+        gain_ffn_ref[...] = everywhere[1:2]
+        conv_bc_ref[...] = everywhere[8 : 8 + CONV, 256:512]
+        core = lax.axis_index("tensor")
+        own = [
+            small_ref[pl.ds(pl.multiple_of((2 * k + core) * 16, 16), 16), :] for k in range(chips)
+        ]
+        conv_x_ref[...] = jnp.concatenate([one[8 : 8 + CONV, :inner] for one in own], axis=1)
+        for row, target in ((12, skip_ref), (13, bias_ref), (14, decay_ref)):
+            target[...] = jnp.concatenate(
+                [
+                    jnp.sum(
+                        one[row : row + 1, h * SSM_DIM : (h + 1) * SSM_DIM], axis=1, keepdims=True
+                    )
+                    for one in own
+                    for h in range(heads)
+                ],
+                axis=1,
+            )
+
+
+def assemble(last, mid, outs, dx, out, small, widths, heads):
     chips = lax.axis_size("context")
     share = last.shape[0] // chips
     turns = 2
     rows = share // turns
     shape = jax.ShapeDtypeStruct
     block = lambda height, width: pl.BlockSpec((height, width), lambda i: (i, 0))
+    fixed = lambda height, width: pl.BlockSpec((height, width), lambda i: (0, 0))
     slab = lambda width: pl.BlockSpec((chips, rows, width), lambda i: (0, i, 0))
     token_rows = dx.shape[0] // turns
     model = dx.shape[1]
+    tiny = [
+        (1, model), (1, model), (CONV, heads * SSM_DIM), (CONV, 2 * STATE), (1, heads), (1, heads),
+        (1, heads),
+    ]
     return pl.pallas_call(
         assemble_kernel,
         grid=(turns,),
         out_shape=(shape(out.shape, BF16), shape(dx.shape, BF16))
-        + tuple(shape((share, width), F32) for width in widths),
+        + tuple(shape((share, width), F32) for width in widths)
+        + tuple(shape(one, F32) for one in tiny),
         in_specs=[
-            slab(last.shape[1]), slab(mid.shape[1]), block(token_rows, model),
-            block(token_rows, model),
+            slab(last.shape[1]), slab(mid.shape[1]), slab(outs.shape[1]),
+            block(token_rows, model), block(token_rows, model), fixed(*small.shape),
         ],
         out_specs=(block(token_rows, model), block(token_rows, model))
-        + tuple(block(rows, width) for width in widths),
-        compiler_params=pltpu.CompilerParams(vmem_limit_bytes=40 << 20),
-    )(last.reshape(chips, share, -1), mid.reshape(chips, share, -1), dx, out)
+        + tuple(block(rows, width) for width in widths)
+        + tuple(fixed(*one) for one in tiny),
+        compiler_params=pltpu.CompilerParams(vmem_limit_bytes=60 << 20),
+    )(*[one.reshape(chips, share, -1) for one in (last, mid, outs)], dx, out, small)
 
 
 def per_device(
@@ -1230,82 +1411,51 @@
     conv_x, conv_bc, step_bias, decay_log, skip, w_ssm_out, gain_ffn, w_ffn_gate, w_ffn_up,
     w_ffn_down, cotangent,
 ):
-    ctx = lax.axis_size("context")
-    c = lax.axis_index("context")
-    t = lax.axis_index("tensor")
-    heads = skip.shape[0] // ctx
-    inner = heads * SSM_DIM
-    qd = w_query.shape[1] // ctx
-
-    def part(array, width):
-        return lax.dynamic_slice_in_dim(array, c * width, width, axis=1)
-
-    order = deal[0]
-    ids = jnp.arange(order.shape[0], dtype=jnp.int32)
-    slot_of = jnp.sum(jnp.where(order[None, :] == ids[:, None], ids[None, :], 0), axis=1)
-
-    def lanes(values):
-        return jnp.repeat(lax.dynamic_slice_in_dim(values, c * heads, heads), SSM_DIM)
-
-    head_rows = jnp.zeros((8, 256), F32)
-    head_rows = head_rows.at[0, :inner].set(lanes(step_bias))
-    head_rows = head_rows.at[1, :inner].set(lanes(decay_log))
-    head_rows = head_rows.at[2, :inner].set(lanes(skip))
-    taps = jnp.concatenate(
-        [part(conv_x, inner), jnp.zeros((CONV, qd), F32), conv_bc], axis=1
-    )
-
-    row_count = tokens.shape[0]
-    half = row_count // 2
-    x_own = lax.dynamic_slice_in_dim(tokens, t * half, half, axis=0)
-    cot_own = lax.dynamic_slice_in_dim(cotangent, t * half, half, axis=0)
-
-    normed, u, w_all, wout_all, cot_all, table = opening(
+    ids = jnp.arange(deal.shape[1], dtype=jnp.int32)
+    holds = (deal[0][:, None] == ids[None, :]).astype(F32)
+    pick = jnp.broadcast_to(jnp.concatenate([holds.T, holds]).reshape(-1, 1), (128, 128))
+    normed_t, u, w_all, wout_all, cot_all, table, head_rows, taps = opening(
         tokens,
         cotangent,
-        (w_in_x, w_query, w_bc, w_gate_z, w_keyval, w_step, w_ssm_out, w_attn_out),
+        (w_in_x, w_query, w_bc, w_gate_z, w_keyval, w_step.T, w_ssm_out, w_attn_out),
         gain_mix,
         segments,
+        (conv_x, conv_bc),
+        (step_bias, decay_log, skip),
     )
-    ag, y, conv, states, keyval = mixer_forward(u, table, head_rows, taps, slot_of)
-
-    nffn, hidden, dgu, dm_all, dag, out_part, mixed, dmixed, dgain_rows, dw_mid = middle(
-        ag, wout_all, (w_ffn_gate, w_ffn_up, w_ffn_down), x_own, cot_own, cot_all, gain_ffn
+    ag, y, conv, states, keyval, kept, normed_t = mixer_forward(u, normed_t, table, head_rows, taps, deal[0])
+    hidden, dag, mixed, dmixed, dgain, down, dffn, dout = middle(
+        ag, wout_all, (w_ffn_gate, w_ffn_up, w_ffn_down), tokens, cotangent, cot_all, gain_ffn
     )
-    du, stats = mixer_backward(dag, ag, u, table, head_rows, taps, y, conv, states, keyval, slot_of)
-    dw_mid = lax.psum_scatter(dw_mid, "fsdp", scatter_dimension=0, tiled=True)
-    dx, out, last, mids, small = ending(
-        du, w_all, normed, x_own, dmixed, gain_mix, mixed, out_part, dw_mid, stats, dgain_rows,
+    dx, out, last, mids, outs, small = closing(
+        (
+            pick, dag, keyval, head_rows, taps, dmixed, mixed, tokens, gain_mix.reshape(1, -1), dffn,
+            dgain, dout,
+        ),
+        (table, y, conv, kept, states),
+        (normed_t, w_all, hidden, down),
         lax.axis_size("fsdp"),
     )
-    cores = lax.axis_size("tensor")
     weights = (
         w_query, w_keyval, w_attn_out, w_gate_z, w_in_x, w_bc, w_step, w_ssm_out, w_ffn_gate,
         w_ffn_up, w_ffn_down,
     )
-    grads = assemble(last, mids, dx, out, [w.shape[1] for w in weights])
-    small = small.reshape(ctx, cores, 16, -1)
-    everywhere = jnp.sum(small[:, :, 0:2] , axis=(0, 1))
-    dconv_bc = jnp.sum(small[:, :, 8 : 8 + CONV, 256:512], axis=(0, 1))
-    own = lax.dynamic_index_in_dim(small, t, axis=1, keepdims=False)
-    dconv_x = own[:, 8 : 8 + CONV, :inner].transpose(1, 0, 2).reshape(CONV, -1)
-    by_head = own[:, 12:15, :inner].reshape(ctx, 3, heads, SSM_DIM)
-    dskip = jnp.sum(by_head[:, 0], axis=2).reshape(-1)
-    dbias = jnp.sum(by_head[:, 1], axis=2).reshape(-1)
-    ddecay = jnp.sum(by_head[:, 2], axis=2).reshape(-1)
+    done = assemble(last, mids, outs, dx, out, small, [w.shape[1] for w in weights], skip.shape[0])
+    grads = done[2:13]
+    gain, gain_two, taps_x, taps_bc, bias, decay, skips = done[13:]
     return (
-        grads[0],
-        grads[1],
-        everywhere[0],
-        *grads[2:9],
-        dconv_x,
-        dconv_bc,
-        dbias,
-        ddecay,
-        dskip,
-        grads[9],
-        everywhere[1],
-        *grads[10:13],
+        done[0],
+        done[1],
+        gain.reshape(-1),
+        *grads[:7],
+        taps_x,
+        taps_bc,
+        bias.reshape(-1),
+        decay.reshape(-1),
+        skips.reshape(-1),
+        grads[7],
+        gain_two.reshape(-1),
+        *grads[8:],
     )
 
 

time: 380 us -> 362 us (0.953)
  Pallas kernels: 333 us -> 354 us
  local copies, waits for them, and re-layouts: 21.3 us -> 2.4 us
  between operations: 14.7 us -> 0.95 us
  other arithmetic: 3.98 us -> 0.08 us
    pallas_call x4 -> x3, Pallas kernels: 301 us -> 318 us  [the longest x1 145 us: closing(): pl.pallas_call(closing_kernel, out_shape=(shape((2 * ROWS, model), BF16),...]
    unnamed x28 -> x3, local copies, waits for them, and re-layouts: 11.7 us -> 1.6 us
    dynamic_slice x5 -> x0, local copies, waits for them, and re-layouts: 4.5 us -> none  [the longest x1 2.24 us: per_device(): cot_own = lax.dynamic_slice_in_dim(cotangent, t * half, half, axis=0)]
  transfers between devices with their start and end apart: 1 -> 0, of which waited for: 0 -> 0; matrix products, arithmetic and copies ran while one was open for 0% -> 0% of each run, Pallas kernels for 12% -> 0%
where the time goes in v5:
time: 362 us; the launch traced here: 358 us
  Pallas kernels  354 us (98%)
    pallas_call x1, Pallas kernels, closing(): pl.pallas_call(closing_kernel, out_shape=(shape((2 * ROWS, model), BF16),...  145 us
    pallas_call x1, Pallas kernels, middle(): pl.pallas_call(middle_kernel, out_shape=(shape((count, hid), BF16), shape...  120 us
    pallas_call x1, Pallas kernels, opening(): pl.pallas_call(opening_kernel, out_shape=tuple((shape(*one) for one in bu...  53.5 us
    pallas_call x1, Pallas kernels, mixer_forward(): pl.pallas_call(mixer_forward_kernel, out_shape=(jax.ShapeDtypeStruct((cou...  29.8 us

profile of v5, /device:TPU:0, one launch (start us, length us, event | category | flops | bytes accessed | tf_op | source)
XLA Modules:
  0.0 357.7 jit_solution(2804962286052385135)
XLA Ops:
  0.7 53.5 %shard_map.365 = (bf16[1024,2048]{1,0:T(8,128)(2,1)}, f32[2048,1024]{1,0:T(8,128)}, bf16[1024,896]{1,0:T(8,128)(2,1)}, bf16[1024,256]{1,0:T(8,128)(2,1)}, bf16[2...) custom-call(bf16[512,1024]{1,0:T(8,128)(2,1)} %tokens_ref.3, ...), custom_call_target="tpu_custom_call" | custom-call | flops 4294967296 | bytes 31457280 | tf_op jit(solution)/shard_map/pallas_call | solution.py:823
  54.2 29.8 %shard_map.366 = (bf16[2048,256]{1,0:T(8,128)(2,1)}, f32[2048,512]{1,0:T(8,128)}, f32[2048,512]{1,0:T(8,128)}, f32[1536,128]{1,0:T(8,128)}, bf16[2048,128]{1,0:T...) custom-call(s32[8]{0:T(128)} %bitcast.18, f32[2048,1024]{1,0:T(8,128)} %get-tuple-element.69.u_ref, ...), custom_call_target="tpu_custom_call" | custom-call | tf_op jit(solution)/shard_map/pallas_call | solution.py:330
  84.0 0.0 copy-start
  84.0 120.0 %shard_map.367 = (bf16[2048,256]{1,0:T(8,128)(2,1)}, bf16[2048,256]{1,0:T(8,128)(2,1)}, f32[256,1024]{1,0:T(8,128)}, f32[256,1024]{1,0:T(8,128)}, f32[8,1024]{1,...) custom-call(bf16[2048,256]{1,0:T(8,128)(2,1)} %get-tuple-element.74.ag_ref, ...), custom_call_target="tpu_custom_call" | custom-call | flops 10737418240 | bytes 41943040 | tf_op jit(solution)/shard_map/pallas_call | solution.py:1006
  204.0 0.0 copy-done
  204.0 0.1 iota_compare_fusion.1
  204.1 0.1 reshape.96
  204.2 0.7 broadcast_in_dim.13.pick_ref
  204.9 144.8 %shard_map.368 = (bf16[512,1024]{1,0:T(8,128)(2,1)}, bf16[512,1024]{1,0:T(8,128)(2,1)}, bf16[1024,896]{1,0:T(8,128)(2,1)}, bf16[1024,768]{1,0:T(8,128)(2,1)}, bf...) custom-call(f32[128,128]{1,0:T(8,128)} %broadcast_in_dim.13.pick_ref, bf16[2048,256]{1,0:T(8,128)(2,1)} %get-tuple-element.77.dag_ref, ...), custom_call_target="tpu_custom_call" | custom-call | flops 7516192768 | bytes 31457280 | tf_op jit(solution)/shard_map/pallas_call | solution.py:1268
  349.8 6.0 %shard_map.369 = (bf16[512,1024]{1,0:T(8,128)(2,1)}, bf16[512,1024]{1,0:T(8,128)(2,1)}, f32[256,256]{1,0:T(8,128)}, f32[256,128]{1,0:T(8,128)}, f32[256,256]{1,0...) custom-call(bf16[4,256,896]{2,1,0:T(8,128)(2,1)} %bitcast.15, ...), custom_call_target="tpu_custom_call" | custom-call | tf_op jit(solution)/shard_map/pallas_call | solution.py:1392
  355.8 1.6 copy.43
  (1 shorter events, 0.0 us)
Async XLA Ops:
  84.0 120.0 %copy-start = (s32[1,8]{1,0:T(1,128)S(1)}, s32[1,8]{1,0:T(1,128)}, u32[]{:S(2)}) copy-start(s32[1,8]{1,0:T(1,128)} %param.24) | copy-start | bytes 100
